TPU v7x, 256 devices: a whole 4x4x8 slice. The times are simulated.
256 devices in a mesh: tok: 32 (over y, x, core), mlp: 8 (over z).
Axes of the slice: x: 4, y: 4, z: 8, core: 2. Of those that a mesh axis runs over, the one named last changes fastest.
Arguments:
- states: bfloat16 [8, 512, 2048], P(None, 'tok', 'mlp')
- w_qkv: bfloat16 [2048, 6144], P('tok', 'mlp')
- w_out: bfloat16 [2048, 2048], P('mlp', 'tok'), may hold values from -0.25 to 0.25
- w_up: bfloat16 [2048, 8192], P(None, 'mlp'), may hold values from -0.125 to 0.125
- w_down: bfloat16 [8192, 2048], P('mlp'), may hold values from -0.0625 to 0.0625
- w_dec: bfloat16 [2048, 128], P('mlp'), may hold values from -0.125 to 0.125
- gain_attn: float32 [2048], replicated, may hold values from 0.25 to 1.75
- gain_mlp: float32 [2048], P('mlp'), may hold values from 0.25 to 1.75
- obs_patch: int32 [256, 32, 64], P(('tok', 'mlp')), may hold values from 0 to 127
- obs_base: int32 [256, 32, 64], P(('tok', 'mlp')), may hold values from 0 to 110, as said below
- obs_count: int32 [256, 32], P(('tok', 'mlp')), may hold values from 1 to 64, as said below
- obs_weight: float32 [256, 32, 4, 64], P(('tok', 'mlp')), may hold values from 0.1 to 1
- obs_value: float32 [256, 32, 64], P(('tok', 'mlp')), may hold values from -6 to 6
Outputs:
- state_out: bfloat16 [8, 512, 2048], P(None, 'tok', 'mlp')
- guidance: float32 [8, 512, 2048], P(None, 'tok', 'mlp')
Inputs may be any that keep to these rules, and one draw needn't show every extreme that they name: `obs_base`: base = r * 16 + c with r below 7 and c below 15. `obs_count`: slots at or above the count are padding; every source device has one block with all 64 slots live.
All inputs are finite; a program needn't handle non-finite values.
Results may differ from a plain program's by a relative error of at most 0.028.
Values may be sent and summed in bfloat16 or wider, within the bound.
No kernel may reach another device: no remote copies, remote signals or barrier semaphores. Data moves between devices by JAX's collectives and lax.ppermute only.
A program may use at most 128 MiB of HBM per device.

v0:
```python
import jax
import jax.numpy as jnp
from jax import lax
from jax.sharding import PartitionSpec as P

D = 2048
HD = 64
PW = 16


EPS = 1e-06


def body(
    states,
    w_qkv,
    w_out,
    w_up,
    w_down,
    w_dec,
    gain_attn,
    gain_mlp,
    obs_patch,
    obs_base,
    obs_count,
    obs_weight,
    obs_value,
):
    seqs, pos, local_width = states.shape
    rows = seqs * pos
    groups = w_qkv.shape[1] // (3 * HD)
    full = lax.all_gather(states, "mlp", axis=2, tiled=True)
    flat = full.reshape(rows, -1).astype(jnp.float32)
    normed = (
        flat * lax.rsqrt(jnp.mean(flat * flat, axis=1, keepdims=True) + EPS) * gain_attn
    ).astype(jnp.bfloat16)
    qkv = jnp.dot(
        normed, lax.all_gather(w_qkv, "tok", axis=0, tiled=True), preferred_element_type=jnp.float32
    )
    qkv = qkv.astype(jnp.bfloat16).reshape(seqs, pos, 3, groups, HD)
    parts = qkv.transpose(2, 0, 3, 1, 4)
    query = parts[0]
    keyval = parts[1:]
    scale = 1.0 / HD**0.5
    start_top = jnp.full((seqs, groups, pos), -1e30, jnp.float32)
    piece = lax.all_gather(keyval, "tok", axis=3, tiled=True)
    top = start_top
    scores = (
        jnp.einsum("sgqe,sgke->sgqk", query, piece[0], preferred_element_type=jnp.float32) * scale
    )
    new_top = jnp.maximum(top, jnp.max(scores, axis=3))
    probs = jnp.exp(scores - new_top[..., None])
    total = jnp.sum(probs, axis=3)
    mixed = jnp.einsum(
        "sgqk,sgke->sgqe", probs.astype(jnp.bfloat16), piece[1], preferred_element_type=jnp.float32
    )
    top, total, acc = (new_top, total, mixed)
    attended = (acc / total[..., None]).astype(jnp.bfloat16)
    attended = attended.transpose(0, 2, 1, 3).reshape(rows, groups * HD)
    mixed = jnp.dot(
        attended,
        lax.all_gather(w_out, "tok", axis=1, tiled=True),
        preferred_element_type=jnp.float32,
    )
    attn_share = lax.psum_scatter(
        mixed.astype(jnp.bfloat16), "mlp", scatter_dimension=1, tiled=True
    ).astype(jnp.float32)
    resid = states.reshape(rows, local_width).astype(jnp.float32) + attn_share
    squares = lax.psum(jnp.sum(resid * resid, axis=1, keepdims=True), "mlp")
    normed2 = (resid * lax.rsqrt(squares / D + EPS) * gain_mlp).astype(jnp.bfloat16)
    wide = lax.all_gather(normed2, "mlp", axis=1, tiled=True)
    hidden = jax.nn.gelu(jnp.dot(wide, w_up, preferred_element_type=jnp.float32)).astype(
        jnp.bfloat16
    )
    down = jnp.dot(hidden, w_down, preferred_element_type=jnp.float32)
    ffn_share = lax.psum_scatter(
        down.astype(jnp.bfloat16), "mlp", scatter_dimension=1, tiled=True
    ).astype(jnp.float32)
    state_out = (resid + ffn_share).astype(jnp.bfloat16)
    decoded = lax.psum(
        jnp.dot(state_out, w_dec, preferred_element_type=jnp.float32).astype(jnp.bfloat16), "mlp"
    ).astype(jnp.float32)
    patch_size = decoded.shape[1]
    patch_rows, bases, counts = (
        lax.all_to_all(obs_patch, "tok", split_axis=1, concat_axis=1, tiled=True),
        lax.all_to_all(obs_base, "tok", split_axis=1, concat_axis=1, tiled=True),
        lax.all_to_all(obs_count, "tok", split_axis=1, concat_axis=1, tiled=True),
    )
    weights, observed = (
        lax.all_to_all(
            obs_weight.astype(jnp.bfloat16), "tok", split_axis=1, concat_axis=1, tiled=True
        ).astype(obs_weight.dtype),
        lax.all_to_all(
            obs_value.astype(jnp.bfloat16), "tok", split_axis=1, concat_axis=1, tiled=True
        ).astype(obs_value.dtype),
    )
    offsets = jnp.array([0, 1, PW, PW + 1], dtype=jnp.int32)
    start = patch_rows * patch_size + bases
    taps = start[:, :, None, :] + offsets[None, None, :, None]
    flat_dec = decoded.reshape(-1)
    interp = jnp.sum(weights * flat_dec[taps], axis=2)
    slots = patch_rows.shape[2]
    live = jnp.arange(slots, dtype=jnp.int32)[None, None, :] < counts[:, :, None]
    misfit = jnp.where(live, interp - observed, 0.0)
    contrib = weights * misfit[:, :, None, :]
    partial_grad = (
        jnp.zeros((rows * patch_size,), jnp.float32).at[taps.reshape(-1)].add(contrib.reshape(-1))
    )
    grad_dec = lax.psum(partial_grad.reshape(rows, patch_size).astype(jnp.bfloat16), "mlp").astype(
        jnp.float32
    )
    guidance = jnp.dot(grad_dec, w_dec.astype(jnp.float32).T, precision=lax.Precision.HIGHEST)
    return (state_out.reshape(seqs, pos, local_width), guidance.reshape(seqs, pos, local_width))


def solution(mesh):
    placed = (
        P(None, "tok", "mlp"),
        P("tok", "mlp"),
        P("mlp", "tok"),
        P(None, "mlp"),
        P("mlp", None),
        P("mlp", None),
        P(),
        P("mlp"),
        P(("tok", "mlp"), None, None),
        P(("tok", "mlp"), None, None),
        P(("tok", "mlp"), None),
        P(("tok", "mlp"), None, None, None),
        P(("tok", "mlp"), None, None),
    )
    return jax.shard_map(
        body,
        mesh=mesh,
        in_specs=placed,
        out_specs=(P(None, "tok", "mlp"), P(None, "tok", "mlp")),
        check_vma=False,
    )
```

profile of v0, /device:TPU:2, one launch (start us, length us, event | category | flops | bytes accessed | tf_op | source)
XLA Modules:
  0.0 455.9 jit_solution(4522725581580568789)
XLA Ops:
  8.0 29.3 %all_gather.15 = bf16[8,16,2048]{2,1,0:T(8,128)(2,1)S(1)} all-gather(bf16[8,16,256]{2,1,0:T(8,128)(2,1)} %param.14), channel_id=1, replica_groups=mesh['tok'=32,'mlp'=8] {'mlp'}, dimensions={2}, use_global_device_ids=true | all-gather | bytes 589824 | tf_op jit(solution)/shard_map/all_gather | solution.py:32
  38.5 24.8 %all-gather.4.cloned.1.call-done = bf16[2048,768]{1,0:T(8,128)(2,1)} async-done(((bf16[64,768]{1,0:T(8,128)(2,1)}), bf16[2048,768]{1,0:T(8,128)(2,1)}) %all-gather.4.cloned.1.call-update) | async-done | bytes 3145744 | tf_op jit(solution)/shard_map/all_gather | solution.py:38
  63.2 2.5 convolution_convert_fusion.2
  67.7 57.1 %all-gather.6.cloned.1.call-done = bf16[2,8,4,512,64]{4,1,2,0,3:T(8,128)(2,1)} async-done(((bf16[2,8,4,16,64]{4,1,2,0,3:T(8,128)(2,1)}), bf16[2,8,4,512,64]{4,1,2,0,3:T(8,128)(2,1)}) %all-gather.6.cloned.1.call-update) | async-done | bytes 4194320 | tf_op jit(solution)/shard_map/all_gather | solution.py:46
  124.8 6.2 %fusion.43 = (bf16[1,8,4,512,64]{4,1,2,0,3:T(8,128)(2,1)}, bf16[1,8,4,512,64]{4,1,2,0,3:T(8,128)(2,1)}) fusion(bf16[2,8,4,512,64]{4,1,2,0,3:T(8,128)(2,1)} %all-gather.6.cloned.1.call-done), kind=kLoop, calls=%fused_computation.62 | loop fusion | bytes 8388608 | tf_op jit(solution)/shard_map/slice | solution.py:49
  131.1 5.5 %copy.41 = bf16[1,8,4,512,64]{3,4,2,1,0:T(8,128)(2,1)} copy(bf16[1,8,4,512,64]{4,1,2,0,3:T(8,128)(2,1)} %get-tuple-element.2) | data formatting | bytes 4194304
  136.5 4.5 copy.42
  141.0 2.1 fusion.44
  144.5 30.1 %all-gather.8.cloned.1.call-done = bf16[256,2048]{0,1:T(8,128)(2,1)} async-done(((bf16[256,64]{0,1:T(8,128)(2,1)}), bf16[256,2048]{0,1:T(8,128)(2,1)}) %all-gather.8.cloned.1.call-update) | async-done | bytes 1048592 | tf_op jit(solution)/shard_map/all_gather | solution.py:62
  174.6 2.5 convolution_convert_fusion.1
  177.2 11.8 %all_to_all.29 = s32[1,32,1]{2,0,1:T(1,128)S(1)} all-to-all(s32[1,32,1]{2,0,1:T(1,128)S(1)} %copy.39), channel_id=1, replica_groups=mesh['tok'=32,'mlp'=8] {'tok'}, dimensions={1} | all-to-all | bytes 256 | tf_op jit(solution)/shard_map/all_to_all | solution.py:87
  188.9 10.7 %all_to_all.30 = s32[1,32,64]{2,0,1:T(1,128)S(1)} all-to-all(s32[1,32,64]{2,0,1:T(1,128)S(1)} %bitcast.92), channel_id=1, replica_groups=mesh['tok'=32,'mlp'=8] {'tok'}, dimensions={1} | all-to-all | bytes 16384 | tf_op jit(solution)/shard_map/all_to_all | solution.py:85
  199.6 4.9 %all-to-all-start.1 = ((s32[1,32,64]{2,0,1:T(1,128)}), s32[1,32,64]{2,0,1:T(1,128)S(1)}, u32[]{:S(2)}, u32[]{:S(2)}) async-start(s32[1,32,64]{2,0,1:T(1,128)} %bitcast.12), calls=%async_computation.3 | async-start | bytes 32768 | tf_op jit(solution)/shard_map/all_to_all | solution.py:86
  206.6 4.2 all-to-all-done.1
  210.7 4.9 %all-to-all-start.2 = ((bf16[32,2,128]{2,1,0:T(2,128)(2,1)}), bf16[32,2,128]{2,1,0:T(2,128)(2,1)S(1)}, u32[]{:S(2)}, u32[]{:S(2)}) async-start(bf16[32,2,128]{2,1,0:T(2,128)(2,1)} %reshape.188), calls=%async_computation.4 | async-start | bytes 32768 | tf_op jit(solution)/shard_map/all_to_all | solution.py:90
  216.9 17.5 %psum.21 = f32[128,1]{0,1:T(1,128)S(1)} all-reduce(f32[128,1]{0,1:T(1,128)S(1)} %bitcast.93), channel_id=1, replica_groups=mesh['tok'=32,'mlp'=8] {'mlp'}, use_global_device_ids=true, to_apply=%region_5.0 | all-reduce | flops 128 | bytes 1024 | tf_op jit(solution)/shard_map/psum | solution.py:69
  235.3 25.4 %all_gather.19 = bf16[128,2048]{1,0:T(8,128)(2,1)S(1)} all-gather(bf16[128,256]{1,0:T(8,128)(2,1)S(1)} %multiply_convert_fusion), channel_id=1, replica_groups=mesh['tok'=32,'mlp'=8] {'mlp'}, dimensions={1}, use_global_device_ids=true | all-gather | bytes 589824 | tf_op jit(solution)/shard_map/all_gather | solution.py:71
  260.7 5.8 %convolution_convert_fusion = bf16[128,2048]{1,0:T(8,128)(2,1)} fusion(bf16[1024,2048]{1,0:T(8,128)(2,1)} %param.18, bf16[128,2048]{1,0:T(8,128)(2,1)S(1)} %all_gather.19, bf16[2048,1024]{1,0:T(8,128)(2,1)} %param.17), kind=kOutput, calls=%fused_computation.2 | convolution fusion | flops 1075183616 | bytes 9437184 | tf_op jit(solution)/shard_map/dot_general | solution.py:75
  266.7 7.5 %all-to-all-start.4 = ((bf16[1,32,64]{2,0,1:T(2,128)(2,1)}), bf16[1,32,64]{2,0,1:T(2,128)(2,1)S(1)}, u32[]{:S(2)}, u32[]{:S(2)}) async-start(bf16[1,32,64]{2,0,1:T(2,128)(2,1)} %copy.40), calls=%async_computation.6 | async-start | bytes 32768 | tf_op jit(solution)/shard_map/all_to_all | solution.py:93
  274.3 28.5 %reduce-scatter.5.cloned.1.call-done = bf16[128,256]{1,0:T(8,128)(2,1)} async-done(((bf16[128,2048]{1,0:T(8,128)(2,1)}), bf16[128,256]{1,0:T(8,128)(2,1)}) %reduce-scatter.5.cloned.1.call-update) | async-done | bytes 65552 | tf_op jit(solution)/shard_map/reduce_scatter | solution.py:76
  303.9 28.4 %psum.22 = bf16[16384]{0:T(1024)(128)(2,1)S(1)} all-reduce(bf16[16384]{0:T(1024)(128)(2,1)S(1)} %fusion.16), channel_id=1, replica_groups=mesh['tok'=32,'mlp'=8] {'mlp'}, use_global_device_ids=true, to_apply=%region_7.0 | all-reduce | flops 16384 | bytes 65536 | tf_op jit(solution)/shard_map/psum | solution.py:80
  332.3 45.5 %gather_fusion = f32[8192]{0:T(1024)S(1)} fusion(f32[16384]{0:T(1024)S(1)} %reshape.162, s32[8192]{0:T(1024)S(1)} %broadcast_clamp_fusion), kind=kCustom, calls=%fused_computation | custom fusion | bytes 98304 | tf_op jit(solution)/shard_map/gather | solution.py:101
  378.2 43.2 %scatter_custom_fusion = f32[16384]{0:T(1024)S(1)} fusion(s32[8192]{0:T(1024)S(1)} %bitcast.91, f32[8192]{0:T(1024)S(1)} %reshape.179, f32[]{:T(128)} %constant.14.clone.1), kind=kCustom, calls=%fused_computation.51 | custom fusion | flops 8192 | bytes 65540 | tf_op jit(solution)/shard_map/scatter-add | solution.py:107
  421.5 27.1 %psum.23 = bf16[128,128]{1,0:T(8,128)(2,1)S(1)} all-reduce(bf16[128,128]{1,0:T(8,128)(2,1)S(1)} %convert_bitcast_fusion), channel_id=1, replica_groups=mesh['tok'=32,'mlp'=8] {'mlp'}, use_global_device_ids=true, to_apply=%region_10.11 | all-reduce | flops 16384 | bytes 65536 | tf_op jit(solution)/shard_map/psum | solution.py:109
  (73 shorter events, 12.1 us)
Async XLA Ops:
  7.2 296.6 %copy-start = (bf16[256,128]{1,0:T(8,128)(2,1)S(1)}, bf16[256,128]{1,0:T(8,128)(2,1)}, u32[]{:S(2)}) copy-start(bf16[256,128]{1,0:T(8,128)(2,1)} %param.19) | copy-start | bytes 196612
  7.2 56.1 %all-gather.4.cloned.1.call-start = ((), (), s32[]{:S(2)}) async-start(), calls=%async_computation.7 | async-start | bytes 3244032 | tf_op jit(solution)/shard_map/all_gather | solution.py:38
  7.9 116.9 %all-gather.6.cloned.1.call-start = ((), (), s32[]{:S(2)}) async-start(), calls=%async_computation.8 | async-start | bytes 8650752 | tf_op jit(solution)/shard_map/all_gather | solution.py:46
  67.0 107.6 %all-gather.8.cloned.1.call-start = ((), (), s32[]{:S(2)}) async-start(), calls=%async_computation.9 | async-start | bytes 1081344 | tf_op jit(solution)/shard_map/all_gather | solution.py:62
  67.7 148.3 %reduce-scatter.3.cloned.1.call-start = ((), (), s32[]{:S(2)}) async-start(), calls=%async_computation.10 | async-start | bytes 589824 | tf_op jit(solution)/shard_map/reduce_scatter | solution.py:65
  143.1 34.0 %copy-start.9 = (s32[1,32]{1,0:T(1,128)S(1)}, s32[1,32]{1,0:T(1,128)}, u32[]{:S(2)}) copy-start(s32[1,32]{1,0:T(1,128)} %param.24) | copy-start | bytes 388
  143.1 45.9 %copy-start.6 = (s32[1,32,64]{2,1,0:T(8,128)S(1)}, s32[1,32,64]{2,1,0:T(8,128)}, u32[]{:S(2)}) copy-start(s32[1,32,64]{2,1,0:T(8,128)} %param.22) | copy-start | bytes 24580
  143.1 61.4 %copy-start.4 = (f32[1,32,4,64]{3,2,1,0:T(4,128)S(1)}, f32[1,32,4,64]{3,2,1,0:T(4,128)}, u32[]{:S(2)}) copy-start(f32[1,32,4,64]{3,2,1,0:T(4,128)} %param.25) | copy-start | bytes 98308
  143.1 62.1 %copy-start.5 = (f32[1,32,64]{2,1,0:T(8,128)S(1)}, f32[1,32,64]{2,1,0:T(8,128)}, u32[]{:S(2)}) copy-start(f32[1,32,64]{2,1,0:T(8,128)} %param.26) | copy-start | bytes 24580
  143.1 72.6 %copy-start.7 = (s32[4]{0:T(128)S(1)}, s32[4]{0:T(128)}, u32[]{:S(2)}) copy-start(s32[4]{0:T(128)} %constant.13.clone) | copy-start | bytes 52
  143.1 72.8 %copy-start.1 = (bf16[8,16,256]{2,1,0:T(8,128)(2,1)S(1)}, bf16[8,16,256]{2,1,0:T(8,128)(2,1)}, u32[]{:S(2)}) copy-start(bf16[8,16,256]{2,1,0:T(8,128)(2,1)} %param.14) | copy-start | bytes 196612
  143.2 91.2 %copy-start.8 = (f32[256]{0:T(256)S(1)}, f32[256]{0:T(256)}, u32[]{:S(2)}) copy-start(f32[256]{0:T(256)} %param.21) | copy-start | bytes 3076
  199.6 11.1 %all-to-all-start.1 = ((s32[1,32,64]{2,0,1:T(1,128)}), s32[1,32,64]{2,0,1:T(1,128)S(1)}, u32[]{:S(2)}, u32[]{:S(2)}) async-start(s32[1,32,64]{2,0,1:T(1,128)} %bitcast.12), calls=%async_computation.3 | async-start | bytes 32768 | tf_op jit(solution)/shard_map/all_to_all | solution.py:86
  210.7 56.0 %all-to-all-start.2 = ((bf16[32,2,128]{2,1,0:T(2,128)(2,1)}), bf16[32,2,128]{2,1,0:T(2,128)(2,1)S(1)}, u32[]{:S(2)}, u32[]{:S(2)}) async-start(bf16[32,2,128]{2,1,0:T(2,128)(2,1)} %reshape.188), calls=%async_computation.4 | async-start | bytes 32768 | tf_op jit(solution)/shard_map/all_to_all | solution.py:90
  215.7 87.2 %reduce-scatter.5.cloned.1.call-start = ((), (), s32[]{:S(2)}) async-start(), calls=%async_computation.11 | async-start | bytes 589824 | tf_op jit(solution)/shard_map/reduce_scatter | solution.py:76
  260.7 42.1 %copy-start.2 = (bf16[128,256]{1,0:T(8,128)(2,1)S(1)}, bf16[128,256]{1,0:T(8,128)(2,1)}, u32[]{:S(2)}) copy-start(bf16[128,256]{1,0:T(8,128)(2,1)} %reduce-scatter.3.cloned.1.call-done) | copy-start | bytes 196612
  266.7 111.2 %all-to-all-start.4 = ((bf16[1,32,64]{2,0,1:T(2,128)(2,1)}), bf16[1,32,64]{2,0,1:T(2,128)(2,1)S(1)}, u32[]{:S(2)}, u32[]{:S(2)}) async-start(bf16[1,32,64]{2,0,1:T(2,128)(2,1)} %copy.40), calls=%async_computation.6 | async-start | bytes 32768 | tf_op jit(solution)/shard_map/all_to_all | solution.py:93
  303.7 74.1 %copy-start.3 = (bf16[128,256]{1,0:T(8,128)(2,1)}, bf16[128,256]{1,0:T(8,128)(2,1)S(1)}, u32[]{:S(2)}) copy-start(bf16[128,256]{1,0:T(8,128)(2,1)S(1)} %add_convert_fusion) | copy-start | bytes 196612
Sparse Core Ops, SparseCore 0:
  10.6 52.6 all-gather.3
  67.1 57.7 all-gather.5
  127.4 47.1 all-gather.7
  177.2 36.9 reduce-scatter.2
  266.6 36.1 reduce-scatter.4
where the time goes:
time: 457 us; the launch traced here: 456 us
  blocking collectives  150 us (33%)
  waiting for transfers between devices  146 us (32%)
  local copies, waits for them, and re-layouts  65.1 us (14%)
  other arithmetic  48.5 us (11%)
  starting transfers between devices  17.6 us (4%)
  matrix products  14.5 us (3%)
  between operations  14.1 us (3%)
    all_gather x1, waiting for transfers between devices, body(): piece = lax.all_gather(keyval, 'tok', axis=3, tiled=True)  57.1 us
    gather x2, local copies, waits for them, and re-layouts, body(): interp = jnp.sum(weights * flat_dec[taps], axis=2)  45.6 us
    scatter-add x1, other arithmetic, body(): jnp.zeros((rows * patch_size,), jnp.float32).at[taps.reshape(-1)]  43.2 us
    all_gather x1, waiting for transfers between devices, body(): lax.all_gather(w_out, 'tok', axis=1, tiled=True)  30.1 us
    all_gather x1, blocking collectives, body(): full = lax.all_gather(states, 'mlp', axis=2, tiled=True)  29.3 us
    reduce_scatter x1, waiting for transfers between devices, body(): lax.psum_scatter(down.astype(jnp.bfloat16), 'mlp', scatter_dimension=1, t...  28.5 us
    psum x1, blocking collectives, body(): lax.psum(jnp.dot(state_out, w_dec, preferred_element_type=jnp.float32).as...  28.4 us
    psum x1, blocking collectives, body(): lax.psum(partial_grad.reshape(rows, patch_size).astype(jnp.bfloat16), 'mlp')  27.1 us
  transfers between devices with their start and end apart: 8, of which 5 were waited for; matrix products, arithmetic and copies ran while one was open for 17% of the time, Pallas kernels for 0%

commit v1 on v0

v1 whole, which is shorter than its diff:
```python
import functools

import jax
import jax.numpy as jnp
from jax import lax
from jax.experimental import pallas as pl
from jax.experimental.pallas import tpu as pltpu
from jax.sharding import PartitionSpec as P

D = 2048
HD = 64
EPS = 1e-06
BF = jnp.bfloat16
F32 = jnp.float32
NT = (((1,), (1,)), ((), ()))
GELU = 0.7978845608028654
STEPS = (0, 1, 15, 16, 17)


def params(mib):
    return pltpu.CompilerParams(vmem_limit_bytes=mib * 1024 * 1024)


def lanes(shape):
    return lax.broadcasted_iota(jnp.int32, shape, len(shape) - 1)


def half(x):
    return pltpu.roll(x, 64, 1)


def left(shape):
    return lanes(shape) < 64


def pack_kernel(wqkv, wout_t, obs, out):
    n = out.shape[0]
    for dest in range(n):
        c = dest % 2
        for j in range(3):
            out[dest, 64 * j : 64 * j + 64, :] = wqkv[:, 256 * j + 128 * c : 256 * j + 128 * c + 128]
        out[dest, 192:256, :] = wout_t[:, 128 * c : 128 * c + 128]
    out[:, 256:272, :] = obs[...]


def norm_kernel(me, *refs):
    packs, sib, gain = refs[:8], refs[8], refs[9]
    normed, wdec, ginv = refs[10:]
    m = me[0]
    own_sq = jnp.zeros((128, 1), F32)
    sib_sq = jnp.zeros((128, 1), F32)
    for d in range(8):
        a = packs[d][0:128, :].astype(F32)
        b = sib[d].astype(F32)
        own_sq += jnp.sum(a * a, axis=1, keepdims=True)
        sib_sq += jnp.sum(b * b, axis=1, keepdims=True)
    own_r = lax.rsqrt(own_sq / D + EPS)
    sib_r = lax.rsqrt(sib_sq / D + EPS)
    for d in range(8):
        at = lax.rem(m - d + 8, 8)
        g = gain[at]
        normed[at, 0:128, :] = (packs[d][0:128, :].astype(F32) * own_r * g).astype(BF)
        normed[at, 128:256, :] = (sib[d].astype(F32) * sib_r * g).astype(BF)
        wdec[at, 0:128, :] = packs[d][144:272, 0:128]
        wdec[at, 128:256, :] = packs[d][144:272, 128:256]
        rows = packs[d][128:144, :].astype(F32)
        total = rows[0:1, :] + rows[1:2, :] + rows[2:3, :]
        ginv[at] = 1.0 / total


def qkv_kernel(normed, w, out):
    acc = jnp.zeros((256, 384), F32)
    for k in range(8):
        cols = [w[4 * k : 4 * k + 4, 64 * j : 64 * j + 64, :].reshape(256, 128) for j in range(3)]
        acc += jnp.dot(normed[k], jnp.concatenate(cols, axis=1), preferred_element_type=F32)
    q, k, v = acc[:, 0:128], acc[:, 128:256], acc[:, 256:384]
    low = left((256, 128))
    pairs = (jnp.where(low, q, half(k)), jnp.where(low, half(q), k))
    own, sib = v[0:128], v[128:256]
    low = left((128, 128))
    values = (jnp.where(low, own, half(sib)), jnp.where(low, half(own), sib))
    for g in range(2):
        qk = pairs[g].astype(BF)
        vv = values[g].astype(BF)
        for s in range(8):
            out[2 * s + g, 0:16, :] = qk[16 * s : 16 * s + 16, :]
            out[2 * s + g, 16:32, :] = qk[128 + 16 * s : 144 + 16 * s, :]
            out[2 * s + g, 32:48, :] = vv[16 * s : 16 * s + 16, :]


def attend_kernel(got, out):
    qk_own = got[:, 0:16, :].reshape(256, 128)
    qk_sib = got[:, 16:32, :].reshape(256, 128)
    vv = got[:, 32:48, :].reshape(256, 128)
    low = left((256, 128))

    def mix(qk):
        query = (jnp.where(low, 0.0, half(qk.astype(F32))) * (1.0 / HD**0.5)).astype(BF)
        first = lax.dot_general(query, qk_own, NT, preferred_element_type=F32)
        second = lax.dot_general(query, qk_sib, NT, preferred_element_type=F32)
        top = jnp.maximum(
            jnp.max(first, axis=1, keepdims=True), jnp.max(second, axis=1, keepdims=True)
        )
        first = jnp.exp(first - top)
        second = jnp.exp(second - top)
        total = jnp.sum(first, axis=1, keepdims=True) + jnp.sum(second, axis=1, keepdims=True)
        one = jnp.dot(first.astype(BF), vv, preferred_element_type=F32)
        two = jnp.dot(second.astype(BF), vv, preferred_element_type=F32)
        return (one + half(two)) / total

    mixed = jnp.where(low, mix(qk_own), half(mix(qk_sib)))
    out[...] = mixed.astype(BF).reshape(16, 16, 128)


def heads_of(got, own):
    a = got[:, 0].reshape(128, 128).astype(F32)
    b = got[:, 1].reshape(128, 128).astype(F32)
    low = left((128, 128))
    if own:
        return jnp.where(low, a, half(b)).astype(BF)
    return jnp.where(low, half(a), b).astype(BF)


def give_kernel(got, w, out):
    rows = heads_of(got, False)
    out[...] = lax.dot_general(
        rows, w[...].reshape(D, 128), NT, preferred_element_type=F32
    ).astype(BF)


def keep_kernel(got, w, other, normal, out):
    rows = heads_of(got, True)
    total = lax.dot_general(rows, w[...].reshape(D, 128), NT, preferred_element_type=F32)
    total = (total + other[...].astype(F32)).astype(BF)
    for z in range(8):
        out[z, 0:128, :] = total[:, 256 * z : 256 * z + 256]
    out[:, 128:176, :] = normal[...]


def normal_kernel(obs, out, hot, high, lows):
    low = left((16, 128))
    cells = lax.broadcasted_iota(jnp.int32, (128, 128), 0)
    for pair in range(16):
        a = obs[2 * pair].astype(F32)
        b = obs[2 * pair + 1].astype(F32)
        one = jnp.where(low, a, half(b))
        two = jnp.where(low, half(a), b)
        patch = one[0:1].astype(jnp.int32)
        base = two[0:1].astype(jnp.int32)
        w0 = one[1:2] + one[4:5]
        w1 = two[1:2] + two[4:5]
        w2 = one[2:3] + one[5:6]
        w3 = two[2:3] + two[5:6]
        v = one[3:4] + two[3:4]
        rel = cells - base
        e0, e1, e2, e3 = rel == 0, rel == 1, rel == 16, rel == 17
        zero = jnp.zeros((128, 128), F32)

        def place(x0, x1, x2, x3):
            out = zero
            for e, x in ((e0, x0), (e1, x1), (e2, x2), (e3, x3)):
                if x is not None:
                    out = jnp.where(e, x, out)
            return out

        terms = (
            place(w0 * w0, w1 * w1, w2 * w2, w3 * w3),
            place(w0 * w1, None, w2 * w3, None),
            place(None, w1 * w2, None, None),
            place(w0 * w2, w1 * w3, None, None),
            place(w0 * w3, None, None, None),
            place(v * w0, v * w1, v * w2, v * w3),
        )
        at = slice(128 * pair, 128 * pair + 128)
        hot[:, at] = jnp.where(cells == patch, 1.0, 0.0).astype(BF)
        for i, term in enumerate(terms):
            top = term.astype(BF)
            high[128 * i : 128 * i + 128, at] = top
            lows[128 * i : 128 * i + 128, at] = (term - top.astype(F32)).astype(BF)
    total = lax.dot_general(hot[...], high[...], NT, preferred_element_type=F32)
    total += lax.dot_general(hot[...], lows[...], NT, preferred_element_type=F32)
    total = total.astype(BF)
    for w in range(8):
        for i in range(6):
            out[w, 16 * (i % 3) : 16 * (i % 3) + 16, 128 * (i // 3) : 128 * (i // 3) + 128] = total[
                16 * w : 16 * w + 16, 128 * i : 128 * i + 128
            ]


def resid_kernel(got, x, gain, resid, out):
    attn = got[0, 0:128, :].astype(F32)
    normal = got[0, 128:176, :].astype(F32)
    for k in range(1, 8):
        attn += got[k, 0:128, :].astype(F32)
        normal += got[k, 128:176, :].astype(F32)
    total = x[...].astype(F32) + attn
    resid[...] = total
    scaled = (total * gain[...]).astype(BF)
    normal = normal.astype(BF)
    for k in range(8):
        out[k, 0:128, :] = scaled
        out[k, 128:176, :] = normal


def ffn_kernel(got, ginv, up, down, wdec, resid, own_dec, out, acc, scale):
    step = pl.program_id(0)

    @pl.when(step == 0)
    def _():
        squares = jnp.zeros((128, 1), F32)
        for k in range(8):
            a = got[k, 0:128, :].astype(F32) * ginv[k]
            squares += jnp.sum(a * a, axis=1, keepdims=True)
        scale[...] = jnp.broadcast_to(lax.rsqrt(squares / D + EPS), (128, 128))

    wide = jnp.concatenate([got[k, 0:128, :] for k in range(8)], axis=1)
    pre = jnp.dot(wide, up[...], preferred_element_type=F32) * scale[:, 0:1]
    hidden = 0.5 * pre * (1.0 + jnp.tanh(GELU * (pre + 0.044715 * (pre * pre * pre))))
    part = jnp.dot(hidden.astype(BF), down[...], preferred_element_type=F32)

    @pl.when(step == 0)
    def _():
        acc[...] = part

    @pl.when(step > 0)
    def _():
        acc[...] += part

    @pl.when(step == pl.num_programs(0) - 1)
    def _():
        total = acc[...].astype(BF)
        decoded = jnp.dot(total, wdec[...].reshape(D, 128), preferred_element_type=F32)
        decoded += jnp.dot(resid[...].astype(BF), own_dec[...], preferred_element_type=F32)
        decoded = decoded.astype(BF)
        for z in range(8):
            out[z, :, 0:256] = total[:, 256 * z : 256 * z + 256]
            out[z, :, 256:384] = decoded


def final_kernel(got, resid, normal, own_dec, state, guidance):
    total = resid[...]
    decoded = jnp.zeros((128, 128), F32)
    for k in range(8):
        total += got[k, :, 0:256].astype(F32)
        decoded += got[k, :, 256:384].astype(F32)
    state[...] = total.astype(BF)

    def diag(i):
        rows = slice(16 * (i % 3), 16 * (i % 3) + 16)
        cols = slice(128 * (i // 3), 128 * (i // 3) + 128)
        return normal[:, rows, cols].reshape(128, 128).astype(F32)

    grad = diag(0) * decoded - diag(5)
    for i, d in enumerate(STEPS):
        if i:
            a = diag(i)
            grad += a * pltpu.roll(decoded, 128 - d, 1) + pltpu.roll(a * decoded, d, 1)
    guidance[...] = lax.dot_general(
        grad,
        own_dec[...].astype(F32),
        NT,
        precision=lax.Precision.HIGHEST,
        preferred_element_type=F32,
    )


def sds(shape, dtype=BF):
    return jax.ShapeDtypeStruct(shape, dtype)


def body(
    states,
    w_qkv,
    w_out,
    w_up,
    w_down,
    w_dec,
    gain_attn,
    gain_mlp,
    obs_patch,
    obs_base,
    obs_count,
    obs_weight,
    obs_value,
):
    n_tok, n_mlp = 32, 8
    x = states.reshape(128, 256)
    me = lax.axis_index("mlp").astype(jnp.int32).reshape(1)
    pairs = [(i, i ^ 1) for i in range(n_tok)]
    chips = [[2 * i + c for i in range(16)] for c in range(2)]

    live = jnp.arange(64, dtype=jnp.int32)[None, :] < obs_count[0][:, None]
    weights = jnp.where(live[:, None, :], obs_weight[0], 0.0)
    values = jnp.where(live, obs_value[0], 0.0)
    weights_hi = lax.reduce_precision(weights, 8, 7)
    values_hi = lax.reduce_precision(values, 8, 7)
    rows = [
        jnp.concatenate([obs_patch[0], obs_base[0]], axis=1).astype(F32)[:, None, :],
        weights_hi.reshape(32, 2, 128),
        jnp.concatenate([values_hi, values - values_hi], axis=1)[:, None, :],
        (weights - weights_hi).reshape(32, 2, 128),
        jnp.zeros((32, 10, 128), F32),
    ]
    obs = jnp.concatenate(rows, axis=1).astype(BF)

    send = pl.pallas_call(pack_kernel, out_shape=sds((32, 272, 128)), compiler_params=params(24))(
        w_qkv, w_out.T, obs
    )
    weights_in = lax.all_to_all(send, "tok", 0, 0, tiled=True)

    g_hi = lax.reduce_precision(gain_mlp, 8, 7)
    g_mid = lax.reduce_precision(gain_mlp - g_hi, 8, 7)
    g_low = gain_mlp - g_hi - g_mid
    gains = jnp.concatenate([jnp.stack([g_hi, g_mid, g_low]), jnp.zeros((13, 256), F32)], axis=0)
    pack = jnp.concatenate(
        [x, gains.astype(BF), jnp.concatenate([w_dec[:128], w_dec[128:]], axis=1)], axis=0
    )
    packs = [pack] + [
        lax.ppermute(pack, "mlp", [(i, (i + d) % n_mlp) for i in range(n_mlp)])
        for d in range(1, n_mlp)
    ]
    sibling = lax.ppermute(jnp.stack([p[:128] for p in packs]), "tok", pairs)
    normed, wdec, ginv = pl.pallas_call(
        norm_kernel,
        out_shape=(sds((8, 256, 256)), sds((8, 256, 128)), sds((8, 1, 256), F32)),
        in_specs=[pl.BlockSpec(memory_space=pltpu.SMEM)]
        + [pl.BlockSpec(memory_space=pltpu.VMEM)] * 10,
        compiler_params=params(24),
    )(me, *packs, sibling, gain_attn.reshape(8, 1, 256))

    qkv = pl.pallas_call(
        qkv_kernel,
        grid=(1,),
        in_specs=[
            pl.BlockSpec((8, 256, 256), lambda i: (0, 0, 0)),
            pl.BlockSpec((32, 192, 128), lambda i: (0, 0, 0)),
        ],
        out_specs=pl.BlockSpec((16, 48, 128), lambda i: (0, 0, 0)),
        out_shape=sds((16, 48, 128)),
        compiler_params=params(24),
    )(normed, weights_in)
    qkv_in = lax.all_to_all(qkv, "tok", 0, 0, tiled=True, axis_index_groups=chips)

    normal = pl.pallas_call(
        normal_kernel,
        grid=(1,),
        in_specs=[pl.BlockSpec((32, 16, 128), lambda i: (0, 16, 0))],
        out_specs=pl.BlockSpec((8, 48, 256), lambda i: (0, 0, 0)),
        out_shape=sds((8, 48, 256)),
        scratch_shapes=[
            pltpu.VMEM((128, 2048), BF),
            pltpu.VMEM((768, 2048), BF),
            pltpu.VMEM((768, 2048), BF),
        ],
        compiler_params=params(24),
    )(weights_in)

    attended = pl.pallas_call(
        attend_kernel, out_shape=sds((16, 16, 128)), compiler_params=params(24)
    )(qkv_in)
    back = lax.all_to_all(attended, "tok", 0, 0, tiled=True, axis_index_groups=chips)
    back = back.reshape(8, 2, 16, 128)

    out_spec = pl.BlockSpec((32, 64, 128), lambda i: (0, 3, 0))
    back_spec = pl.BlockSpec((8, 2, 16, 128), lambda i: (0, 0, 0, 0))
    flat_spec = pl.BlockSpec((128, D), lambda i: (0, 0))
    give = pl.pallas_call(
        give_kernel,
        grid=(1,),
        in_specs=[back_spec, out_spec],
        out_specs=flat_spec,
        out_shape=sds((128, D)),
        compiler_params=params(24),
    )(back, weights_in)
    taken = lax.ppermute(give, "tok", pairs)
    shares = pl.pallas_call(
        keep_kernel,
        grid=(1,),
        in_specs=[
            back_spec,
            out_spec,
            flat_spec,
            pl.BlockSpec((8, 48, 256), lambda i: (0, 0, 0)),
        ],
        out_specs=pl.BlockSpec((8, 176, 256), lambda i: (0, 0, 0)),
        out_shape=sds((8, 176, 256)),
        compiler_params=params(24),
    )(back, weights_in, taken, normal)
    shares_in = lax.all_to_all(shares, "mlp", 0, 0, tiled=True)

    resid, scaled = pl.pallas_call(
        resid_kernel,
        out_shape=(sds((128, 256), F32), sds((8, 176, 256))),
        compiler_params=params(24),
    )(shares_in, x, gain_mlp.reshape(1, 256))
    wide = lax.all_to_all(scaled, "mlp", 0, 0, tiled=True)

    whole = lambda *shape: pl.BlockSpec(shape, lambda i: (0,) * len(shape))
    chunk = 256
    down = pl.pallas_call(
        ffn_kernel,
        grid=(1024 // chunk,),
        in_specs=[
            whole(8, 176, 256),
            whole(8, 1, 256),
            pl.BlockSpec((D, chunk), lambda i: (0, i)),
            pl.BlockSpec((chunk, D), lambda i: (i, 0)),
            whole(8, 256, 128),
            whole(128, 256),
            whole(256, 128),
        ],
        out_specs=whole(8, 128, 384),
        out_shape=sds((8, 128, 384)),
        scratch_shapes=[pltpu.VMEM((128, D), F32), pltpu.VMEM((128, 128), F32)],
        compiler_params=params(32),
    )(wide, ginv, w_up, w_down, wdec, resid, w_dec)
    down_in = lax.all_to_all(down, "mlp", 0, 0, tiled=True)

    state, guidance = pl.pallas_call(
        final_kernel,
        grid=(1,),
        in_specs=[
            whole(8, 128, 384),
            whole(128, 256),
            whole(8, 48, 256),
            whole(256, 128),
        ],
        out_specs=(whole(128, 256), whole(128, 256)),
        out_shape=(sds((128, 256)), sds((128, 256), F32)),
        compiler_params=params(24),
    )(down_in, resid, wide[:, 128:176, :], w_dec)
    return state.reshape(8, 16, 256), guidance.reshape(8, 16, 256)


def solution(mesh):
    placed = (
        P(None, "tok", "mlp"),
        P("tok", "mlp"),
        P("mlp", "tok"),
        P(None, "mlp"),
        P("mlp", None),
        P("mlp", None),
        P(),
        P("mlp"),
        P(("tok", "mlp"), None, None),
        P(("tok", "mlp"), None, None),
        P(("tok", "mlp"), None),
        P(("tok", "mlp"), None, None, None),
        P(("tok", "mlp"), None, None),
    )
    return jax.shard_map(
        body,
        mesh=mesh,
        in_specs=placed,
        out_specs=(P(None, "tok", "mlp"), P(None, "tok", "mlp")),
        check_vma=False,
    )
```

time: 457 us -> 189 us (0.41)
  waiting for transfers between devices: 146 us -> 45.2 us
  blocking collectives: 150 us -> 77.1 us
  other arithmetic: 48.5 us -> 3.21 us
  local copies, waits for them, and re-layouts: 65.1 us -> 22 us
  matrix products: 14.5 us -> 0 us
  Pallas kernels: 0 us -> 13.9 us
  between operations: 14.1 us -> 0.93 us
  starting transfers between devices: 17.6 us -> 25.3 us
    all_gather x3 -> x0, waiting for transfers between devices: 112 us -> none  [the longest x1 57.1 us: body(): piece = lax.all_gather(keyval, 'tok', axis=3, tiled=True)]
    psum x3 -> x0, blocking collectives: 72.9 us -> none  [the longest x1 28.4 us: body(): lax.psum(jnp.dot(state_out, w_dec, preferred_element_type=jnp.float32).as...]
    all_to_all x2 -> x4, blocking collectives: 22.4 us -> 77.1 us  [the longest x1 27.9 us: body(): shares_in = lax.all_to_all(shares, 'mlp', 0, 0, tiled=True)]
    all_gather x2 -> x0, blocking collectives: 54.7 us -> none  [the longest x1 29.3 us: body(): full = lax.all_gather(states, 'mlp', axis=2, tiled=True)]
    gather x2 -> x0, local copies, waits for them, and re-layouts: 45.6 us -> none  [body(): interp = jnp.sum(weights * flat_dec[taps], axis=2)]
    scatter-add x1 -> x0, other arithmetic: 43.2 us -> none  [body(): jnp.zeros((rows * patch_size,), jnp.float32).at[taps.reshape(-1)]]
    reduce_scatter x2 -> x0, waiting for transfers between devices: 28.5 us -> none  [the longest x1 28.5 us: body(): lax.psum_scatter(down.astype(jnp.bfloat16), 'mlp', scatter_dimension=1, t...]
    ppermute x0 -> x9, waiting for transfers between devices: none -> 21.9 us  [the longest x7 19.7 us: body(): lax.ppermute(pack, 'mlp', [(i, (i + d) % n_mlp) for i in range(n_mlp)])]
  transfers between devices with their start and end apart: 8 -> 11, of which waited for: 5 -> 4; matrix products, arithmetic and copies ran while one was open for 17% -> 5% of each run, Pallas kernels for 0% -> 3%
where the time goes in v1:
time: 189 us; the launch traced here: 188 us
  blocking collectives  77.1 us (41%)
  waiting for transfers between devices  45.2 us (24%)
  starting transfers between devices  25.3 us (13%)
  local copies, waits for them, and re-layouts  22 us (12%)
  Pallas kernels  13.9 us (7%)
  other arithmetic  3.21 us (2%)
    all_to_all x1, blocking collectives, body(): shares_in = lax.all_to_all(shares, 'mlp', 0, 0, tiled=True)  27.9 us
    all_to_all x1, blocking collectives, body(): wide = lax.all_to_all(scaled, 'mlp', 0, 0, tiled=True)  24.6 us
    all_to_all x1, waiting for transfers between devices, body(): down_in = lax.all_to_all(down, 'mlp', 0, 0, tiled=True)  23.4 us
    ppermute x7, waiting for transfers between devices, body(): lax.ppermute(pack, 'mlp', [(i, (i + d) % n_mlp) for i in range(n_mlp)])  19.7 us
    unnamed x61, local copies, waits for them, and re-layouts  17.9 us
    all_to_all x1, blocking collectives, body(): lax.all_to_all(qkv, 'tok', 0, 0, tiled=True, axis_index_groups=chips)  14 us
    ppermute x7, starting transfers between devices, body(): lax.ppermute(pack, 'mlp', [(i, (i + d) % n_mlp) for i in range(n_mlp)])  13.9 us
    all_to_all x1, blocking collectives, body(): lax.all_to_all(attended, 'tok', 0, 0, tiled=True, axis_index_groups=chips)  10.7 us
  transfers between devices with their start and end apart: 11, of which 4 were waited for; matrix products, arithmetic and copies ran while one was open for 5% of the time, Pallas kernels for 3%

profile of v1, /device:TPU:2, one launch (start us, length us, event | category | flops | bytes accessed | tf_op | source)
XLA Modules:
  0.0 187.8 jit_solution(15437152055703998761)
XLA Ops:
  2.2 1.0 concatenate.32.refs_0_
  3.2 5.9 %collective-permute-start.6 = (bf16[272,256]{1,0:T(8,128)(2,1)S(1)}, bf16[272,256]{1,0:T(8,128)(2,1)S(1)}, u32[]{:S(2)}, u32[]{:S(2)}) collective-permute-start(bf16[272,256]{1,0:T(8,128)(2,1)S(1)} %concatenate.32.refs_0_), channel_id=1, source_target_pairs={{0,7},{1,0},{2,1},{3,2},{4,3},{5,4},{6,5},{7,6},{8,15},{9,8},{10,9... | collective-permute-start | bytes 417800 | tf_op jit(solution)/shard_map/ppermute | solution.py:319
  9.1 1.5 collective-permute-start.5
  11.0 5.0 %collective-permute-start.3 = (bf16[272,256]{1,0:T(8,128)(2,1)S(1)}, bf16[272,256]{1,0:T(8,128)(2,1)S(1)}, u32[]{:S(2)}, u32[]{:S(2)}) collective-permute-start(bf16[272,256]{1,0:T(8,128)(2,1)S(1)} %concatenate.32.refs_0_), channel_id=1, source_target_pairs={{0,4},{1,5},{2,6},{3,7},{4,0},{5,1},{6,2},{7,3},{8,12},{9,13},{10,... | collective-permute-start | bytes 417800 | tf_op jit(solution)/shard_map/ppermute | solution.py:319
  16.0 1.0 collective-permute-start
  18.7 0.9 squeeze.8
  23.2 1.4 copy-done
  24.5 7.6 %all-to-all-start = ((bf16[32,272,128]{2,1,0:T(8,128)(2,1)}), bf16[32,272,128]{2,1,0:T(8,128)(2,1)S(1)}, u32[]{:S(2)}, u32[]{:S(2)}) async-start(bf16[32,272,128]{2,1,0:T(8,128)(2,1)} %copy-done), calls=%async_computation | async-start | bytes 4456448 | tf_op jit(solution)/shard_map/all_to_all | solution.py:309
  33.5 10.1 %collective-permute-done.1.refs_2_ = bf16[272,256]{1,0:T(8,128)(2,1)S(1)} collective-permute-done((bf16[272,256]{1,0:T(8,128)(2,1)S(1)}, bf16[272,256]{1,0:T(8,128)(2,1)S(1)}, u32[]{:S(2)}, u32[]{:S(2)}) %collective-permute-start.1) | collective-permute-done | bytes 139296 | tf_op jit(solution)/shard_map/ppermute | solution.py:319
  44.3 9.6 %collective-permute-done.2.refs_3_ = bf16[272,256]{1,0:T(8,128)(2,1)S(1)} collective-permute-done((bf16[272,256]{1,0:T(8,128)(2,1)S(1)}, bf16[272,256]{1,0:T(8,128)(2,1)S(1)}, u32[]{:S(2)}, u32[]{:S(2)}) %collective-permute-start.2) | collective-permute-done | bytes 139296 | tf_op jit(solution)/shard_map/ppermute | solution.py:319
  58.5 2.1 %collective-permute-done.7.refs_8_ = bf16[8,128,256]{2,1,0:T(8,128)(2,1)S(1)} collective-permute-done((bf16[8,128,256]{2,1,0:T(8,128)(2,1)}, bf16[8,128,256]{2,1,0:T(8,128)(2,1)S(1)}, u32[]{:S(2)}, u32[]{:S(2)}) %collective-permute-start.7) | collective-permute-done | bytes 524320 | tf_op jit(solution)/shard_map/ppermute | solution.py:322
  61.4 1.0 copy-done.8
  62.5 0.9 copy-done.10
  63.4 0.9 copy-done.12
  71.2 14.0 %all_to_all.30.got = bf16[16,48,128]{2,1,0:T(8,128)(2,1)S(1)} all-to-all(bf16[16,48,128]{2,1,0:T(8,128)(2,1)S(1)} %shard_map.142), channel_id=1, replica_groups={{0,16,32,48,64,80,96,112,128,144,160,176,192,208,224,240},{8,24,40,56,7..., dimensions={0} | all-to-all | bytes 393216 | tf_op jit(solution)/shard_map/all_to_all | solution.py:342
  85.2 0.9 shard_map.143
  86.1 10.7 %all_to_all.31 = bf16[16,16,128]{2,1,0:T(8,128)(2,1)S(1)} all-to-all(bf16[16,16,128]{2,1,0:T(8,128)(2,1)S(1)} %shard_map.143), channel_id=1, replica_groups={{0,16,32,48,64,80,96,112,128,144,160,176,192,208,224,240},{8,24,40,56,7..., dimensions={0} | all-to-all | bytes 131072 | tf_op jit(solution)/shard_map/all_to_all | solution.py:361
  97.4 3.7 %shard_map.145.normal = bf16[8,48,256]{2,1,0:T(8,128)(2,1)S(1)} custom-call(bf16[32,272,128]{2,1,0:T(8,128)(2,1)S(1)} %all-to-all-done.w.obs), custom_call_target="tpu_custom_call" | custom-call | tf_op jit(solution)/shard_map/pallas_call | solution.py:344
  101.6 27.9 %all_to_all.32.got = bf16[8,176,256]{2,1,0:T(8,128)(2,1)S(1)} all-to-all(bf16[8,176,256]{2,1,0:T(8,128)(2,1)S(1)} %shard_map.146), channel_id=1, replica_groups=mesh['tok'=32,'mlp'=8] {'mlp'}, dimensions={0} | all-to-all | bytes 1441792 | tf_op jit(solution)/shard_map/all_to_all | solution.py:389
  129.5 24.6 %all_to_all.33.got = bf16[8,176,256]{2,1,0:T(8,128)(2,1)S(1)} all-to-all(bf16[8,176,256]{2,1,0:T(8,128)(2,1)S(1)} %get-tuple-element.10), channel_id=1, replica_groups=mesh['tok'=32,'mlp'=8] {'mlp'}, dimensions={0} | all-to-all | bytes 1441792 | tf_op jit(solution)/shard_map/all_to_all | solution.py:396
  154.2 5.6 %shard_map.148 = bf16[8,128,384]{2,1,0:T(8,128)(2,1)} custom-call(bf16[8,176,256]{2,1,0:T(8,128)(2,1)S(1)} %all_to_all.33.got, f32[8,1,256]{2,1,0:T(1,128)S(1)} %get-tuple-element.11.ginv, bf16[2048,1024]{1,0:T(8,128)(2,1)S(1)} %copy-done.1, bf16[1024,2048]{1,0:T(8,128)(2,1)S(1)} %copy-done.2, bf16[8,256,128]{2,1,0:T(8,128)(2,1)S(1)} %copy-done.6, ...), custom_call_target="tpu_custom_call" | custom-call | tf_op jit(solution)/shard_map/pallas_call | solution.py:400
  159.7 3.5 %all-to-all-start.5 = ((bf16[8,128,384]{2,1,0:T(8,128)(2,1)}), bf16[8,128,384]{2,1,0:T(8,128)(2,1)S(1)}, u32[]{:S(2)}, u32[]{:S(2)}) async-start(bf16[8,128,384]{2,1,0:T(8,128)(2,1)} %shard_map.148), calls=%async_computation.5 | async-start | bytes 1572864 | tf_op jit(solution)/shard_map/all_to_all | solution.py:417
  163.3 23.4 %all-to-all-done.5.got = bf16[8,128,384]{2,1,0:T(8,128)(2,1)S(1)} async-done(((bf16[8,128,384]{2,1,0:T(8,128)(2,1)}), bf16[8,128,384]{2,1,0:T(8,128)(2,1)S(1)}, u32[]{:S(2)}, u32[]{:S(2)}) %all-to-all-start.5) | async-done | bytes 786464 | tf_op jit(solution)/shard_map/all_to_all | solution.py:417
  186.7 1.1 shard_map.149
  (94 shorter events, 22.4 us)
Async XLA Ops:
  0.6 31.5 %copy-start.4 = (bf16[8,16,256]{2,1,0:T(8,128)(2,1)S(1)}, bf16[8,16,256]{2,1,0:T(8,128)(2,1)}, u32[]{:S(2)}) copy-start(bf16[8,16,256]{2,1,0:T(8,128)(2,1)} %param.13) | copy-start | bytes 196612
  3.2 54.0 %collective-permute-start.6 = (bf16[272,256]{1,0:T(8,128)(2,1)S(1)}, bf16[272,256]{1,0:T(8,128)(2,1)S(1)}, u32[]{:S(2)}, u32[]{:S(2)}) collective-permute-start(bf16[272,256]{1,0:T(8,128)(2,1)S(1)} %concatenate.32.refs_0_), channel_id=1, source_target_pairs={{0,7},{1,0},{2,1},{3,2},{4,3},{5,4},{6,5},{7,6},{8,15},{9,8},{10,9... | collective-permute-start | bytes 417800 | tf_op jit(solution)/shard_map/ppermute | solution.py:319
  9.1 46.8 %collective-permute-start.5 = (bf16[272,256]{1,0:T(8,128)(2,1)S(1)}, bf16[272,256]{1,0:T(8,128)(2,1)S(1)}, u32[]{:S(2)}, u32[]{:S(2)}) collective-permute-start(bf16[272,256]{1,0:T(8,128)(2,1)S(1)} %concatenate.32.refs_0_), channel_id=1, source_target_pairs={{0,6},{1,7},{2,0},{3,1},{4,2},{5,3},{6,4},{7,5},{8,14},{9,15},{10,... | collective-permute-start | bytes 417800 | tf_op jit(solution)/shard_map/ppermute | solution.py:319
  10.6 44.7 %collective-permute-start.4 = (bf16[272,256]{1,0:T(8,128)(2,1)S(1)}, bf16[272,256]{1,0:T(8,128)(2,1)S(1)}, u32[]{:S(2)}, u32[]{:S(2)}) collective-permute-start(bf16[272,256]{1,0:T(8,128)(2,1)S(1)} %concatenate.32.refs_0_), channel_id=1, source_target_pairs={{0,5},{1,6},{2,7},{3,0},{4,1},{5,2},{6,3},{7,4},{8,13},{9,14},{10,... | collective-permute-start | bytes 417800 | tf_op jit(solution)/shard_map/ppermute | solution.py:319
  11.0 43.6 %collective-permute-start.3 = (bf16[272,256]{1,0:T(8,128)(2,1)S(1)}, bf16[272,256]{1,0:T(8,128)(2,1)S(1)}, u32[]{:S(2)}, u32[]{:S(2)}) collective-permute-start(bf16[272,256]{1,0:T(8,128)(2,1)S(1)} %concatenate.32.refs_0_), channel_id=1, source_target_pairs={{0,4},{1,5},{2,6},{3,7},{4,0},{5,1},{6,2},{7,3},{8,12},{9,13},{10,... | collective-permute-start | bytes 417800 | tf_op jit(solution)/shard_map/ppermute | solution.py:319
  16.0 16.8 %collective-permute-start = (bf16[272,256]{1,0:T(8,128)(2,1)S(1)}, bf16[272,256]{1,0:T(8,128)(2,1)S(1)}, u32[]{:S(2)}, u32[]{:S(2)}) collective-permute-start(bf16[272,256]{1,0:T(8,128)(2,1)S(1)} %concatenate.32.refs_0_), channel_id=1, source_target_pairs={{0,1},{1,2},{2,3},{3,4},{4,5},{5,6},{6,7},{7,0},{8,9},{9,10},{10,1... | collective-permute-start | bytes 417800 | tf_op jit(solution)/shard_map/ppermute | solution.py:319
  20.7 40.7 %copy-start.25 = (f32[2048]{0:T(1024)S(1)}, f32[2048]{0:T(1024)}, u32[]{:S(2)}) copy-start(f32[2048]{0:T(1024)} %param.19) | copy-start | bytes 24580
  23.2 1.4 copy-start
  24.5 45.8 %all-to-all-start = ((bf16[32,272,128]{2,1,0:T(8,128)(2,1)}), bf16[32,272,128]{2,1,0:T(8,128)(2,1)S(1)}, u32[]{:S(2)}, u32[]{:S(2)}) async-start(bf16[32,272,128]{2,1,0:T(8,128)(2,1)} %copy-done), calls=%async_computation | async-start | bytes 4456448 | tf_op jit(solution)/shard_map/all_to_all | solution.py:309
  32.8 28.6 %copy-start.17 = (bf16[272,256]{1,0:T(8,128)(2,1)}, bf16[272,256]{1,0:T(8,128)(2,1)S(1)}, u32[]{:S(2)}) copy-start(bf16[272,256]{1,0:T(8,128)(2,1)S(1)} %collective-permute-done.refs_1_) | copy-start | bytes 417796
  32.8 10.8 %collective-permute-start.1 = (bf16[272,256]{1,0:T(8,128)(2,1)S(1)}, bf16[272,256]{1,0:T(8,128)(2,1)S(1)}, u32[]{:S(2)}, u32[]{:S(2)}) collective-permute-start(bf16[272,256]{1,0:T(8,128)(2,1)S(1)} %concatenate.32.refs_0_), channel_id=1, source_target_pairs={{0,2},{1,3},{2,4},{3,5},{4,6},{5,7},{6,0},{7,1},{8,10},{9,11},{10,... | collective-permute-start | bytes 417800 | tf_op jit(solution)/shard_map/ppermute | solution.py:319
  43.6 17.8 %copy-start.19 = (bf16[272,256]{1,0:T(8,128)(2,1)}, bf16[272,256]{1,0:T(8,128)(2,1)S(1)}, u32[]{:S(2)}) copy-start(bf16[272,256]{1,0:T(8,128)(2,1)S(1)} %collective-permute-done.1.refs_2_) | copy-start | bytes 417796
  43.6 10.3 %collective-permute-start.2 = (bf16[272,256]{1,0:T(8,128)(2,1)S(1)}, bf16[272,256]{1,0:T(8,128)(2,1)S(1)}, u32[]{:S(2)}, u32[]{:S(2)}) collective-permute-start(bf16[272,256]{1,0:T(8,128)(2,1)S(1)} %concatenate.32.refs_0_), channel_id=1, source_target_pairs={{0,3},{1,4},{2,5},{3,6},{4,7},{5,0},{6,1},{7,2},{8,11},{9,12},{10,... | collective-permute-start | bytes 417800 | tf_op jit(solution)/shard_map/ppermute | solution.py:319
  53.9 7.5 %copy-start.21 = (bf16[272,256]{1,0:T(8,128)(2,1)}, bf16[272,256]{1,0:T(8,128)(2,1)S(1)}, u32[]{:S(2)}) copy-start(bf16[272,256]{1,0:T(8,128)(2,1)S(1)} %collective-permute-done.2.refs_3_) | copy-start | bytes 417796
  54.6 2.6 %copy-start.15 = (bf16[272,256]{1,0:T(8,128)(2,1)}, bf16[272,256]{1,0:T(8,128)(2,1)S(1)}, u32[]{:S(2)}) copy-start(bf16[272,256]{1,0:T(8,128)(2,1)S(1)} %collective-permute-done.3.refs_4_) | copy-start | bytes 417796
  55.2 2.0 %copy-start.13 = (bf16[272,256]{1,0:T(8,128)(2,1)}, bf16[272,256]{1,0:T(8,128)(2,1)S(1)}, u32[]{:S(2)}) copy-start(bf16[272,256]{1,0:T(8,128)(2,1)S(1)} %collective-permute-done.4.refs_5_) | copy-start | bytes 417796
  58.5 2.1 %collective-permute-start.7 = (bf16[8,128,256]{2,1,0:T(8,128)(2,1)}, bf16[8,128,256]{2,1,0:T(8,128)(2,1)S(1)}, u32[]{:S(2)}, u32[]{:S(2)}) collective-permute-start(bf16[8,128,256]{2,1,0:T(8,128)(2,1)} %fusion), channel_id=1, source_target_pairs={{0,8},{8,0},{16,24},{24,16},{32,40},{40,32},{48,56},{56,48},{64,72... | collective-permute-start | bytes 1572872 | tf_op jit(solution)/shard_map/ppermute | solution.py:322
  97.1 32.3 %copy-start.26 = (f32[256]{0:T(256)S(1)}, f32[256]{0:T(256)}, u32[]{:S(2)}) copy-start(f32[256]{0:T(256)} %param.20) | copy-start | bytes 3076
  97.1 4.1 %collective-permute-start.8 = (bf16[128,2048]{1,0:T(8,128)(2,1)S(1)}, bf16[128,2048]{1,0:T(8,128)(2,1)S(1)}, u32[]{:S(2)}, u32[]{:S(2)}) collective-permute-start(bf16[128,2048]{1,0:T(8,128)(2,1)S(1)} %shard_map.144), channel_id=1, source_target_pairs={{0,8},{8,0},{16,24},{24,16},{32,40},{40,32},{48,56},{56,48},{64,72... | collective-permute-start | bytes 1572872 | tf_op jit(solution)/shard_map/ppermute | solution.py:375
  97.4 56.7 %copy-start.2 = (bf16[1024,2048]{1,0:T(8,128)(2,1)S(1)}, bf16[1024,2048]{1,0:T(8,128)(2,1)}, u32[]{:S(2)}) copy-start(bf16[1024,2048]{1,0:T(8,128)(2,1)} %down.1) | copy-start | bytes 12582916
  101.2 53.0 %copy-start.1 = (bf16[2048,1024]{1,0:T(8,128)(2,1)S(1)}, bf16[2048,1024]{1,0:T(8,128)(2,1)}, u32[]{:S(2)}) copy-start(bf16[2048,1024]{1,0:T(8,128)(2,1)} %up.1) | copy-start | bytes 12582916
  101.2 53.0 %copy-start.3 = (bf16[256,128]{1,0:T(8,128)(2,1)S(1)}, bf16[256,128]{1,0:T(8,128)(2,1)}, u32[]{:S(2)}) copy-start(bf16[256,128]{1,0:T(8,128)(2,1)} %own_dec.3) | copy-start | bytes 196612
  101.2 53.0 %copy-start.6 = (bf16[8,256,128]{2,1,0:T(8,128)(2,1)S(1)}, bf16[8,256,128]{2,1,0:T(8,128)(2,1)}, u32[]{:S(2)}) copy-start(bf16[8,256,128]{2,1,0:T(8,128)(2,1)} %copy-done.5) | copy-start | bytes 1572868
  159.7 27.0 %all-to-all-start.5 = ((bf16[8,128,384]{2,1,0:T(8,128)(2,1)}), bf16[8,128,384]{2,1,0:T(8,128)(2,1)S(1)}, u32[]{:S(2)}, u32[]{:S(2)}) async-start(bf16[8,128,384]{2,1,0:T(8,128)(2,1)} %shard_map.148), calls=%async_computation.5 | async-start | bytes 1572864 | tf_op jit(solution)/shard_map/all_to_all | solution.py:417
  (14 other events, 11.9 us)

commit v2 on v1

v2 whole, which is shorter than its diff:
```python
import functools

import jax
import jax.numpy as jnp
from jax import lax
from jax.experimental import pallas as pl
from jax.experimental.pallas import tpu as pltpu
from jax.sharding import PartitionSpec as P

D = 2048
HD = 64
EPS = 1e-06
BF = jnp.bfloat16
F32 = jnp.float32
NT = (((1,), (1,)), ((), ()))
GELU = 0.7978845608028654
STEPS = (0, 1, 15, 16, 17)


def params(mib):
    return pltpu.CompilerParams(vmem_limit_bytes=mib * 1024 * 1024)


def lanes(shape):
    return lax.broadcasted_iota(jnp.int32, shape, len(shape) - 1)


def half(x):
    return pltpu.roll(x, 64, 1)


def left(shape):
    return lanes(shape) < 64


def pack_kernel(counts, wqkv, wout_t, x, gain, wdec, patch, base, weight, value, out, pack):
    n = out.shape[0]
    slots = lanes((4, 64))
    zero = jnp.zeros((1, 64), F32)
    rest = jnp.zeros((12, 128), F32)
    for dest in range(n):
        c = dest % 2
        for j in range(3):
            out[dest, 64 * j : 64 * j + 64, :] = wqkv[:, 256 * j + 128 * c : 256 * j + 128 * c + 128]
        out[dest, 192:256, :] = wout_t[:, 128 * c : 128 * c + 128]
        row = slice(dest, dest + 1)
        live = slots < counts[0, dest]
        w = jnp.where(live, weight[0, dest], 0.0)
        v = jnp.where(live[0:1], value[0, row, :], 0.0)
        other = [v, patch[0, row, :].astype(F32), base[0, row, :].astype(F32), zero]
        both = jnp.concatenate([w, jnp.concatenate(other, axis=0)], axis=1)
        out[dest, 256:272, :] = jnp.concatenate([both, rest], axis=0).astype(BF)
    pack[0:128, :] = x[...]
    g = gain[...]
    high = g.astype(BF).astype(F32)
    mid = (g - high).astype(BF).astype(F32)
    low = g - high - mid
    pack[128:144, :] = jnp.concatenate([high, mid, low, jnp.zeros((13, 256), F32)], axis=0).astype(BF)
    pack[144:272, 0:128] = wdec[0:128, :]
    pack[144:272, 128:256] = wdec[128:256, :]


def norm_kernel(me, *refs):
    packs, gain = refs[:8], refs[8]
    normed, wdec, ginv = refs[9:]
    m = me[0]
    squares = jnp.zeros((128, 1), F32)
    for d in range(8):
        a = packs[d][0:128, :].astype(F32)
        squares += jnp.sum(a * a, axis=1, keepdims=True)
    r = lax.rsqrt(squares / D + EPS)
    for d in range(8):
        at = lax.rem(m - d + 8, 8)
        normed[at] = (packs[d][0:128, :].astype(F32) * r * gain[at]).astype(BF)
        wdec[at, 0:128, :] = packs[d][144:272, 0:128]
        wdec[at, 128:256, :] = packs[d][144:272, 128:256]
        rows = packs[d][128:144, :].astype(F32)
        ginv[at] = 1.0 / (rows[0:1, :] + rows[1:2, :] + rows[2:3, :])


def qkv_kernel(mine, sibling, w, out, slots):
    acc = jnp.zeros((256, 384), F32)
    for k in range(8):
        cols = [w[4 * k : 4 * k + 4, 64 * j : 64 * j + 64, :].reshape(256, 128) for j in range(3)]
        rows = jnp.concatenate([mine[k], sibling[k]], axis=0)
        acc += jnp.dot(rows, jnp.concatenate(cols, axis=1), preferred_element_type=F32)
    q, k, v = acc[:, 0:128], acc[:, 128:256], acc[:, 256:384]
    low = left((256, 128))
    pairs = (jnp.where(low, q, half(k)), jnp.where(low, half(q), k))
    own, sib = v[0:128], v[128:256]
    low = left((128, 128))
    values = (jnp.where(low, own, half(sib)), jnp.where(low, half(own), sib))
    for g in range(2):
        qk = pairs[g].astype(BF)
        vv = values[g].astype(BF)
        for s in range(8):
            out[2 * s + g, 0:16, :] = qk[16 * s : 16 * s + 16, :]
            out[2 * s + g, 16:32, :] = qk[128 + 16 * s : 144 + 16 * s, :]
            out[2 * s + g, 32:48, :] = vv[16 * s : 16 * s + 16, :]
    low = left((16, 128))
    tiles = []
    for pair in range(16):
        a = w[2 * pair, 256:272, :].astype(F32)
        b = w[2 * pair + 1, 256:272, :].astype(F32)
        tiles.append(jnp.where(low, a, half(b))[0:4])
        tiles.append(jnp.where(low, half(a), b)[0:4])
    slots[...] = jnp.concatenate(tiles, axis=0).astype(BF)


def attend_kernel(got, out):
    qk_own = got[:, 0:16, :].reshape(256, 128)
    qk_sib = got[:, 16:32, :].reshape(256, 128)
    vv = got[:, 32:48, :].reshape(256, 128)
    low = left((256, 128))

    def mix(qk):
        query = (jnp.where(low, 0.0, half(qk.astype(F32))) * (1.0 / HD**0.5)).astype(BF)
        first = lax.dot_general(query, qk_own, NT, preferred_element_type=F32)
        second = lax.dot_general(query, qk_sib, NT, preferred_element_type=F32)
        top = jnp.maximum(
            jnp.max(first, axis=1, keepdims=True), jnp.max(second, axis=1, keepdims=True)
        )
        first = jnp.exp(first - top)
        second = jnp.exp(second - top)
        total = jnp.sum(first, axis=1, keepdims=True) + jnp.sum(second, axis=1, keepdims=True)
        one = jnp.dot(first.astype(BF), vv, preferred_element_type=F32)
        two = jnp.dot(second.astype(BF), vv, preferred_element_type=F32)
        return (one + half(two)) / total

    mixed = jnp.where(low, mix(qk_own), half(mix(qk_sib)))
    out[...] = mixed.astype(BF).reshape(16, 16, 128)


def heads_of(got, own):
    a = got[:, 0].reshape(128, 128).astype(F32)
    b = got[:, 1].reshape(128, 128).astype(F32)
    low = left((128, 128))
    if own:
        return jnp.where(low, a, half(b)).astype(BF)
    return jnp.where(low, half(a), b).astype(BF)


def give_kernel(got, w, out):
    rows = heads_of(got, False)
    out[...] = lax.dot_general(
        rows, w[...].reshape(D, 128), NT, preferred_element_type=F32
    ).astype(BF)


def keep_kernel(got, w, other, out):
    rows = heads_of(got, True)
    total = lax.dot_general(rows, w[...].reshape(D, 128), NT, preferred_element_type=F32)
    total = (total + other[...].astype(F32)).astype(BF)
    for z in range(8):
        out[z] = total[:, 256 * z : 256 * z + 256]


def normal_kernel(*refs):
    n = len(refs) - 4
    slots, start, out, hot, terms = refs[:n], refs[n], refs[n + 1], refs[n + 2], refs[n + 3]
    cells = lax.broadcasted_iota(jnp.int32, (128, 128), 0).astype(F32).astype(BF)
    zero = jnp.zeros((128, 128), BF)
    one = jnp.ones((128, 128), BF)

    def place(*picks):
        out = zero
        for e, x in picks:
            out = jnp.where(e, jnp.broadcast_to(x.astype(BF), (128, 128)), out)
        return out

    total = start[...]
    for k in range(n):

        def pair(i, _):
            rows = slots[k][pl.ds(pl.multiple_of(16 * i, 16), 16), :].astype(F32)
            for h in range(2):
                t = rows[8 * h : 8 * h + 8]
                w0, w1, w2, w3, v = (t[j : j + 1] for j in range(5))
                rel = cells - jnp.broadcast_to(t[6:7].astype(BF), (128, 128))
                e0, e1, e2, e3 = rel == 0, rel == 1, rel == 16, rel == 17
                parts = (
                    place((e0, w0 * w0), (e1, w1 * w1), (e2, w2 * w2), (e3, w3 * w3)),
                    place((e0, w0 * w1), (e2, w2 * w3)),
                    place((e1, w1 * w2)),
                    place((e0, w0 * w2), (e1, w1 * w3)),
                    place((e0, w0 * w3)),
                    place((e0, v * w0), (e1, v * w1), (e2, v * w2), (e3, v * w3)),
                )
                at = pl.ds(pl.multiple_of(256 * i + 128 * h, 128), 128)
                patch = jnp.broadcast_to(t[5:6].astype(BF), (128, 128))
                hot[:, at] = jnp.where(cells == patch, one, zero)
                for j, part in enumerate(parts):
                    terms[128 * j : 128 * j + 128, at] = part
            return 0

        lax.fori_loop(0, 8, pair, 0)
        total += lax.dot_general(hot[...], terms[...], NT, preferred_element_type=F32)
    out[...] = total


def resid_kernel(got, x, gain, resid, out):
    total = x[...].astype(F32)
    for k in range(8):
        total += got[k].astype(F32)
    resid[...] = total
    scaled = (total * gain[...]).astype(BF)
    for k in range(8):
        out[k] = scaled


def ffn_kernel(got, ginv, up, down, wdec, resid, own_dec, out):
    squares = jnp.zeros((128, 1), F32)
    for k in range(8):
        a = got[k].astype(F32) * ginv[k]
        squares += jnp.sum(a * a, axis=1, keepdims=True)
    scale = lax.rsqrt(squares / D + EPS)
    wide = jnp.concatenate([got[k] for k in range(8)], axis=1)
    hidden = []
    for i in range(4):
        pre = jnp.dot(wide, up[:, 256 * i : 256 * i + 256], preferred_element_type=F32) * scale
        act = 0.5 * pre * (1.0 + jnp.tanh(GELU * (pre + 0.044715 * (pre * pre * pre))))
        hidden.append(act.astype(BF))
    hidden = jnp.concatenate(hidden, axis=1)
    decoded = jnp.dot(resid[...].astype(BF), own_dec[...], preferred_element_type=F32)
    for z in range(8):
        part = jnp.dot(hidden, down[:, 256 * z : 256 * z + 256], preferred_element_type=F32)
        part = part.astype(BF)
        out[z, :, 0:256] = part
        decoded += jnp.dot(part, wdec[z], preferred_element_type=F32)
    decoded = decoded.astype(BF)
    for z in range(8):
        out[z, :, 256:384] = decoded


def final_kernel(got, resid, normal, own_dec, state, guidance):
    total = resid[...]
    decoded = jnp.zeros((128, 128), F32)
    for k in range(8):
        total += got[k, :, 0:256].astype(F32)
        decoded += got[k, :, 256:384].astype(F32)
    state[...] = total.astype(BF)
    grad = normal[:, 0:128] * decoded - normal[:, 640:768]
    for i, d in enumerate(STEPS):
        if i:
            a = normal[:, 128 * i : 128 * i + 128]
            grad += a * pltpu.roll(decoded, 128 - d, 1) + pltpu.roll(a * decoded, d, 1)
    guidance[...] = lax.dot_general(
        grad,
        own_dec[...].astype(F32),
        NT,
        precision=lax.Precision.HIGHEST,
        preferred_element_type=F32,
    )


def sds(shape, dtype=BF):
    return jax.ShapeDtypeStruct(shape, dtype)


def body(
    states,
    w_qkv,
    w_out,
    w_up,
    w_down,
    w_dec,
    gain_attn,
    gain_mlp,
    obs_patch,
    obs_base,
    obs_count,
    obs_weight,
    obs_value,
):
    n_tok, n_mlp = 32, 8
    x = states.reshape(128, 256)
    me = lax.axis_index("mlp").astype(jnp.int32).reshape(1)
    pairs = [(i, i ^ 1) for i in range(n_tok)]
    chips = [[2 * i + c for i in range(16)] for c in range(2)]
    ring = [[(i, (i + d) % n_mlp) for i in range(n_mlp)] for d in range(n_mlp)]
    vmem = pl.BlockSpec(memory_space=pltpu.VMEM)
    smem = pl.BlockSpec(memory_space=pltpu.SMEM)
    whole = lambda *shape: pl.BlockSpec(shape, lambda i: (0,) * len(shape))

    send, pack = pl.pallas_call(
        pack_kernel,
        in_specs=[smem] + [vmem] * 9,
        out_shape=(sds((32, 272, 128)), sds((272, 256))),
        compiler_params=params(8),
    )(
        obs_count,
        w_qkv,
        w_out.T,
        x,
        gain_mlp.reshape(1, 256),
        w_dec,
        obs_patch,
        obs_base,
        obs_weight,
        obs_value,
    )
    weights_in = lax.all_to_all(send, "tok", 0, 0, tiled=True)
    packs = [pack] + [lax.ppermute(pack, "mlp", ring[d]) for d in range(1, n_mlp)]
    normed, wdec, ginv = pl.pallas_call(
        norm_kernel,
        out_shape=(sds((8, 128, 256)), sds((8, 256, 128)), sds((8, 1, 256), F32)),
        in_specs=[smem] + [vmem] * 9,
        compiler_params=params(8),
    )(me, *packs, gain_attn.reshape(8, 1, 256))
    sibling = lax.ppermute(normed, "tok", pairs)

    qkv, slots = pl.pallas_call(
        qkv_kernel,
        out_shape=(sds((16, 48, 128)), sds((128, 128))),
        compiler_params=params(8),
    )(normed, sibling, weights_in)
    qkv_in = lax.all_to_all(qkv, "tok", 0, 0, tiled=True, axis_index_groups=chips)
    slots_in = [slots] + [lax.ppermute(slots, "mlp", ring[d]) for d in range(1, n_mlp)]

    attended = pl.pallas_call(
        attend_kernel, out_shape=sds((16, 16, 128)), compiler_params=params(8)
    )(qkv_in)
    back = lax.all_to_all(attended, "tok", 0, 0, tiled=True, axis_index_groups=chips)
    back = back.reshape(8, 2, 16, 128)

    out_spec = pl.BlockSpec((32, 64, 128), lambda i: (0, 3, 0))
    give = pl.pallas_call(
        give_kernel,
        grid=(1,),
        in_specs=[whole(8, 2, 16, 128), out_spec],
        out_specs=whole(128, D),
        out_shape=sds((128, D)),
        compiler_params=params(8),
    )(back, weights_in)
    taken = lax.ppermute(give, "tok", pairs)
    shares = pl.pallas_call(
        keep_kernel,
        grid=(1,),
        in_specs=[whole(8, 2, 16, 128), out_spec, whole(128, D)],
        out_specs=whole(8, 128, 256),
        out_shape=sds((8, 128, 256)),
        compiler_params=params(8),
    )(back, weights_in, taken)
    shares_in = lax.all_to_all(shares, "mlp", 0, 0, tiled=True)

    def normals(parts, start):
        return pl.pallas_call(
            normal_kernel,
            out_shape=sds((128, 768), F32),
            scratch_shapes=[pltpu.VMEM((128, 2048), BF), pltpu.VMEM((768, 2048), BF)],
            compiler_params=params(12),
            cost_estimate=pl.CostEstimate(
                flops=len(parts) * 500_000_000, bytes_accessed=1_000_000, transcendentals=0
            ),
        )(*parts, start)

    normal = normals(slots_in[:4], jnp.zeros((128, 768), F32))
    shares_in, normal = lax.optimization_barrier((shares_in, normal))

    resid, scaled = pl.pallas_call(
        resid_kernel,
        out_shape=(sds((128, 256), F32), sds((8, 128, 256))),
        compiler_params=params(8),
    )(shares_in, x, gain_mlp.reshape(1, 256))
    wide = lax.all_to_all(scaled, "mlp", 0, 0, tiled=True)
    normal = normals(slots_in[4:], normal)
    wide, normal = lax.optimization_barrier((wide, normal))

    down = pl.pallas_call(
        ffn_kernel, out_shape=sds((8, 128, 384)), compiler_params=params(24)
    )(wide, ginv, w_up, w_down, wdec, resid, w_dec)
    down_in = lax.all_to_all(down, "mlp", 0, 0, tiled=True)

    state, guidance = pl.pallas_call(
        final_kernel,
        out_shape=(sds((128, 256)), sds((128, 256), F32)),
        compiler_params=params(8),
    )(down_in, resid, normal, w_dec)
    return state.reshape(8, 16, 256), guidance.reshape(8, 16, 256)


def solution(mesh):
    placed = (
        P(None, "tok", "mlp"),
        P("tok", "mlp"),
        P("mlp", "tok"),
        P(None, "mlp"),
        P("mlp", None),
        P("mlp", None),
        P(),
        P("mlp"),
        P(("tok", "mlp"), None, None),
        P(("tok", "mlp"), None, None),
        P(("tok", "mlp"), None),
        P(("tok", "mlp"), None, None, None),
        P(("tok", "mlp"), None, None),
    )
    return jax.shard_map(
        body,
        mesh=mesh,
        in_specs=placed,
        out_specs=(P(None, "tok", "mlp"), P(None, "tok", "mlp")),
        check_vma=False,
    )
```

time: 189 us -> 205 us (1.085)
  blocking collectives: 77.1 us -> 52.2 us
  starting transfers between devices: 25.3 us -> 49.5 us
  Pallas kernels: 13.9 us -> 31.9 us
  local copies, waits for them, and re-layouts: 22 us -> 25.9 us
  other arithmetic: 3.21 us -> 0 us
    all_to_all x2 -> x1, blocking collectives: 52.5 us -> 27.5 us  [body(): down_in = lax.all_to_all(down, 'mlp', 0, 0, tiled=True)]
    all_to_all x1 -> x2, waiting for transfers between devices: 23.4 us -> 0.01 us  [the longest x1 0.01 us: body(): shares_in = lax.all_to_all(shares, 'mlp', 0, 0, tiled=True)]
    ppermute x8 -> x15, starting transfers between devices: 13.9 us -> 34 us  [the longest x7 17.6 us: body(): lax.ppermute(slots, 'mlp', ring[d])]
    ppermute x8 -> x15, waiting for transfers between devices: 21.9 us -> 41.5 us  [the longest x7 21.5 us: body(): lax.ppermute(slots, 'mlp', ring[d])]
    pallas_call x9 -> x10, Pallas kernels: 13 us -> 30.9 us  [the longest x2 22.3 us: normals(): pl.pallas_call(normal_kernel, out_shape=sds((128, 768), F32), scratch_sha...]
    unnamed x61 -> x66, local copies, waits for them, and re-layouts: 17.9 us -> 25.8 us
    all_to_all x1 -> x2, starting transfers between devices: 3.55 us -> 7.78 us  [the longest x1 4.16 us: body(): wide = lax.all_to_all(scaled, 'mlp', 0, 0, tiled=True)]
    another operation x4 -> x0, other arithmetic: 2.39 us -> none
  transfers between devices with their start and end apart: 11 -> 19, of which waited for: 4 -> 12; matrix products, arithmetic and copies ran while one was open for 5% -> 0% of each run, Pallas kernels for 3% -> 11%
where the time goes in v2:
time: 205 us; the launch traced here: 204 us
  blocking collectives  52.2 us (25%)
  starting transfers between devices  49.5 us (24%)
  waiting for transfers between devices  43.4 us (21%)
  Pallas kernels  31.9 us (16%)
  local copies, waits for them, and re-layouts  25.9 us (13%)
    all_to_all x1, blocking collectives, body(): down_in = lax.all_to_all(down, 'mlp', 0, 0, tiled=True)  27.5 us
    unnamed x66, local copies, waits for them, and re-layouts  25.8 us
    pallas_call x2, Pallas kernels, normals(): pl.pallas_call(normal_kernel, out_shape=sds((128, 768), F32), scratch_sha...  22.3 us
    ppermute x7, waiting for transfers between devices, body(): lax.ppermute(slots, 'mlp', ring[d])  21.5 us
    ppermute x7, waiting for transfers between devices, body(): lax.ppermute(pack, 'mlp', ring[d])  18 us
    ppermute x7, starting transfers between devices, body(): lax.ppermute(slots, 'mlp', ring[d])  17.6 us
    ppermute x7, starting transfers between devices, body(): lax.ppermute(pack, 'mlp', ring[d])  16.4 us
    all_to_all x1, blocking collectives, body(): lax.all_to_all(qkv, 'tok', 0, 0, tiled=True, axis_index_groups=chips)  14 us
  transfers between devices with their start and end apart: 19, of which 12 were waited for; matrix products, arithmetic and copies ran while one was open for 0% of the time, Pallas kernels for 11%

profile of v2, /device:TPU:2, one launch (start us, length us, event | category | flops | bytes accessed | tf_op | source)
XLA Modules:
  0.0 203.6 jit_solution(15290935535001964666)
XLA Ops:
  10.6 7.6 %all-to-all-start = ((bf16[32,272,128]{2,1,0:T(8,128)(2,1)}), bf16[32,272,128]{2,1,0:T(8,128)(2,1)S(1)}, u32[]{:S(2)}, u32[]{:S(2)}) async-start(bf16[32,272,128]{2,1,0:T(8,128)(2,1)} %copy-done.2), calls=%async_computation | async-start | bytes 4456448 | tf_op jit(solution)/shard_map/all_to_all | solution.py:302
  18.2 5.9 %collective-permute-start.6 = (bf16[272,256]{1,0:T(8,128)(2,1)S(1)}, bf16[272,256]{1,0:T(8,128)(2,1)S(1)}, u32[]{:S(2)}, u32[]{:S(2)}) collective-permute-start(bf16[272,256]{1,0:T(8,128)(2,1)S(1)} %get-tuple-element.17.refs_0_), channel_id=1, source_target_pairs={{0,7},{1,0},{2,1},{3,2},{4,3},{5,4},{6,5},{7,6},{8,15},{9,8},{10,9... | collective-permute-start | bytes 417800 | tf_op jit(solution)/shard_map/ppermute | solution.py:303
  26.0 5.0 %collective-permute-start.3 = (bf16[272,256]{1,0:T(8,128)(2,1)S(1)}, bf16[272,256]{1,0:T(8,128)(2,1)S(1)}, u32[]{:S(2)}, u32[]{:S(2)}) collective-permute-start(bf16[272,256]{1,0:T(8,128)(2,1)S(1)} %get-tuple-element.17.refs_0_), channel_id=1, source_target_pairs={{0,4},{1,5},{2,6},{3,7},{4,0},{5,1},{6,2},{7,3},{8,12},{9,13},{10,... | collective-permute-start | bytes 417800 | tf_op jit(solution)/shard_map/ppermute | solution.py:303
  31.1 2.5 %collective-permute-start.1 = (bf16[272,256]{1,0:T(8,128)(2,1)S(1)}, bf16[272,256]{1,0:T(8,128)(2,1)S(1)}, u32[]{:S(2)}, u32[]{:S(2)}) collective-permute-start(bf16[272,256]{1,0:T(8,128)(2,1)S(1)} %get-tuple-element.17.refs_0_), channel_id=1, source_target_pairs={{0,2},{1,3},{2,4},{3,5},{4,6},{5,7},{6,0},{7,1},{8,10},{9,11},{10,... | collective-permute-start | bytes 417800 | tf_op jit(solution)/shard_map/ppermute | solution.py:303
  37.1 11.1 %collective-permute-done.4.refs_5_ = bf16[272,256]{1,0:T(8,128)(2,1)S(1)} collective-permute-done((bf16[272,256]{1,0:T(8,128)(2,1)S(1)}, bf16[272,256]{1,0:T(8,128)(2,1)S(1)}, u32[]{:S(2)}, u32[]{:S(2)}) %collective-permute-start.4) | collective-permute-done | bytes 139296 | tf_op jit(solution)/shard_map/ppermute | solution.py:303
  51.4 2.2 %collective-permute-done.1.refs_2_ = bf16[272,256]{1,0:T(8,128)(2,1)S(1)} collective-permute-done((bf16[272,256]{1,0:T(8,128)(2,1)S(1)}, bf16[272,256]{1,0:T(8,128)(2,1)S(1)}, u32[]{:S(2)}, u32[]{:S(2)}) %collective-permute-start.1) | collective-permute-done | bytes 139296 | tf_op jit(solution)/shard_map/ppermute | solution.py:303
  63.7 1.9 collective-permute-done.7.sibling
  68.2 14.0 %all_to_all.30.got = bf16[16,48,128]{2,1,0:T(8,128)(2,1)S(1)} all-to-all(bf16[16,48,128]{2,1,0:T(8,128)(2,1)S(1)} %get-tuple-element.20), channel_id=1, replica_groups={{0,16,32,48,64,80,96,112,128,144,160,176,192,208,224,240},{8,24,40,56,7..., dimensions={0} | all-to-all | bytes 393216 | tf_op jit(solution)/shard_map/all_to_all | solution.py:317
  83.2 10.7 %all_to_all.31 = bf16[16,16,128]{2,1,0:T(8,128)(2,1)S(1)} all-to-all(bf16[16,16,128]{2,1,0:T(8,128)(2,1)S(1)} %shard_map.143), channel_id=1, replica_groups={{0,16,32,48,64,80,96,112,128,144,160,176,192,208,224,240},{8,24,40,56,7..., dimensions={0} | all-to-all | bytes 131072 | tf_op jit(solution)/shard_map/all_to_all | solution.py:323
  97.4 3.6 %all-to-all-start.3 = ((bf16[8,128,256]{2,1,0:T(8,128)(2,1)}), bf16[8,128,256]{2,1,0:T(8,128)(2,1)S(1)}, u32[]{:S(2)}, u32[]{:S(2)}) async-start(bf16[8,128,256]{2,1,0:T(8,128)(2,1)} %shard_map.145), calls=%async_computation.3 | async-start | bytes 1048576 | tf_op jit(solution)/shard_map/all_to_all | solution.py:344
  101.0 3.7 %collective-permute-start.11 = (bf16[128,128]{1,0:T(8,128)(2,1)S(1)}, bf16[128,128]{1,0:T(8,128)(2,1)S(1)}, u32[]{:S(2)}, u32[]{:S(2)}) collective-permute-start(bf16[128,128]{1,0:T(8,128)(2,1)S(1)} %get-tuple-element.21.refs_0_), channel_id=1, source_target_pairs={{0,3},{1,4},{2,5},{3,6},{4,7},{5,0},{6,1},{7,2},{8,11},{9,12},{10,... | collective-permute-start | bytes 98312 | tf_op jit(solution)/shard_map/ppermute | solution.py:318
  104.7 2.7 %collective-permute-start.10 = (bf16[128,128]{1,0:T(8,128)(2,1)S(1)}, bf16[128,128]{1,0:T(8,128)(2,1)S(1)}, u32[]{:S(2)}, u32[]{:S(2)}) collective-permute-start(bf16[128,128]{1,0:T(8,128)(2,1)S(1)} %get-tuple-element.21.refs_0_), channel_id=1, source_target_pairs={{0,2},{1,3},{2,4},{3,5},{4,6},{5,7},{6,0},{7,1},{8,10},{9,11},{10,... | collective-permute-start | bytes 98312 | tf_op jit(solution)/shard_map/ppermute | solution.py:318
  108.0 12.4 %collective-permute-done.11.refs_3_ = bf16[128,128]{1,0:T(8,128)(2,1)S(1)} collective-permute-done((bf16[128,128]{1,0:T(8,128)(2,1)S(1)}, bf16[128,128]{1,0:T(8,128)(2,1)S(1)}, u32[]{:S(2)}, u32[]{:S(2)}) %collective-permute-start.11) | collective-permute-done | bytes 32800 | tf_op jit(solution)/shard_map/ppermute | solution.py:318
  121.1 11.2 %shard_map.146.refs_4_ = f32[128,768]{1,0:T(8,128)S(1)} custom-call(bf16[128,128]{1,0:T(8,128)(2,1)S(1)} %get-tuple-element.21.refs_0_, bf16[128,128]{1,0:T(8,128)(2,1)S(1)} %collective-permute-done.9.refs_1_, bf16[128,128]{1,0:T(8,128)(2,1)S(1)} %collective-permute-done.10.refs_2_, bf16[128,128]{1,0:T(8,128)(2,1)S(1)} %collective-permute-done.11.refs_3_, ...), custom_call_target="tpu_custom_call" | custom-call | flops 2000000000 | bytes 1000000 | tf_op jit(solution)/shard_map/pallas_call | solution.py:347
  133.2 4.2 %all-to-all-start.4 = ((bf16[8,128,256]{2,1,0:T(8,128)(2,1)}), bf16[8,128,256]{2,1,0:T(8,128)(2,1)S(1)}, u32[]{:S(2)}, u32[]{:S(2)}) async-start(bf16[8,128,256]{2,1,0:T(8,128)(2,1)} %get-tuple-element.23), calls=%async_computation.4 | async-start | bytes 1048576 | tf_op jit(solution)/shard_map/all_to_all | solution.py:365
  137.3 3.2 %collective-permute-start.15 = (bf16[128,128]{1,0:T(8,128)(2,1)S(1)}, bf16[128,128]{1,0:T(8,128)(2,1)S(1)}, u32[]{:S(2)}, u32[]{:S(2)}) collective-permute-start(bf16[128,128]{1,0:T(8,128)(2,1)S(1)} %get-tuple-element.21.refs_0_), channel_id=1, source_target_pairs={{0,7},{1,0},{2,1},{3,2},{4,3},{5,4},{6,5},{7,6},{8,15},{9,8},{10,9... | collective-permute-start | bytes 98312 | tf_op jit(solution)/shard_map/ppermute | solution.py:318
  140.6 2.4 %collective-permute-start.14 = (bf16[128,128]{1,0:T(8,128)(2,1)S(1)}, bf16[128,128]{1,0:T(8,128)(2,1)S(1)}, u32[]{:S(2)}, u32[]{:S(2)}) collective-permute-start(bf16[128,128]{1,0:T(8,128)(2,1)S(1)} %get-tuple-element.21.refs_0_), channel_id=1, source_target_pairs={{0,6},{1,7},{2,0},{3,1},{4,2},{5,3},{6,4},{7,5},{8,14},{9,15},{10,... | collective-permute-start | bytes 98312 | tf_op jit(solution)/shard_map/ppermute | solution.py:318
  144.4 3.6 %collective-permute-start.12 = (bf16[128,128]{1,0:T(8,128)(2,1)S(1)}, bf16[128,128]{1,0:T(8,128)(2,1)S(1)}, u32[]{:S(2)}, u32[]{:S(2)}) collective-permute-start(bf16[128,128]{1,0:T(8,128)(2,1)S(1)} %get-tuple-element.21.refs_0_), channel_id=1, source_target_pairs={{0,4},{1,5},{2,6},{3,7},{4,0},{5,1},{6,2},{7,3},{8,12},{9,13},{10,... | collective-permute-start | bytes 98312 | tf_op jit(solution)/shard_map/ppermute | solution.py:318
  148.0 6.9 %collective-permute-done.15.refs_3_ = bf16[128,128]{1,0:T(8,128)(2,1)S(1)} collective-permute-done((bf16[128,128]{1,0:T(8,128)(2,1)S(1)}, bf16[128,128]{1,0:T(8,128)(2,1)S(1)}, u32[]{:S(2)}, u32[]{:S(2)}) %collective-permute-start.15) | collective-permute-done | bytes 32800 | tf_op jit(solution)/shard_map/ppermute | solution.py:318
  156.4 11.1 %shard_map.148.normal = f32[128,768]{1,0:T(8,128)S(1)} custom-call(bf16[128,128]{1,0:T(8,128)(2,1)S(1)} %collective-permute-done.12.refs_0_, bf16[128,128]{1,0:T(8,128)(2,1)S(1)} %collective-permute-done.13.refs_1_, bf16[128,128]{1,0:T(8,128)(2,1)S(1)} %collective-permute-done.14.refs_2_, bf16[128,128]{1,0:T(8,128)(2,1)S(1)} %collective-permute-done.15.refs_3_, ...), custom_call_target="tpu_custom_call" | custom-call | flops 2000000000 | bytes 1000000 | tf_op jit(solution)/shard_map/pallas_call | solution.py:347
  167.6 2.2 %copy-done = bf16[2048,1024]{1,0:T(8,128)(2,1)S(1)} copy-done((bf16[2048,1024]{1,0:T(8,128)(2,1)S(1)}, bf16[2048,1024]{1,0:T(8,128)(2,1)}, u32[]{:S(2)}) %copy-start) | copy-done | bytes 4194328
  169.8 2.2 %copy-done.1 = bf16[1024,2048]{1,0:T(8,128)(2,1)S(1)} copy-done((bf16[1024,2048]{1,0:T(8,128)(2,1)S(1)}, bf16[1024,2048]{1,0:T(8,128)(2,1)}, u32[]{:S(2)}) %copy-start.1) | copy-done | bytes 4194328
  172.0 3.0 %shard_map.149 = bf16[8,128,384]{2,1,0:T(8,128)(2,1)S(1)} custom-call(bf16[8,128,256]{2,1,0:T(8,128)(2,1)S(1)} %all-to-all-done.4.got, f32[8,1,256]{2,1,0:T(1,128)S(1)} %copy-done.29, bf16[2048,1024]{1,0:T(8,128)(2,1)S(1)} %copy-done, bf16[1024,2048]{1,0:T(8,128)(2,1)S(1)} %copy-done.1, bf16[8,256,128]{2,1,0:T(8,128)(2,1)S(1)} %get-tuple-element.27.wdec, ...), custom_call_target="tpu_custom_call" | custom-call | tf_op jit(solution)/shard_map/pallas_call | solution.py:369
  175.0 27.5 %all_to_all.32.got = bf16[8,128,384]{2,1,0:T(8,128)(2,1)S(1)} all-to-all(bf16[8,128,384]{2,1,0:T(8,128)(2,1)S(1)} %shard_map.149), channel_id=1, replica_groups=mesh['tok'=32,'mlp'=8] {'mlp'}, dimensions={0} | all-to-all | bytes 1572864 | tf_op jit(solution)/shard_map/all_to_all | solution.py:372
  (95 shorter events, 42.0 us)
Async XLA Ops:
  10.6 55.8 %all-to-all-start = ((bf16[32,272,128]{2,1,0:T(8,128)(2,1)}), bf16[32,272,128]{2,1,0:T(8,128)(2,1)S(1)}, u32[]{:S(2)}, u32[]{:S(2)}) async-start(bf16[32,272,128]{2,1,0:T(8,128)(2,1)} %copy-done.2), calls=%async_computation | async-start | bytes 4456448 | tf_op jit(solution)/shard_map/all_to_all | solution.py:302
  18.2 12.9 %collective-permute-start.6 = (bf16[272,256]{1,0:T(8,128)(2,1)S(1)}, bf16[272,256]{1,0:T(8,128)(2,1)S(1)}, u32[]{:S(2)}, u32[]{:S(2)}) collective-permute-start(bf16[272,256]{1,0:T(8,128)(2,1)S(1)} %get-tuple-element.17.refs_0_), channel_id=1, source_target_pairs={{0,7},{1,0},{2,1},{3,2},{4,3},{5,4},{6,5},{7,6},{8,15},{9,8},{10,9... | collective-permute-start | bytes 417800 | tf_op jit(solution)/shard_map/ppermute | solution.py:303
  24.1 11.3 %collective-permute-start.5 = (bf16[272,256]{1,0:T(8,128)(2,1)S(1)}, bf16[272,256]{1,0:T(8,128)(2,1)S(1)}, u32[]{:S(2)}, u32[]{:S(2)}) collective-permute-start(bf16[272,256]{1,0:T(8,128)(2,1)S(1)} %get-tuple-element.17.refs_0_), channel_id=1, source_target_pairs={{0,6},{1,7},{2,0},{3,1},{4,2},{5,3},{6,4},{7,5},{8,14},{9,15},{10,... | collective-permute-start | bytes 417800 | tf_op jit(solution)/shard_map/ppermute | solution.py:303
  25.6 22.7 %collective-permute-start.4 = (bf16[272,256]{1,0:T(8,128)(2,1)S(1)}, bf16[272,256]{1,0:T(8,128)(2,1)S(1)}, u32[]{:S(2)}, u32[]{:S(2)}) collective-permute-start(bf16[272,256]{1,0:T(8,128)(2,1)S(1)} %get-tuple-element.17.refs_0_), channel_id=1, source_target_pairs={{0,5},{1,6},{2,7},{3,0},{4,1},{5,2},{6,3},{7,4},{8,13},{9,14},{10,... | collective-permute-start | bytes 417800 | tf_op jit(solution)/shard_map/ppermute | solution.py:303
  26.0 22.9 %collective-permute-start.3 = (bf16[272,256]{1,0:T(8,128)(2,1)S(1)}, bf16[272,256]{1,0:T(8,128)(2,1)S(1)}, u32[]{:S(2)}, u32[]{:S(2)}) collective-permute-start(bf16[272,256]{1,0:T(8,128)(2,1)S(1)} %get-tuple-element.17.refs_0_), channel_id=1, source_target_pairs={{0,4},{1,5},{2,6},{3,7},{4,0},{5,1},{6,2},{7,3},{8,12},{9,13},{10,... | collective-permute-start | bytes 417800 | tf_op jit(solution)/shard_map/ppermute | solution.py:303
  31.1 19.7 %collective-permute-start.2 = (bf16[272,256]{1,0:T(8,128)(2,1)S(1)}, bf16[272,256]{1,0:T(8,128)(2,1)S(1)}, u32[]{:S(2)}, u32[]{:S(2)}) collective-permute-start(bf16[272,256]{1,0:T(8,128)(2,1)S(1)} %get-tuple-element.17.refs_0_), channel_id=1, source_target_pairs={{0,3},{1,4},{2,5},{3,6},{4,7},{5,0},{6,1},{7,2},{8,11},{9,12},{10,... | collective-permute-start | bytes 417800 | tf_op jit(solution)/shard_map/ppermute | solution.py:303
  31.1 22.5 %collective-permute-start.1 = (bf16[272,256]{1,0:T(8,128)(2,1)S(1)}, bf16[272,256]{1,0:T(8,128)(2,1)S(1)}, u32[]{:S(2)}, u32[]{:S(2)}) collective-permute-start(bf16[272,256]{1,0:T(8,128)(2,1)S(1)} %get-tuple-element.17.refs_0_), channel_id=1, source_target_pairs={{0,2},{1,3},{2,4},{3,5},{4,6},{5,7},{6,0},{7,1},{8,10},{9,11},{10,... | collective-permute-start | bytes 417800 | tf_op jit(solution)/shard_map/ppermute | solution.py:303
  36.1 19.8 %collective-permute-start = (bf16[272,256]{1,0:T(8,128)(2,1)S(1)}, bf16[272,256]{1,0:T(8,128)(2,1)S(1)}, u32[]{:S(2)}, u32[]{:S(2)}) collective-permute-start(bf16[272,256]{1,0:T(8,128)(2,1)S(1)} %get-tuple-element.17.refs_0_), channel_id=1, source_target_pairs={{0,1},{1,2},{2,3},{3,4},{4,5},{5,6},{6,7},{7,0},{8,9},{9,10},{10,1... | collective-permute-start | bytes 417800 | tf_op jit(solution)/shard_map/ppermute | solution.py:303
  63.7 1.9 collective-permute-start.7
  94.2 2.0 collective-permute-start.8
  97.3 34.9 %copy-start.8 = (bf16[8,16,256]{2,1,0:T(8,128)(2,1)S(1)}, bf16[8,16,256]{2,1,0:T(8,128)(2,1)}, u32[]{:S(2)}) copy-start(bf16[8,16,256]{2,1,0:T(8,128)(2,1)} %param.13) | copy-start | bytes 196612
  97.3 34.9 %copy-start.31 = (f32[256]{0:T(256)S(1)}, f32[256]{0:T(256)}, u32[]{:S(2)}) copy-start(f32[256]{0:T(256)} %param.20) | copy-start | bytes 3076
  97.4 34.9 %all-to-all-start.3 = ((bf16[8,128,256]{2,1,0:T(8,128)(2,1)}), bf16[8,128,256]{2,1,0:T(8,128)(2,1)S(1)}, u32[]{:S(2)}, u32[]{:S(2)}) async-start(bf16[8,128,256]{2,1,0:T(8,128)(2,1)} %shard_map.145), calls=%async_computation.3 | async-start | bytes 1048576 | tf_op jit(solution)/shard_map/all_to_all | solution.py:344
  101.0 19.4 %collective-permute-start.11 = (bf16[128,128]{1,0:T(8,128)(2,1)S(1)}, bf16[128,128]{1,0:T(8,128)(2,1)S(1)}, u32[]{:S(2)}, u32[]{:S(2)}) collective-permute-start(bf16[128,128]{1,0:T(8,128)(2,1)S(1)} %get-tuple-element.21.refs_0_), channel_id=1, source_target_pairs={{0,3},{1,4},{2,5},{3,6},{4,7},{5,0},{6,1},{7,2},{8,11},{9,12},{10,... | collective-permute-start | bytes 98312 | tf_op jit(solution)/shard_map/ppermute | solution.py:318
  104.7 16.3 %collective-permute-start.10 = (bf16[128,128]{1,0:T(8,128)(2,1)S(1)}, bf16[128,128]{1,0:T(8,128)(2,1)S(1)}, u32[]{:S(2)}, u32[]{:S(2)}) collective-permute-start(bf16[128,128]{1,0:T(8,128)(2,1)S(1)} %get-tuple-element.21.refs_0_), channel_id=1, source_target_pairs={{0,2},{1,3},{2,4},{3,5},{4,6},{5,7},{6,0},{7,1},{8,10},{9,11},{10,... | collective-permute-start | bytes 98312 | tf_op jit(solution)/shard_map/ppermute | solution.py:318
  107.4 13.6 %collective-permute-start.9 = (bf16[128,128]{1,0:T(8,128)(2,1)S(1)}, bf16[128,128]{1,0:T(8,128)(2,1)S(1)}, u32[]{:S(2)}, u32[]{:S(2)}) collective-permute-start(bf16[128,128]{1,0:T(8,128)(2,1)S(1)} %get-tuple-element.21.refs_0_), channel_id=1, source_target_pairs={{0,1},{1,2},{2,3},{3,4},{4,5},{5,6},{6,7},{7,0},{8,9},{9,10},{10,1... | collective-permute-start | bytes 98312 | tf_op jit(solution)/shard_map/ppermute | solution.py:318
  133.2 34.4 %copy-start.4 = (bf16[256,128]{1,0:T(8,128)(2,1)S(1)}, bf16[256,128]{1,0:T(8,128)(2,1)}, u32[]{:S(2)}) copy-start(bf16[256,128]{1,0:T(8,128)(2,1)} %own_dec.3) | copy-start | bytes 196612
  133.2 34.4 %copy-start.29 = (f32[8,1,256]{2,1,0:T(1,128)S(1)}, f32[8,1,256]{2,1,0:T(1,128)}, u32[]{:S(2)}) copy-start(f32[8,1,256]{2,1,0:T(1,128)} %copy-done.28) | copy-start | bytes 24580
  133.2 34.4 %all-to-all-start.4 = ((bf16[8,128,256]{2,1,0:T(8,128)(2,1)}), bf16[8,128,256]{2,1,0:T(8,128)(2,1)S(1)}, u32[]{:S(2)}, u32[]{:S(2)}) async-start(bf16[8,128,256]{2,1,0:T(8,128)(2,1)} %get-tuple-element.23), calls=%async_computation.4 | async-start | bytes 1048576 | tf_op jit(solution)/shard_map/all_to_all | solution.py:365
  137.3 17.5 %collective-permute-start.15 = (bf16[128,128]{1,0:T(8,128)(2,1)S(1)}, bf16[128,128]{1,0:T(8,128)(2,1)S(1)}, u32[]{:S(2)}, u32[]{:S(2)}) collective-permute-start(bf16[128,128]{1,0:T(8,128)(2,1)S(1)} %get-tuple-element.21.refs_0_), channel_id=1, source_target_pairs={{0,7},{1,0},{2,1},{3,2},{4,3},{5,4},{6,5},{7,6},{8,15},{9,8},{10,9... | collective-permute-start | bytes 98312 | tf_op jit(solution)/shard_map/ppermute | solution.py:318
  140.6 14.3 %collective-permute-start.14 = (bf16[128,128]{1,0:T(8,128)(2,1)S(1)}, bf16[128,128]{1,0:T(8,128)(2,1)S(1)}, u32[]{:S(2)}, u32[]{:S(2)}) collective-permute-start(bf16[128,128]{1,0:T(8,128)(2,1)S(1)} %get-tuple-element.21.refs_0_), channel_id=1, source_target_pairs={{0,6},{1,7},{2,0},{3,1},{4,2},{5,3},{6,4},{7,5},{8,14},{9,15},{10,... | collective-permute-start | bytes 98312 | tf_op jit(solution)/shard_map/ppermute | solution.py:318
  142.9 12.5 %collective-permute-start.13 = (bf16[128,128]{1,0:T(8,128)(2,1)S(1)}, bf16[128,128]{1,0:T(8,128)(2,1)S(1)}, u32[]{:S(2)}, u32[]{:S(2)}) collective-permute-start(bf16[128,128]{1,0:T(8,128)(2,1)S(1)} %get-tuple-element.21.refs_0_), channel_id=1, source_target_pairs={{0,5},{1,6},{2,7},{3,0},{4,1},{5,2},{6,3},{7,4},{8,13},{9,14},{10,... | collective-permute-start | bytes 98312 | tf_op jit(solution)/shard_map/ppermute | solution.py:318
  144.4 12.0 %collective-permute-start.12 = (bf16[128,128]{1,0:T(8,128)(2,1)S(1)}, bf16[128,128]{1,0:T(8,128)(2,1)S(1)}, u32[]{:S(2)}, u32[]{:S(2)}) collective-permute-start(bf16[128,128]{1,0:T(8,128)(2,1)S(1)} %get-tuple-element.21.refs_0_), channel_id=1, source_target_pairs={{0,4},{1,5},{2,6},{3,7},{4,0},{5,1},{6,2},{7,3},{8,12},{9,13},{10,... | collective-permute-start | bytes 98312 | tf_op jit(solution)/shard_map/ppermute | solution.py:318
  167.6 2.2 %copy-start = (bf16[2048,1024]{1,0:T(8,128)(2,1)S(1)}, bf16[2048,1024]{1,0:T(8,128)(2,1)}, u32[]{:S(2)}) copy-start(bf16[2048,1024]{1,0:T(8,128)(2,1)} %up.1) | copy-start | bytes 12582916
  (28 other events, 23.7 us)

commit v3 on v2

v3 whole, which is shorter than its diff:
```python
import functools

import jax
import jax.numpy as jnp
from jax import lax
from jax.experimental import pallas as pl
from jax.experimental.pallas import tpu as pltpu
from jax.sharding import PartitionSpec as P

D = 2048
HD = 64
EPS = 1e-06
BF = jnp.bfloat16
F32 = jnp.float32
NT = (((1,), (1,)), ((), ()))
GELU = 0.7978845608028654
STEPS = (0, 1, 15, 16, 17)


def params(mib):
    return pltpu.CompilerParams(vmem_limit_bytes=mib * 1024 * 1024)


def lanes(shape):
    return lax.broadcasted_iota(jnp.int32, shape, len(shape) - 1)


def half(x):
    return pltpu.roll(x, 64, 1)


def left(shape):
    return lanes(shape) < 64


def fetch(pairs, sem):
    copies = [pltpu.make_async_copy(src, dst, sem.at[i]) for i, (src, dst) in enumerate(pairs)]
    for copy in copies:
        copy.start()
    for copy in copies:
        copy.wait()


def pack_kernel(*refs):
    ins, out, bufs, counts, sem = refs[:7], refs[7], refs[8:16], refs[16], refs[17]
    wqkv, wout_t, patch, base, weight, value, blocks, obs = bufs
    dests = [*bufs[:6], counts]
    loads = [pltpu.make_async_copy(ins[i], dests[i], sem.at[i]) for i in range(7)]
    for load in loads:
        load.start()
    loads[0].wait()
    loads[1].wait()
    for c in range(2):
        for j in range(3):
            blocks[c, 64 * j : 64 * j + 64, :] = wqkv[:, 256 * j + 128 * c : 256 * j + 128 * c + 128]
        blocks[c, 192:256, :] = wout_t[:, 128 * c : 128 * c + 128]
    n = out.shape[0]
    copies = [
        pltpu.make_async_copy(blocks.at[d % 2], out.at[d, pl.ds(0, 256), :], sem.at[7 + d])
        for d in range(n)
    ]
    for copy in copies:
        copy.start()
    for load in loads[2:]:
        load.wait()
    slots = lanes((4, 64))
    zero = jnp.zeros((1, 64), F32)
    rest = jnp.zeros((12, 128), F32)
    for dest in range(n):
        row = slice(dest, dest + 1)
        live = slots < counts[0, dest]
        w = jnp.where(live, weight[0, dest], 0.0)
        v = jnp.where(live[0:1], value[0, row, :], 0.0)
        other = [v, patch[0, row, :].astype(F32), base[0, row, :].astype(F32), zero]
        both = jnp.concatenate([w, jnp.concatenate(other, axis=0)], axis=1)
        obs[dest] = jnp.concatenate([both, rest], axis=0).astype(BF)
    last = pltpu.make_async_copy(obs, out.at[:, pl.ds(256, 16), :], sem.at[7 + n])
    last.start()
    for copy in copies:
        copy.wait()
    last.wait()


def shared_kernel(wdec, gain, out, w_buf, g_buf, buf, sem):
    fetch([(gain, g_buf), (wdec, w_buf)], sem)
    g = g_buf[...]
    high = g.astype(BF).astype(F32)
    mid = (g - high).astype(BF).astype(F32)
    rows = jnp.concatenate([high, mid, g - high - mid, jnp.zeros((13, 256), F32)], axis=0)
    buf[0:128, 0:128] = w_buf[0:128, :]
    buf[0:128, 128:256] = w_buf[128:256, :]
    buf[128:144, :] = rows.astype(BF)
    fetch([(buf, out)], sem)


def groups_of(me, core):
    turn = 1 - 2 * core[0]
    mine = [lax.rem(me[0] - turn * k + 8, 8) for k in (1, 2, 3)]
    theirs = [lax.rem(me[0] + turn * k + 8, 8) for k in (1, 2, 3)]
    return mine, theirs, lax.rem(me[0] + 4, 8)


def norm_kernel(me, core, *refs):
    x, other, far, far_sib, mine, theirs = *refs[:4], refs[4:7], refs[7:10]
    gain, out, buf, sem = refs[10:]
    near, across, opposite = groups_of(me, core)
    low, top = pl.ds(0, 128), pl.ds(128, 128)
    pairs = [
        (x, buf.at[me[0], low, :]),
        (other, buf.at[me[0], top, :]),
        (far, buf.at[opposite, low, :]),
        (far_sib, buf.at[opposite, top, :]),
    ]
    for k in range(3):
        pairs.append((mine[k], buf.at[near[k]]))
        pairs.append((theirs[k].at[top, :], buf.at[across[k], low, :]))
        pairs.append((theirs[k].at[low, :], buf.at[across[k], top, :]))
    fetch(pairs, sem)
    squares = jnp.zeros((256, 1), F32)
    for k in range(8):
        a = buf[k].astype(F32)
        squares += jnp.sum(a * a, axis=1, keepdims=True)
    r = lax.rsqrt(squares / D + EPS)
    for k in range(8):
        out[k] = (buf[k].astype(F32) * r * gain[k]).astype(BF)


def qkv_kernel(normed, w, out, slots):
    acc = jnp.zeros((256, 384), F32)
    for k in range(8):
        cols = [w[4 * k : 4 * k + 4, 64 * j : 64 * j + 64, :].reshape(256, 128) for j in range(3)]
        acc += jnp.dot(normed[k], jnp.concatenate(cols, axis=1), preferred_element_type=F32)
    q, k, v = acc[:, 0:128], acc[:, 128:256], acc[:, 256:384]
    low = left((256, 128))
    pairs = (jnp.where(low, q, half(k)), jnp.where(low, half(q), k))
    own, sib = v[0:128], v[128:256]
    low = left((128, 128))
    values = (jnp.where(low, own, half(sib)), jnp.where(low, half(own), sib))
    for g in range(2):
        qk = pairs[g].astype(BF)
        vv = values[g].astype(BF)
        for s in range(8):
            out[2 * s + g, 0:16, :] = qk[16 * s : 16 * s + 16, :]
            out[2 * s + g, 16:32, :] = qk[128 + 16 * s : 144 + 16 * s, :]
            out[2 * s + g, 32:48, :] = vv[16 * s : 16 * s + 16, :]
    low = left((16, 128))
    tiles = []
    for pair in range(16):
        a = w[2 * pair, 256:272, :].astype(F32)
        b = w[2 * pair + 1, 256:272, :].astype(F32)
        tiles.append(jnp.where(low, a, half(b))[0:4])
        tiles.append(jnp.where(low, half(a), b)[0:4])
    slots[:, 0:128] = jnp.concatenate(tiles[:16], axis=0).astype(BF)
    slots[:, 128:256] = jnp.concatenate(tiles[16:], axis=0).astype(BF)


def attend_kernel(got, out):
    qk_own = got[:, 0:16, :].reshape(256, 128)
    qk_sib = got[:, 16:32, :].reshape(256, 128)
    vv = got[:, 32:48, :].reshape(256, 128)
    low = left((256, 128))

    def mix(qk):
        query = (jnp.where(low, 0.0, half(qk.astype(F32))) * (1.0 / HD**0.5)).astype(BF)
        first = lax.dot_general(query, qk_own, NT, preferred_element_type=F32)
        second = lax.dot_general(query, qk_sib, NT, preferred_element_type=F32)
        top = jnp.maximum(
            jnp.max(first, axis=1, keepdims=True), jnp.max(second, axis=1, keepdims=True)
        )
        first = jnp.exp(first - top)
        second = jnp.exp(second - top)
        total = jnp.sum(first, axis=1, keepdims=True) + jnp.sum(second, axis=1, keepdims=True)
        one = jnp.dot(first.astype(BF), vv, preferred_element_type=F32)
        two = jnp.dot(second.astype(BF), vv, preferred_element_type=F32)
        return (one + half(two)) / total

    mixed = jnp.where(low, mix(qk_own), half(mix(qk_sib)))
    out[...] = mixed.astype(BF).reshape(16, 16, 128)


def heads_of(got, own):
    a = got[:, 0].reshape(128, 128).astype(F32)
    b = got[:, 1].reshape(128, 128).astype(F32)
    low = left((128, 128))
    if own:
        return jnp.where(low, a, half(b)).astype(BF)
    return jnp.where(low, half(a), b).astype(BF)


def give_kernel(got, w, out):
    rows = heads_of(got, False)
    out[...] = lax.dot_general(
        rows, w[...].reshape(D, 128), NT, preferred_element_type=F32
    ).astype(BF)


def keep_kernel(me, got, w, other, slots, *refs):
    outs, buf = refs[:8], refs[8]
    rows = heads_of(got, True)
    total = lax.dot_general(rows, w[...].reshape(D, 128), NT, preferred_element_type=F32)
    total = (total + other[...].astype(F32)).astype(BF)
    for z in range(8):
        buf[z] = total[:, 256 * z : 256 * z + 256]
    for d in range(8):
        outs[d][0:128, :] = buf[lax.rem(me[0] + d, 8)]
        outs[d][128:192, :] = slots[...]


def normal_kernel(slots, out, hot_a, hot_b, terms_a, terms_b):
    cells = lax.broadcasted_iota(jnp.int32, (128, 128), 0).astype(F32).astype(BF)
    zero = jnp.zeros((128, 128), BF)
    one = jnp.ones((128, 128), BF)

    def place(*picks):
        out = zero
        for e, x in picks:
            out = jnp.where(e, jnp.broadcast_to(x.astype(BF), (128, 128)), out)
        return out

    def build(step, hot, terms):
        group, first = lax.div(step, 4), lax.rem(step, 2) * 32
        side = pl.ds(pl.multiple_of(lax.div(lax.rem(step, 4), 2) * 128, 128), 128)
        for c in range(2):
            rows = slots[group, pl.ds(pl.multiple_of(first + 16 * c, 16), 16), side].astype(F32)
            for h in range(2):
                t = rows[8 * h : 8 * h + 8]
                w0, w1, w2, w3, v = (t[j : j + 1] for j in range(5))
                rel = cells - jnp.broadcast_to(t[6:7].astype(BF), (128, 128))
                e0, e1, e2, e3 = rel == 0, rel == 1, rel == 16, rel == 17
                parts = (
                    place((e0, w0 * w0), (e1, w1 * w1), (e2, w2 * w2), (e3, w3 * w3)),
                    place((e0, w0 * w1), (e2, w2 * w3)),
                    place((e1, w1 * w2)),
                    place((e0, w0 * w2), (e1, w1 * w3)),
                    place((e0, w0 * w3)),
                    place((e0, v * w0), (e1, v * w1), (e2, v * w2), (e3, v * w3)),
                )
                at = slice(256 * c + 128 * h, 256 * c + 128 * h + 128)
                patch = jnp.broadcast_to(t[5:6].astype(BF), (128, 128))
                hot[:, at] = jnp.where(cells == patch, one, zero)
                for j, part in enumerate(parts):
                    terms[128 * j : 128 * j + 128, at] = part

    def add(hot, terms):
        out[...] += lax.dot_general(hot[...], terms[...], NT, preferred_element_type=F32)

    out[...] = jnp.zeros(out.shape, F32)
    build(jnp.int32(0), hot_a, terms_a)

    def two(i, _):
        add(hot_a, terms_a)
        build(2 * i + 1, hot_b, terms_b)
        add(hot_b, terms_b)
        build(2 * i + 2, hot_a, terms_a)
        return 0

    lax.fori_loop(0, 15, two, 0)
    add(hot_a, terms_a)
    build(jnp.int32(31), hot_b, terms_b)
    add(hot_b, terms_b)


def resid_kernel(x, gain, *refs):
    got, (resid, scaled, slots) = refs[:8], refs[8:]
    total = x[...].astype(F32)
    for d in range(8):
        total += got[d][0:128, :].astype(F32)
        slots[d] = got[d][128:192, :]
    resid[...] = total
    out = (total * gain[...]).astype(BF)
    for k in range(8):
        scaled[k] = out


def ffn_kernel(me, core, got, *refs):
    own, far, mine, theirs = refs[0], refs[1], refs[2:5], refs[5:8]
    up, down, resid, own_dec, out, shared, sem = refs[8:]
    near, across, opposite = groups_of(me, core)
    pairs = [(own, shared.at[me[0]]), (far, shared.at[opposite])]
    for k in range(3):
        pairs.append((mine[k], shared.at[near[k]]))
        pairs.append((theirs[k], shared.at[across[k]]))
    fetch(pairs, sem)
    squares = jnp.zeros((128, 1), F32)
    for k in range(8):
        g = shared[k, 128:144, :].astype(F32)
        a = got[k].astype(F32) / (g[0:1] + g[1:2] + g[2:3])
        squares += jnp.sum(a * a, axis=1, keepdims=True)
    scale = lax.rsqrt(squares / D + EPS)
    wide = jnp.concatenate([got[k] for k in range(8)], axis=1)
    hidden = []
    for i in range(4):
        pre = jnp.dot(wide, up[:, 256 * i : 256 * i + 256], preferred_element_type=F32) * scale
        act = 0.5 * pre * (1.0 + jnp.tanh(GELU * (pre + 0.044715 * (pre * pre * pre))))
        hidden.append(act.astype(BF))
    hidden = jnp.concatenate(hidden, axis=1)
    decoded = jnp.dot(resid[...].astype(BF), own_dec[...], preferred_element_type=F32)
    for z in range(8):
        at = slice(256 * z, 256 * z + 256)
        part = jnp.dot(hidden, down[:, at], preferred_element_type=F32).astype(BF)
        out[z, :, 0:256] = part
        for i in range(2):
            side = slice(128 * i, 128 * i + 128)
            decoded += jnp.dot(part[:, side], shared[z, 0:128, side], preferred_element_type=F32)
    decoded = decoded.astype(BF)
    for z in range(8):
        out[z, :, 256:384] = decoded


def final_kernel(got, resid, normal, own_dec, state, guidance):
    total = resid[...]
    decoded = jnp.zeros((128, 128), F32)
    for k in range(8):
        total += got[k, :, 0:256].astype(F32)
        decoded += got[k, :, 256:384].astype(F32)
    state[...] = total.astype(BF)
    grad = normal[:, 0:128] * decoded - normal[:, 640:768]
    for i, d in enumerate(STEPS):
        if i:
            a = normal[:, 128 * i : 128 * i + 128]
            grad += a * pltpu.roll(decoded, 128 - d, 1) + pltpu.roll(a * decoded, d, 1)
    guidance[...] = lax.dot_general(
        grad,
        own_dec[...].astype(F32),
        NT,
        precision=lax.Precision.HIGHEST,
        preferred_element_type=F32,
    )


def stay(x):
    return pltpu.with_memory_space_constraint(x, pltpu.HBM)


def sds(shape, dtype=BF):
    return jax.ShapeDtypeStruct(shape, dtype)


def body(
    states,
    w_qkv,
    w_out,
    w_up,
    w_down,
    w_dec,
    gain_attn,
    gain_mlp,
    obs_patch,
    obs_base,
    obs_count,
    obs_weight,
    obs_value,
):
    n_tok, n_mlp = 32, 8
    x = states.reshape(128, 256)
    me = lax.axis_index("mlp").astype(jnp.int32).reshape(1)
    core = lax.rem(lax.axis_index("tok"), 2).astype(jnp.int32).reshape(1)
    pairs = [(i, i ^ 1) for i in range(n_tok)]
    chips = [[2 * i + c for i in range(16)] for c in range(2)]
    order = (1, 7, 2, 6, 3, 5, 4)
    ring = [[(i, (i + d) % n_mlp) for i in range(n_mlp)] for d in range(n_mlp)]
    vmem = pl.BlockSpec(memory_space=pltpu.VMEM)
    hbm = pl.BlockSpec(memory_space=pltpu.HBM)
    smem = pl.BlockSpec(memory_space=pltpu.SMEM)
    whole = lambda *shape: pl.BlockSpec(shape, lambda i: (0,) * len(shape))

    send = pl.pallas_call(
        pack_kernel,
        in_specs=[hbm] * 7,
        out_specs=hbm,
        out_shape=pltpu.HBM((32, 272, 128), BF),
        scratch_shapes=[
            pltpu.VMEM((64, 768), BF),
            pltpu.VMEM((64, 256), BF),
            pltpu.VMEM((1, 32, 64), jnp.int32),
            pltpu.VMEM((1, 32, 64), jnp.int32),
            pltpu.VMEM((1, 32, 4, 64), F32),
            pltpu.VMEM((1, 32, 64), F32),
            pltpu.VMEM((2, 256, 128), BF),
            pltpu.VMEM((32, 16, 128), BF),
            pltpu.SMEM((1, 32), jnp.int32),
            pltpu.SemaphoreType.DMA((40,)),
        ],
        compiler_params=params(8),
    )(*map(stay, (w_qkv, w_out.T, obs_patch, obs_base, obs_weight, obs_value, obs_count)))

    weights_in = lax.all_to_all(send, "tok", 0, 0, tiled=True)

    def shifted(k):
        return [
            (t * n_mlp + z, t * n_mlp + (z + (k if t % 2 == 0 else -k)) % n_mlp)
            for t in range(n_tok)
            for z in range(n_mlp)
        ]

    def gathered(near, far):
        mine = [lax.ppermute(near, ("tok", "mlp"), shifted(k)) for k in (1, 2, 3)]
        far_in = lax.ppermute(far, "mlp", ring[4])
        theirs = [lax.ppermute(r, "tok", pairs) for r in mine]
        return far_in, mine, theirs

    other = lax.ppermute(x, "tok", pairs)
    both, first, _ = lax.optimization_barrier((jnp.concatenate([x, other], axis=0), x, send))
    far_in, mine, theirs = gathered(both, first)
    normed = pl.pallas_call(
        norm_kernel,
        in_specs=[smem] * 2 + [hbm] * 10 + [vmem],
        out_shape=sds((8, 256, 256)),
        scratch_shapes=[pltpu.VMEM((8, 256, 256), BF), pltpu.SemaphoreType.DMA((13,))],
        compiler_params=params(8),
    )(
        me,
        core,
        *map(stay, (x, other, far_in, lax.ppermute(far_in, "tok", pairs), *mine, *theirs)),
        gain_attn.reshape(8, 1, 256),
    )
    shared = pl.pallas_call(
        shared_kernel,
        in_specs=[hbm] * 2,
        out_specs=hbm,
        out_shape=pltpu.HBM((144, 256), BF),
        scratch_shapes=[
            pltpu.VMEM((256, 128), BF),
            pltpu.VMEM((1, 256), F32),
            pltpu.VMEM((144, 256), BF),
            pltpu.SemaphoreType.DMA((2,)),
        ],
        compiler_params=params(4),
    )(stay(w_dec), stay(gain_mlp.reshape(1, 256)))
    shared, _ = lax.optimization_barrier((shared, both))
    far_shared, mine_shared, theirs_shared = gathered(shared, shared)
    weights_in, *others = lax.optimization_barrier(
        (weights_in, far_shared, *mine_shared, *theirs_shared)
    )

    qkv, slots = pl.pallas_call(
        qkv_kernel,
        out_shape=(sds((16, 48, 128)), sds((64, 256))),
        compiler_params=params(8),
    )(normed, weights_in)
    qkv_in = lax.all_to_all(qkv, "tok", 0, 0, tiled=True, axis_index_groups=chips)
    attended = pl.pallas_call(
        attend_kernel, out_shape=sds((16, 16, 128)), compiler_params=params(8)
    )(qkv_in)
    back = lax.all_to_all(attended, "tok", 0, 0, tiled=True, axis_index_groups=chips)
    back = back.reshape(8, 2, 16, 128)

    out_spec = pl.BlockSpec((32, 64, 128), lambda i: (0, 3, 0))
    give = pl.pallas_call(
        give_kernel,
        grid=(1,),
        in_specs=[whole(8, 2, 16, 128), out_spec],
        out_specs=whole(128, D),
        out_shape=sds((128, D)),
        compiler_params=params(8),
    )(back, weights_in)
    taken = lax.ppermute(give, "tok", pairs)
    shares = pl.pallas_call(
        keep_kernel,
        grid=(1,),
        in_specs=[smem, whole(8, 2, 16, 128), out_spec, whole(128, D), whole(64, 256)],
        out_specs=[whole(192, 256)] * 8,
        out_shape=[sds((192, 256))] * 8,
        scratch_shapes=[pltpu.VMEM((8, 128, 256), BF)],
        compiler_params=params(8),
    )(me, back, weights_in, taken, slots)
    shares_in = [shares[0]] + [lax.ppermute(shares[d], "mlp", ring[d]) for d in order]

    resid, scaled, slots_in = pl.pallas_call(
        resid_kernel,
        out_shape=(sds((128, 256), F32), sds((8, 128, 256)), sds((8, 64, 256))),
        compiler_params=params(8),
    )(x, gain_mlp.reshape(1, 256), *shares_in)
    wide = lax.all_to_all(scaled, "mlp", 0, 0, tiled=True)

    down_out = pl.pallas_call(
        ffn_kernel,
        in_specs=[smem] * 2 + [vmem] + [hbm] * 8 + [vmem] * 4,
        out_shape=sds((8, 128, 384)),
        scratch_shapes=[
            pltpu.VMEM((8, 144, 256), BF),
            pltpu.SemaphoreType.DMA((8,)),
        ],
        compiler_params=params(8),
    )(
        me,
        core,
        wide,
        *map(stay, (shared, *others)),
        w_up,
        w_down,
        resid,
        w_dec,
    )
    down_in = lax.all_to_all(down_out, "mlp", 0, 0, tiled=True)

    slots, _ = lax.optimization_barrier((slots_in, down_out))
    normal = pl.pallas_call(
        normal_kernel,
        grid=(1,),
        in_specs=[whole(8, 64, 256)],
        out_specs=whole(128, 768),
        out_shape=sds((128, 768), F32),
        scratch_shapes=[pltpu.VMEM((128, 512), BF)] * 2 + [pltpu.VMEM((768, 512), BF)] * 2,
        compiler_params=params(8),
        cost_estimate=pl.CostEstimate(
            flops=4_000_000_000, bytes_accessed=1_000_000, transcendentals=0
        ),
    )(slots)
    down_in, normal = lax.optimization_barrier((down_in, normal))

    state, guidance = pl.pallas_call(
        final_kernel,
        out_shape=(sds((128, 256)), sds((128, 256), F32)),
        compiler_params=params(8),
    )(down_in, resid, normal, w_dec)
    return state.reshape(8, 16, 256), guidance.reshape(8, 16, 256)


def solution(mesh):
    placed = (
        P(None, "tok", "mlp"),
        P("tok", "mlp"),
        P("mlp", "tok"),
        P(None, "mlp"),
        P("mlp", None),
        P("mlp", None),
        P(),
        P("mlp"),
        P(("tok", "mlp"), None, None),
        P(("tok", "mlp"), None, None),
        P(("tok", "mlp"), None),
        P(("tok", "mlp"), None, None, None),
        P(("tok", "mlp"), None, None),
    )
    return jax.shard_map(
        body,
        mesh=mesh,
        in_specs=placed,
        out_specs=(P(None, "tok", "mlp"), P(None, "tok", "mlp")),
        check_vma=False,
    )
```

time: 205 us -> 155 us (0.76)
  local copies, waits for them, and re-layouts: 25.9 us -> 0.68 us
  waiting for transfers between devices: 43.4 us -> 27.8 us
  Pallas kernels: 31.9 us -> 26.8 us
  blocking collectives: 52.2 us -> 48.9 us
    unnamed x66 -> x34, local copies, waits for them, and re-layouts: 25.8 us -> 0.68 us
    ppermute x15 -> x23, waiting for transfers between devices: 41.5 us -> 17.1 us  [the longest x7 6.1 us: body(): lax.ppermute(shares[d], 'mlp', ring[d])]
    all_to_all x2 -> x1, waiting for transfers between devices: 0.01 us -> 8.78 us  [body(): down_in = lax.all_to_all(down_out, 'mlp', 0, 0, tiled=True)]
    ppermute x15 -> x23, starting transfers between devices: 34 us -> 38.5 us  [the longest x6 15.9 us: gathered(): mine = [lax.ppermute(near, ('tok', 'mlp'), shifted(k)) for k in (1, 2, 3)]]
    pallas_call x7, Pallas kernels: 28.6 us -> 24.3 us  [the longest x1 12.6 us: body(): pl.pallas_call(normal_kernel, grid=(1,), in_specs=[whole(8, 64, 256)], ou...]
    all_to_all x2 -> x1, starting transfers between devices: 7.78 us -> 3.56 us  [body(): down_in = lax.all_to_all(down_out, 'mlp', 0, 0, tiled=True)]
    all_to_all x1, blocking collectives: 27.5 us -> 24 us  [body(): wide = lax.all_to_all(scaled, 'mlp', 0, 0, tiled=True)]
  transfers between devices with their start and end apart: 19 -> 26, of which waited for: 12 -> 9; matrix products, arithmetic and copies ran while one was open for 0% -> 0% of each run, Pallas kernels for 11% -> 10%
where the time goes in v3:
time: 155 us
  starting transfers between devices  49.8 us (32%)
  blocking collectives  48.9 us (32%)
  waiting for transfers between devices  27.8 us (18%)
  Pallas kernels  26.8 us (17%)
    all_to_all x1, blocking collectives, body(): wide = lax.all_to_all(scaled, 'mlp', 0, 0, tiled=True)  24 us
    ppermute x6, starting transfers between devices, gathered(): mine = [lax.ppermute(near, ('tok', 'mlp'), shifted(k)) for k in (1, 2, 3)]  15.9 us
    ppermute x7, starting transfers between devices, body(): lax.ppermute(shares[d], 'mlp', ring[d])  15.7 us
    all_to_all x1, blocking collectives, body(): lax.all_to_all(qkv, 'tok', 0, 0, tiled=True, axis_index_groups=chips)  14.3 us
    pallas_call x1, Pallas kernels, body(): pl.pallas_call(normal_kernel, grid=(1,), in_specs=[whole(8, 64, 256)], ou...  12.6 us
    all_to_all x1, blocking collectives, body(): lax.all_to_all(attended, 'tok', 0, 0, tiled=True, axis_index_groups=chips)  10.7 us
    all_to_all x1, waiting for transfers between devices, body(): down_in = lax.all_to_all(down_out, 'mlp', 0, 0, tiled=True)  8.78 us
    all_to_all x1, starting transfers between devices, body(): weights_in = lax.all_to_all(send, 'tok', 0, 0, tiled=True)  7.63 us
  transfers between devices with their start and end apart: 26, of which 9 were waited for; matrix products, arithmetic and copies ran while one was open for 0% of the time, Pallas kernels for 10%

profile of v3, /device:TPU:2, one launch (start us, length us, event | category | flops | bytes accessed | tf_op | source)
XLA Modules:
  0.0 154.8 jit_solution(17997321609457356664)
XLA Ops:
  0.7 2.7 %shard_map.140 = bf16[32,272,128]{2,1,0:T(8,128)(2,1)} custom-call(bf16[64,768]{1,0:T(8,128)(2,1)} %refs_0_.1, bf16[64,256]{1,0:T(8,128)(2,1)} %bitcast.19, s32[1,32,64]{2,1,0:T(8,128)} %refs_2_.1, s32[1,32,64]{2,1,0:T(8,128)} %refs_3_.1, f32[1,32,4,64]{3,2,1,0:T(4,128)} %refs_4_.1, f32[1,32,64]{2,1,0:T(8,128)} %refs_5_.1, s32[1,32]{1,0:T(1,128)} %refs_6_.1), custom_call_target="tpu_custom_call" | custom-call | tf_op jit(solution)/shard_map/pallas_call | solution.py:367
  3.4 7.6 %all-to-all-start = ((bf16[32,272,128]{2,1,0:T(8,128)(2,1)}), bf16[32,272,128]{2,1,0:T(8,128)(2,1)S(1)}, u32[]{:S(2)}, u32[]{:S(2)}) async-start(bf16[32,272,128]{2,1,0:T(8,128)(2,1)} %shard_map.140), calls=%async_computation | async-start | bytes 4456448 | tf_op jit(solution)/shard_map/all_to_all | solution.py:387
  12.4 4.7 %collective-permute-start.5 = (bf16[256,256]{1,0:T(8,128)(2,1)S(1)}, bf16[256,256]{1,0:T(8,128)(2,1)S(1)}, u32[]{:S(2)}, u32[]{:S(2)}) collective-permute-start(bf16[256,256]{1,0:T(8,128)(2,1)S(1)} %pad_maximum_fusion), channel_id=1, source_target_pairs={{0,3},{1,4},{2,5},{3,6},{4,7},{5,0},{6,1},{7,2},{8,13},{9,14},{10,... | collective-permute-start | bytes 393224 | tf_op jit(solution)/shard_map/ppermute | solution.py:397
  17.1 3.6 %collective-permute-start.4 = (bf16[256,256]{1,0:T(8,128)(2,1)S(1)}, bf16[256,256]{1,0:T(8,128)(2,1)S(1)}, u32[]{:S(2)}, u32[]{:S(2)}) collective-permute-start(bf16[256,256]{1,0:T(8,128)(2,1)S(1)} %pad_maximum_fusion), channel_id=1, source_target_pairs={{0,2},{1,3},{2,4},{3,5},{4,6},{5,7},{6,0},{7,1},{8,14},{9,15},{10,... | collective-permute-start | bytes 393224 | tf_op jit(solution)/shard_map/ppermute | solution.py:397
  23.7 5.0 %collective-permute-start.12 = (bf16[144,256]{1,0:T(8,128)(2,1)}, bf16[144,256]{1,0:T(8,128)(2,1)S(1)}, u32[]{:S(2)}, u32[]{:S(2)}) collective-permute-start(bf16[144,256]{1,0:T(8,128)(2,1)} %shard_map.142.refs_0_), channel_id=1, source_target_pairs={{0,3},{1,4},{2,5},{3,6},{4,7},{5,0},{6,1},{7,2},{8,13},{9,14},{10,... | collective-permute-start | bytes 221192 | tf_op jit(solution)/shard_map/ppermute | solution.py:397
  28.8 3.1 %collective-permute-done.1.refs_2_ = bf16[128,256]{1,0:T(8,128)(2,1)S(1)} collective-permute-done((bf16[128,256]{1,0:T(8,128)(2,1)S(1)}, bf16[128,256]{1,0:T(8,128)(2,1)S(1)}, u32[]{:S(2)}, u32[]{:S(2)}) %collective-permute-start.1) | collective-permute-done | bytes 65568 | tf_op jit(solution)/shard_map/ppermute | solution.py:398
  32.9 1.9 %collective-permute-start.10 = (bf16[144,256]{1,0:T(8,128)(2,1)}, bf16[144,256]{1,0:T(8,128)(2,1)}, u32[]{:S(2)}, u32[]{:S(2)}) collective-permute-start(bf16[144,256]{1,0:T(8,128)(2,1)} %shard_map.142.refs_0_), channel_id=1, source_target_pairs={{0,1},{1,2},{2,3},{3,4},{4,5},{5,6},{6,7},{7,0},{8,15},{9,8},{10,9... | collective-permute-start | bytes 221192 | tf_op jit(solution)/shard_map/ppermute | solution.py:397
  34.8 4.3 %collective-permute-done.11.refs_3_ = bf16[144,256]{1,0:T(8,128)(2,1)} collective-permute-done((bf16[144,256]{1,0:T(8,128)(2,1)}, bf16[144,256]{1,0:T(8,128)(2,1)}, u32[]{:S(2)}, u32[]{:S(2)}) %collective-permute-start.11) | collective-permute-done | bytes 73760 | tf_op jit(solution)/shard_map/ppermute | solution.py:397
  39.7 3.9 %collective-permute-start.9 = (bf16[144,256]{1,0:T(8,128)(2,1)}, bf16[144,256]{1,0:T(8,128)(2,1)}, u32[]{:S(2)}, u32[]{:S(2)}) collective-permute-start(bf16[144,256]{1,0:T(8,128)(2,1)} %shard_map.142.refs_0_), channel_id=1, source_target_pairs={{0,4},{1,5},{2,6},{3,7},{4,0},{5,1},{6,2},{7,3},{8,12},{9,13},{10,... | collective-permute-start | bytes 221192 | tf_op jit(solution)/shard_map/ppermute | solution.py:398
  45.1 1.9 %shard_map.141.normed = bf16[8,256,256]{2,1,0:T(8,128)(2,1)S(1)} custom-call(s32[1]{0:T(128)} %bitcast.me, s32[1]{0:T(128)} %bitcast.1.core, bf16[128,256]{1,0:T(8,128)(2,1)} %bitcast.11, bf16[128,256]{1,0:T(8,128)(2,1)} %copy-done.7, bf16[128,256]{1,0:T(8,128)(2,1)} %copy-done.15, bf16[128,256]{1,0:T(8,128)(2,1)} %copy-done.16, ...), custom_call_target="tpu_custom_call" | custom-call | tf_op jit(solution)/shard_map/pallas_call | solution.py:405
  47.0 2.0 %collective-permute-done.9.refs_1_ = bf16[144,256]{1,0:T(8,128)(2,1)} collective-permute-done((bf16[144,256]{1,0:T(8,128)(2,1)}, bf16[144,256]{1,0:T(8,128)(2,1)}, u32[]{:S(2)}, u32[]{:S(2)}) %collective-permute-start.9) | collective-permute-done | bytes 73760 | tf_op jit(solution)/shard_map/ppermute | solution.py:398
  49.9 14.3 %all_to_all.25.got = bf16[16,48,128]{2,1,0:T(8,128)(2,1)S(1)} all-to-all(bf16[16,48,128]{2,1,0:T(8,128)(2,1)S(1)} %get-tuple-element.35), channel_id=1, replica_groups={{0,16,32,48,64,80,96,112,128,144,160,176,192,208,224,240},{8,24,40,56,7..., dimensions={0} | all-to-all | bytes 393216 | tf_op jit(solution)/shard_map/all_to_all | solution.py:441
  65.1 10.7 %all_to_all.26 = bf16[16,16,128]{2,1,0:T(8,128)(2,1)S(1)} all-to-all(bf16[16,16,128]{2,1,0:T(8,128)(2,1)S(1)} %shard_map.144), channel_id=1, replica_groups={{0,16,32,48,64,80,96,112,128,144,160,176,192,208,224,240},{8,24,40,56,7..., dimensions={0} | all-to-all | bytes 131072 | tf_op jit(solution)/shard_map/all_to_all | solution.py:445
  78.6 3.2 %collective-permute-start.18 = (bf16[192,256]{1,0:T(8,128)(2,1)S(1)}, bf16[192,256]{1,0:T(8,128)(2,1)S(1)}, u32[]{:S(2)}, u32[]{:S(2)}) collective-permute-start(bf16[192,256]{1,0:T(8,128)(2,1)S(1)} %get-tuple-element.39), channel_id=1, source_target_pairs={{0,7},{1,0},{2,1},{3,2},{4,3},{5,4},{6,5},{7,6},{8,15},{9,8},{10,9... | collective-permute-start | bytes 294920 | tf_op jit(solution)/shard_map/ppermute | solution.py:467
  82.2 3.8 %collective-permute-start.20 = (bf16[192,256]{1,0:T(8,128)(2,1)S(1)}, bf16[192,256]{1,0:T(8,128)(2,1)S(1)}, u32[]{:S(2)}, u32[]{:S(2)}) collective-permute-start(bf16[192,256]{1,0:T(8,128)(2,1)S(1)} %get-tuple-element.41), channel_id=1, source_target_pairs={{0,6},{1,7},{2,0},{3,1},{4,2},{5,3},{6,4},{7,5},{8,14},{9,15},{10,... | collective-permute-start | bytes 294920 | tf_op jit(solution)/shard_map/ppermute | solution.py:467
  86.0 5.0 %collective-permute-start.22 = (bf16[192,256]{1,0:T(8,128)(2,1)S(1)}, bf16[192,256]{1,0:T(8,128)(2,1)S(1)}, u32[]{:S(2)}, u32[]{:S(2)}) collective-permute-start(bf16[192,256]{1,0:T(8,128)(2,1)S(1)} %get-tuple-element.43), channel_id=1, source_target_pairs={{0,5},{1,6},{2,7},{3,0},{4,1},{5,2},{6,3},{7,4},{8,13},{9,14},{10,... | collective-permute-start | bytes 294920 | tf_op jit(solution)/shard_map/ppermute | solution.py:467
  91.0 3.2 %collective-permute-start.23 = (bf16[192,256]{1,0:T(8,128)(2,1)S(1)}, bf16[192,256]{1,0:T(8,128)(2,1)S(1)}, u32[]{:S(2)}, u32[]{:S(2)}) collective-permute-start(bf16[192,256]{1,0:T(8,128)(2,1)S(1)} %get-tuple-element.44), channel_id=1, source_target_pairs={{0,4},{1,5},{2,6},{3,7},{4,0},{5,1},{6,2},{7,3},{8,12},{9,13},{10,... | collective-permute-start | bytes 294920 | tf_op jit(solution)/shard_map/ppermute | solution.py:467
  94.2 4.0 %collective-permute-done.21.refs_5_ = bf16[192,256]{1,0:T(8,128)(2,1)S(1)} collective-permute-done((bf16[192,256]{1,0:T(8,128)(2,1)S(1)}, bf16[192,256]{1,0:T(8,128)(2,1)S(1)}, u32[]{:S(2)}, u32[]{:S(2)}) %collective-permute-start.21) | collective-permute-done | bytes 98336 | tf_op jit(solution)/shard_map/ppermute | solution.py:467
  98.2 2.1 %collective-permute-done.22.refs_6_ = bf16[192,256]{1,0:T(8,128)(2,1)S(1)} collective-permute-done((bf16[192,256]{1,0:T(8,128)(2,1)S(1)}, bf16[192,256]{1,0:T(8,128)(2,1)S(1)}, u32[]{:S(2)}, u32[]{:S(2)}) %collective-permute-start.22) | collective-permute-done | bytes 98336 | tf_op jit(solution)/shard_map/ppermute | solution.py:467
  100.4 24.0 %all_to_all.27.got = bf16[8,128,256]{2,1,0:T(8,128)(2,1)S(1)} all-to-all(bf16[8,128,256]{2,1,0:T(8,128)(2,1)S(1)} %get-tuple-element.45), channel_id=1, replica_groups=mesh['tok'=32,'mlp'=8] {'mlp'}, dimensions={0} | all-to-all | bytes 1048576 | tf_op jit(solution)/shard_map/all_to_all | solution.py:474
  124.4 4.4 %shard_map.148 = bf16[8,128,384]{2,1,0:T(8,128)(2,1)} custom-call(s32[1]{0:T(128)} %bitcast.me, s32[1]{0:T(128)} %bitcast.1.core, bf16[8,128,256]{2,1,0:T(8,128)(2,1)S(1)} %all_to_all.27.got, bf16[144,256]{1,0:T(8,128)(2,1)} %shard_map.142.refs_0_, bf16[144,256]{1,0:T(8,128)(2,1)} %collective-permute-done.9.refs_1_, ...), custom_call_target="tpu_custom_call" | custom-call | tf_op jit(solution)/shard_map/pallas_call | solution.py:476
  128.8 3.6 %all-to-all-start.4 = ((bf16[8,128,384]{2,1,0:T(8,128)(2,1)}), bf16[8,128,384]{2,1,0:T(8,128)(2,1)S(1)}, u32[]{:S(2)}, u32[]{:S(2)}) async-start(bf16[8,128,384]{2,1,0:T(8,128)(2,1)} %shard_map.148), calls=%async_computation.4 | async-start | bytes 1572864 | tf_op jit(solution)/shard_map/all_to_all | solution.py:495
  132.4 12.6 %shard_map.149.normal = f32[128,768]{1,0:T(8,128)S(1)} custom-call(bf16[8,64,256]{2,1,0:T(8,128)(2,1)S(1)} %get-tuple-element.55.slots), custom_call_target="tpu_custom_call" | custom-call | flops 4000000000 | bytes 1000000 | tf_op jit(solution)/shard_map/pallas_call | solution.py:498
  145.0 8.8 %all-to-all-done.4.got = bf16[8,128,384]{2,1,0:T(8,128)(2,1)S(1)} async-done(((bf16[8,128,384]{2,1,0:T(8,128)(2,1)}), bf16[8,128,384]{2,1,0:T(8,128)(2,1)S(1)}, u32[]{:S(2)}, u32[]{:S(2)}) %all-to-all-start.4) | async-done | bytes 786464 | tf_op jit(solution)/shard_map/all_to_all | solution.py:495
  (77 shorter events, 13.5 us)
Async XLA Ops:
  3.4 45.7 %all-to-all-start = ((bf16[32,272,128]{2,1,0:T(8,128)(2,1)}), bf16[32,272,128]{2,1,0:T(8,128)(2,1)S(1)}, u32[]{:S(2)}, u32[]{:S(2)}) async-start(bf16[32,272,128]{2,1,0:T(8,128)(2,1)} %shard_map.140), calls=%async_computation | async-start | bytes 4456448 | tf_op jit(solution)/shard_map/all_to_all | solution.py:387
  12.4 19.5 %collective-permute-start.5 = (bf16[256,256]{1,0:T(8,128)(2,1)S(1)}, bf16[256,256]{1,0:T(8,128)(2,1)S(1)}, u32[]{:S(2)}, u32[]{:S(2)}) collective-permute-start(bf16[256,256]{1,0:T(8,128)(2,1)S(1)} %pad_maximum_fusion), channel_id=1, source_target_pairs={{0,3},{1,4},{2,5},{3,6},{4,7},{5,0},{6,1},{7,2},{8,13},{9,14},{10,... | collective-permute-start | bytes 393224 | tf_op jit(solution)/shard_map/ppermute | solution.py:397
  17.1 14.9 %collective-permute-start.4 = (bf16[256,256]{1,0:T(8,128)(2,1)S(1)}, bf16[256,256]{1,0:T(8,128)(2,1)S(1)}, u32[]{:S(2)}, u32[]{:S(2)}) collective-permute-start(bf16[256,256]{1,0:T(8,128)(2,1)S(1)} %pad_maximum_fusion), channel_id=1, source_target_pairs={{0,2},{1,3},{2,4},{3,5},{4,6},{5,7},{6,0},{7,1},{8,14},{9,15},{10,... | collective-permute-start | bytes 393224 | tf_op jit(solution)/shard_map/ppermute | solution.py:397
  20.7 11.2 %collective-permute-start.1 = (bf16[128,256]{1,0:T(8,128)(2,1)S(1)}, bf16[128,256]{1,0:T(8,128)(2,1)S(1)}, u32[]{:S(2)}, u32[]{:S(2)}) collective-permute-start(bf16[128,256]{1,0:T(8,128)(2,1)S(1)} %bitcast.14), channel_id=1, source_target_pairs={{0,4},{1,5},{2,6},{3,7},{4,0},{5,1},{6,2},{7,3},{8,12},{9,13},{10,... | collective-permute-start | bytes 196616 | tf_op jit(solution)/shard_map/ppermute | solution.py:398
  21.6 17.6 %collective-permute-start.3 = (bf16[256,256]{1,0:T(8,128)(2,1)S(1)}, bf16[256,256]{1,0:T(8,128)(2,1)S(1)}, u32[]{:S(2)}, u32[]{:S(2)}) collective-permute-start(bf16[256,256]{1,0:T(8,128)(2,1)S(1)} %pad_maximum_fusion), channel_id=1, source_target_pairs={{0,1},{1,2},{2,3},{3,4},{4,5},{5,6},{6,7},{7,0},{8,15},{9,8},{10,9... | collective-permute-start | bytes 393224 | tf_op jit(solution)/shard_map/ppermute | solution.py:397
  23.7 9.1 %collective-permute-start.12 = (bf16[144,256]{1,0:T(8,128)(2,1)}, bf16[144,256]{1,0:T(8,128)(2,1)S(1)}, u32[]{:S(2)}, u32[]{:S(2)}) collective-permute-start(bf16[144,256]{1,0:T(8,128)(2,1)} %shard_map.142.refs_0_), channel_id=1, source_target_pairs={{0,3},{1,4},{2,5},{3,6},{4,7},{5,0},{6,1},{7,2},{8,13},{9,14},{10,... | collective-permute-start | bytes 221192 | tf_op jit(solution)/shard_map/ppermute | solution.py:397
  31.9 7.3 %collective-permute-start.11 = (bf16[144,256]{1,0:T(8,128)(2,1)}, bf16[144,256]{1,0:T(8,128)(2,1)}, u32[]{:S(2)}, u32[]{:S(2)}) collective-permute-start(bf16[144,256]{1,0:T(8,128)(2,1)} %shard_map.142.refs_0_), channel_id=1, source_target_pairs={{0,2},{1,3},{2,4},{3,5},{4,6},{5,7},{6,0},{7,1},{8,14},{9,15},{10,... | collective-permute-start | bytes 221192 | tf_op jit(solution)/shard_map/ppermute | solution.py:397
  31.9 11.7 %collective-permute-start.8 = (bf16[256,256]{1,0:T(8,128)(2,1)S(1)}, bf16[256,256]{1,0:T(8,128)(2,1)S(1)}, u32[]{:S(2)}, u32[]{:S(2)}) collective-permute-start(bf16[256,256]{1,0:T(8,128)(2,1)S(1)} %collective-permute-done.5.refs_6_), channel_id=1, source_target_pairs={{0,8},{8,0},{16,24},{24,16},{32,40},{40,32},{48,56},{56,48},{64,72... | collective-permute-start | bytes 393224 | tf_op jit(solution)/shard_map/ppermute | solution.py:399
  32.0 12.1 %collective-permute-start.7 = (bf16[256,256]{1,0:T(8,128)(2,1)S(1)}, bf16[256,256]{1,0:T(8,128)(2,1)S(1)}, u32[]{:S(2)}, u32[]{:S(2)}) collective-permute-start(bf16[256,256]{1,0:T(8,128)(2,1)S(1)} %collective-permute-done.4.refs_5_), channel_id=1, source_target_pairs={{0,8},{8,0},{16,24},{24,16},{32,40},{40,32},{48,56},{56,48},{64,72... | collective-permute-start | bytes 393224 | tf_op jit(solution)/shard_map/ppermute | solution.py:399
  32.9 6.8 %collective-permute-start.10 = (bf16[144,256]{1,0:T(8,128)(2,1)}, bf16[144,256]{1,0:T(8,128)(2,1)}, u32[]{:S(2)}, u32[]{:S(2)}) collective-permute-start(bf16[144,256]{1,0:T(8,128)(2,1)} %shard_map.142.refs_0_), channel_id=1, source_target_pairs={{0,1},{1,2},{2,3},{3,4},{4,5},{5,6},{6,7},{7,0},{8,15},{9,8},{10,9... | collective-permute-start | bytes 221192 | tf_op jit(solution)/shard_map/ppermute | solution.py:397
  39.2 4.4 %collective-permute-start.2 = (bf16[128,256]{1,0:T(8,128)(2,1)S(1)}, bf16[128,256]{1,0:T(8,128)(2,1)S(1)}, u32[]{:S(2)}, u32[]{:S(2)}) collective-permute-start(bf16[128,256]{1,0:T(8,128)(2,1)S(1)} %collective-permute-done.1.refs_2_), channel_id=1, source_target_pairs={{0,8},{8,0},{16,24},{24,16},{32,40},{40,32},{48,56},{56,48},{64,72... | collective-permute-start | bytes 196616 | tf_op jit(solution)/shard_map/ppermute | solution.py:414
  39.2 5.2 %collective-permute-start.6 = (bf16[256,256]{1,0:T(8,128)(2,1)S(1)}, bf16[256,256]{1,0:T(8,128)(2,1)S(1)}, u32[]{:S(2)}, u32[]{:S(2)}) collective-permute-start(bf16[256,256]{1,0:T(8,128)(2,1)S(1)} %collective-permute-done.3.refs_4_), channel_id=1, source_target_pairs={{0,8},{8,0},{16,24},{24,16},{32,40},{40,32},{48,56},{56,48},{64,72... | collective-permute-start | bytes 393224 | tf_op jit(solution)/shard_map/ppermute | solution.py:399
  39.7 9.4 %collective-permute-start.9 = (bf16[144,256]{1,0:T(8,128)(2,1)}, bf16[144,256]{1,0:T(8,128)(2,1)}, u32[]{:S(2)}, u32[]{:S(2)}) collective-permute-start(bf16[144,256]{1,0:T(8,128)(2,1)} %shard_map.142.refs_0_), channel_id=1, source_target_pairs={{0,4},{1,5},{2,6},{3,7},{4,0},{5,1},{6,2},{7,3},{8,12},{9,13},{10,... | collective-permute-start | bytes 221192 | tf_op jit(solution)/shard_map/ppermute | solution.py:398
  43.6 5.5 %collective-permute-start.15 = (bf16[144,256]{1,0:T(8,128)(2,1)S(1)}, bf16[144,256]{1,0:T(8,128)(2,1)}, u32[]{:S(2)}, u32[]{:S(2)}) collective-permute-start(bf16[144,256]{1,0:T(8,128)(2,1)S(1)} %collective-permute-done.12.refs_4_), channel_id=1, source_target_pairs={{0,8},{8,0},{16,24},{24,16},{32,40},{40,32},{48,56},{56,48},{64,72... | collective-permute-start | bytes 221192 | tf_op jit(solution)/shard_map/ppermute | solution.py:399
  43.6 5.4 %collective-permute-start.14 = (bf16[144,256]{1,0:T(8,128)(2,1)}, bf16[144,256]{1,0:T(8,128)(2,1)}, u32[]{:S(2)}, u32[]{:S(2)}) collective-permute-start(bf16[144,256]{1,0:T(8,128)(2,1)} %collective-permute-done.11.refs_3_), channel_id=1, source_target_pairs={{0,8},{8,0},{16,24},{24,16},{32,40},{40,32},{48,56},{56,48},{64,72... | collective-permute-start | bytes 221192 | tf_op jit(solution)/shard_map/ppermute | solution.py:399
  44.1 4.9 %collective-permute-start.13 = (bf16[144,256]{1,0:T(8,128)(2,1)}, bf16[144,256]{1,0:T(8,128)(2,1)}, u32[]{:S(2)}, u32[]{:S(2)}) collective-permute-start(bf16[144,256]{1,0:T(8,128)(2,1)} %collective-permute-done.10.refs_2_), channel_id=1, source_target_pairs={{0,8},{8,0},{16,24},{24,16},{32,40},{40,32},{48,56},{56,48},{64,72... | collective-permute-start | bytes 221192 | tf_op jit(solution)/shard_map/ppermute | solution.py:399
  78.5 7.5 %collective-permute-start.17 = (bf16[192,256]{1,0:T(8,128)(2,1)S(1)}, bf16[192,256]{1,0:T(8,128)(2,1)S(1)}, u32[]{:S(2)}, u32[]{:S(2)}) collective-permute-start(bf16[192,256]{1,0:T(8,128)(2,1)S(1)} %get-tuple-element.38), channel_id=1, source_target_pairs={{0,1},{1,2},{2,3},{3,4},{4,5},{5,6},{6,7},{7,0},{8,9},{9,10},{10,1... | collective-permute-start | bytes 294920 | tf_op jit(solution)/shard_map/ppermute | solution.py:467
  78.6 12.4 %collective-permute-start.18 = (bf16[192,256]{1,0:T(8,128)(2,1)S(1)}, bf16[192,256]{1,0:T(8,128)(2,1)S(1)}, u32[]{:S(2)}, u32[]{:S(2)}) collective-permute-start(bf16[192,256]{1,0:T(8,128)(2,1)S(1)} %get-tuple-element.39), channel_id=1, source_target_pairs={{0,7},{1,0},{2,1},{3,2},{4,3},{5,4},{6,5},{7,6},{8,15},{9,8},{10,9... | collective-permute-start | bytes 294920 | tf_op jit(solution)/shard_map/ppermute | solution.py:467
  81.8 12.4 %collective-permute-start.19 = (bf16[192,256]{1,0:T(8,128)(2,1)S(1)}, bf16[192,256]{1,0:T(8,128)(2,1)S(1)}, u32[]{:S(2)}, u32[]{:S(2)}) collective-permute-start(bf16[192,256]{1,0:T(8,128)(2,1)S(1)} %get-tuple-element.40), channel_id=1, source_target_pairs={{0,2},{1,3},{2,4},{3,5},{4,6},{5,7},{6,0},{7,1},{8,10},{9,11},{10,... | collective-permute-start | bytes 294920 | tf_op jit(solution)/shard_map/ppermute | solution.py:467
  82.2 12.0 %collective-permute-start.20 = (bf16[192,256]{1,0:T(8,128)(2,1)S(1)}, bf16[192,256]{1,0:T(8,128)(2,1)S(1)}, u32[]{:S(2)}, u32[]{:S(2)}) collective-permute-start(bf16[192,256]{1,0:T(8,128)(2,1)S(1)} %get-tuple-element.41), channel_id=1, source_target_pairs={{0,6},{1,7},{2,0},{3,1},{4,2},{5,3},{6,4},{7,5},{8,14},{9,15},{10,... | collective-permute-start | bytes 294920 | tf_op jit(solution)/shard_map/ppermute | solution.py:467
  86.0 12.3 %collective-permute-start.21 = (bf16[192,256]{1,0:T(8,128)(2,1)S(1)}, bf16[192,256]{1,0:T(8,128)(2,1)S(1)}, u32[]{:S(2)}, u32[]{:S(2)}) collective-permute-start(bf16[192,256]{1,0:T(8,128)(2,1)S(1)} %get-tuple-element.42), channel_id=1, source_target_pairs={{0,3},{1,4},{2,5},{3,6},{4,7},{5,0},{6,1},{7,2},{8,11},{9,12},{10,... | collective-permute-start | bytes 294920 | tf_op jit(solution)/shard_map/ppermute | solution.py:467
  86.0 14.3 %collective-permute-start.22 = (bf16[192,256]{1,0:T(8,128)(2,1)S(1)}, bf16[192,256]{1,0:T(8,128)(2,1)S(1)}, u32[]{:S(2)}, u32[]{:S(2)}) collective-permute-start(bf16[192,256]{1,0:T(8,128)(2,1)S(1)} %get-tuple-element.43), channel_id=1, source_target_pairs={{0,5},{1,6},{2,7},{3,0},{4,1},{5,2},{6,3},{7,4},{8,13},{9,14},{10,... | collective-permute-start | bytes 294920 | tf_op jit(solution)/shard_map/ppermute | solution.py:467
  91.0 9.3 %collective-permute-start.23 = (bf16[192,256]{1,0:T(8,128)(2,1)S(1)}, bf16[192,256]{1,0:T(8,128)(2,1)S(1)}, u32[]{:S(2)}, u32[]{:S(2)}) collective-permute-start(bf16[192,256]{1,0:T(8,128)(2,1)S(1)} %get-tuple-element.44), channel_id=1, source_target_pairs={{0,4},{1,5},{2,6},{3,7},{4,0},{5,1},{6,2},{7,3},{8,12},{9,13},{10,... | collective-permute-start | bytes 294920 | tf_op jit(solution)/shard_map/ppermute | solution.py:467
  128.8 25.0 %all-to-all-start.4 = ((bf16[8,128,384]{2,1,0:T(8,128)(2,1)}), bf16[8,128,384]{2,1,0:T(8,128)(2,1)S(1)}, u32[]{:S(2)}, u32[]{:S(2)}) async-start(bf16[8,128,384]{2,1,0:T(8,128)(2,1)} %shard_map.148), calls=%async_computation.4 | async-start | bytes 1572864 | tf_op jit(solution)/shard_map/all_to_all | solution.py:495
  (19 other events, 559.1 us)

commit v4 on v3

--- a/solution.py
+++ b/solution.py
@@ -154,7 +154,7 @@
     slots[:, 128:256] = jnp.concatenate(tiles[16:], axis=0).astype(BF)
 
 
-def attend_kernel(got, out):
+def attend_kernel(core, got, out):
     qk_own = got[:, 0:16, :].reshape(256, 128)
     qk_sib = got[:, 16:32, :].reshape(256, 128)
     vv = got[:, 32:48, :].reshape(256, 128)
@@ -174,33 +174,26 @@
         two = jnp.dot(second.astype(BF), vv, preferred_element_type=F32)
         return (one + half(two)) / total
 
-    mixed = jnp.where(low, mix(qk_own), half(mix(qk_sib)))
-    out[...] = mixed.astype(BF).reshape(16, 16, 128)
-
-
-def heads_of(got, own):
-    a = got[:, 0].reshape(128, 128).astype(F32)
-    b = got[:, 1].reshape(128, 128).astype(F32)
+    c = core[0]
+    out[:, c] = mix(qk_own).astype(BF).reshape(16, 16, 128)
+    out[:, 1 - c] = mix(qk_sib).astype(BF).reshape(16, 16, 128)
+
+
+def share_kernel(me, core, got, w, w_sib, slots, *refs):
+    outs, buf = refs[:8], refs[8]
     low = left((128, 128))
-    if own:
+
+    def heads_of(c):
+        a = got[:, 0, c].reshape(128, 128).astype(F32)
+        b = got[:, 1, c].reshape(128, 128).astype(F32)
         return jnp.where(low, a, half(b)).astype(BF)
-    return jnp.where(low, half(a), b).astype(BF)
-
-
-def give_kernel(got, w, out):
-    rows = heads_of(got, False)
-    out[...] = lax.dot_general(
-        rows, w[...].reshape(D, 128), NT, preferred_element_type=F32
-    ).astype(BF)
-
-
-def keep_kernel(me, got, w, other, slots, *refs):
-    outs, buf = refs[:8], refs[8]
-    rows = heads_of(got, True)
-    total = lax.dot_general(rows, w[...].reshape(D, 128), NT, preferred_element_type=F32)
-    total = (total + other[...].astype(F32)).astype(BF)
+
+    own, other = heads_of(core[0]), heads_of(1 - core[0])
     for z in range(8):
-        buf[z] = total[:, 256 * z : 256 * z + 256]
+        at = slice(4 * z, 4 * z + 4)
+        part = lax.dot_general(own, w[at].reshape(256, 128), NT, preferred_element_type=F32)
+        part += lax.dot_general(other, w_sib[at].reshape(256, 128), NT, preferred_element_type=F32)
+        buf[z] = part.astype(BF)
     for d in range(8):
         outs[d][0:128, :] = buf[lax.rem(me[0] + d, 8)]
         outs[d][128:192, :] = slots[...]
@@ -439,31 +432,34 @@
         compiler_params=params(8),
     )(normed, weights_in)
     qkv_in = lax.all_to_all(qkv, "tok", 0, 0, tiled=True, axis_index_groups=chips)
+    half_out, _ = lax.optimization_barrier((weights_in, qkv))
+    half_out = lax.ppermute(half_out[:, 192:256, :], "tok", pairs)
+
     attended = pl.pallas_call(
-        attend_kernel, out_shape=sds((16, 16, 128)), compiler_params=params(8)
-    )(qkv_in)
-    back = lax.all_to_all(attended, "tok", 0, 0, tiled=True, axis_index_groups=chips)
-    back = back.reshape(8, 2, 16, 128)
-
-    out_spec = pl.BlockSpec((32, 64, 128), lambda i: (0, 3, 0))
-    give = pl.pallas_call(
-        give_kernel,
+        attend_kernel,
+        in_specs=[smem, vmem],
+        out_shape=sds((16, 2, 16, 128)),
+        compiler_params=params(8),
+    )(core, qkv_in)
+    back = lax.all_to_all(attended.reshape(32, 16, 128), "tok", 0, 0, tiled=True)
+    back, half_out = lax.optimization_barrier((back, half_out))
+
+    shares = pl.pallas_call(
+        share_kernel,
         grid=(1,),
-        in_specs=[whole(8, 2, 16, 128), out_spec],
-        out_specs=whole(128, D),
-        out_shape=sds((128, D)),
-        compiler_params=params(8),
-    )(back, weights_in)
-    taken = lax.ppermute(give, "tok", pairs)
-    shares = pl.pallas_call(
-        keep_kernel,
-        grid=(1,),
-        in_specs=[smem, whole(8, 2, 16, 128), out_spec, whole(128, D), whole(64, 256)],
+        in_specs=[
+            smem,
+            smem,
+            whole(8, 2, 2, 16, 128),
+            pl.BlockSpec((32, 64, 128), lambda i: (0, 3, 0)),
+            whole(32, 64, 128),
+            whole(64, 256),
+        ],
         out_specs=[whole(192, 256)] * 8,
         out_shape=[sds((192, 256))] * 8,
         scratch_shapes=[pltpu.VMEM((8, 128, 256), BF)],
         compiler_params=params(8),
-    )(me, back, weights_in, taken, slots)
+    )(me, core, back.reshape(8, 2, 2, 16, 128), weights_in, half_out, slots)
     shares_in = [shares[0]] + [lax.ppermute(shares[d], "mlp", ring[d]) for d in order]
 
     resid, scaled, slots_in = pl.pallas_call(

time: 155 us -> 154 us (level)
  waiting for transfers between devices: 27.8 us -> 25.9 us
    ppermute x1, waiting for transfers between devices: 1.9 us -> 0.01 us  [body(): half_out = lax.ppermute(half_out[:, 192:256, :], 'tok', pairs)]
  transfers between devices with their start and end apart: 26 -> 26, of which waited for: 9 -> 8; matrix products, arithmetic and copies ran while one was open for 0% -> 0% of each run, Pallas kernels for 10% -> 11%
where the time goes in v4:
time: 154 us; the launch traced here: 153 us
  starting transfers between devices  49.8 us (32%)
  blocking collectives  49.3 us (32%)
  Pallas kernels  26.6 us (17%)
  waiting for transfers between devices  25.9 us (17%)
    all_to_all x1, blocking collectives, body(): wide = lax.all_to_all(scaled, 'mlp', 0, 0, tiled=True)  23.9 us
    ppermute x6, starting transfers between devices, gathered(): mine = [lax.ppermute(near, ('tok', 'mlp'), shifted(k)) for k in (1, 2, 3)]  15.9 us
    ppermute x7, starting transfers between devices, body(): lax.ppermute(shares[d], 'mlp', ring[d])  15.7 us
    all_to_all x1, blocking collectives, body(): lax.all_to_all(qkv, 'tok', 0, 0, tiled=True, axis_index_groups=chips)  14.3 us
    pallas_call x1, Pallas kernels, body(): pl.pallas_call(normal_kernel, grid=(1,), in_specs=[whole(8, 64, 256)], ou...  12.6 us
    all_to_all x1, blocking collectives, body(): lax.all_to_all(attended.reshape(32, 16, 128), 'tok', 0, 0, tiled=True)  11.1 us
    all_to_all x1, waiting for transfers between devices, body(): down_in = lax.all_to_all(down_out, 'mlp', 0, 0, tiled=True)  8.71 us
    all_to_all x1, starting transfers between devices, body(): weights_in = lax.all_to_all(send, 'tok', 0, 0, tiled=True)  7.63 us
  transfers between devices with their start and end apart: 26, of which 8 were waited for; matrix products, arithmetic and copies ran while one was open for 0% of the time, Pallas kernels for 11%

profile of v4, /device:TPU:2, one launch (start us, length us, event | category | flops | bytes accessed | tf_op | source)
XLA Modules:
  0.0 153.2 jit_solution(13783783401582033201)
XLA Ops:
  0.7 2.7 %shard_map.140 = bf16[32,272,128]{2,1,0:T(8,128)(2,1)} custom-call(bf16[64,768]{1,0:T(8,128)(2,1)} %refs_0_.1, bf16[64,256]{1,0:T(8,128)(2,1)} %bitcast.20, s32[1,32,64]{2,1,0:T(8,128)} %refs_2_.1, s32[1,32,64]{2,1,0:T(8,128)} %refs_3_.1, f32[1,32,4,64]{3,2,1,0:T(4,128)} %refs_4_.1, f32[1,32,64]{2,1,0:T(8,128)} %refs_5_.1, s32[1,32]{1,0:T(1,128)} %refs_6_.1), custom_call_target="tpu_custom_call" | custom-call | tf_op jit(solution)/shard_map/pallas_call | solution.py:360
  3.4 7.6 %all-to-all-start = ((bf16[32,272,128]{2,1,0:T(8,128)(2,1)}), bf16[32,272,128]{2,1,0:T(8,128)(2,1)S(1)}, u32[]{:S(2)}, u32[]{:S(2)}) async-start(bf16[32,272,128]{2,1,0:T(8,128)(2,1)} %shard_map.140), calls=%async_computation | async-start | bytes 4456448 | tf_op jit(solution)/shard_map/all_to_all | solution.py:380
  12.4 4.7 %collective-permute-start.5 = (bf16[256,256]{1,0:T(8,128)(2,1)S(1)}, bf16[256,256]{1,0:T(8,128)(2,1)S(1)}, u32[]{:S(2)}, u32[]{:S(2)}) collective-permute-start(bf16[256,256]{1,0:T(8,128)(2,1)S(1)} %pad_maximum_fusion), channel_id=1, source_target_pairs={{0,3},{1,4},{2,5},{3,6},{4,7},{5,0},{6,1},{7,2},{8,13},{9,14},{10,... | collective-permute-start | bytes 393224 | tf_op jit(solution)/shard_map/ppermute | solution.py:390
  17.1 3.6 %collective-permute-start.4 = (bf16[256,256]{1,0:T(8,128)(2,1)S(1)}, bf16[256,256]{1,0:T(8,128)(2,1)S(1)}, u32[]{:S(2)}, u32[]{:S(2)}) collective-permute-start(bf16[256,256]{1,0:T(8,128)(2,1)S(1)} %pad_maximum_fusion), channel_id=1, source_target_pairs={{0,2},{1,3},{2,4},{3,5},{4,6},{5,7},{6,0},{7,1},{8,14},{9,15},{10,... | collective-permute-start | bytes 393224 | tf_op jit(solution)/shard_map/ppermute | solution.py:390
  23.7 5.0 %collective-permute-start.12 = (bf16[144,256]{1,0:T(8,128)(2,1)}, bf16[144,256]{1,0:T(8,128)(2,1)S(1)}, u32[]{:S(2)}, u32[]{:S(2)}) collective-permute-start(bf16[144,256]{1,0:T(8,128)(2,1)} %shard_map.142.refs_0_), channel_id=1, source_target_pairs={{0,3},{1,4},{2,5},{3,6},{4,7},{5,0},{6,1},{7,2},{8,13},{9,14},{10,... | collective-permute-start | bytes 221192 | tf_op jit(solution)/shard_map/ppermute | solution.py:390
  28.8 3.1 %collective-permute-done.1.refs_2_ = bf16[128,256]{1,0:T(8,128)(2,1)S(1)} collective-permute-done((bf16[128,256]{1,0:T(8,128)(2,1)S(1)}, bf16[128,256]{1,0:T(8,128)(2,1)S(1)}, u32[]{:S(2)}, u32[]{:S(2)}) %collective-permute-start.1) | collective-permute-done | bytes 65568 | tf_op jit(solution)/shard_map/ppermute | solution.py:391
  32.9 1.9 %collective-permute-start.10 = (bf16[144,256]{1,0:T(8,128)(2,1)}, bf16[144,256]{1,0:T(8,128)(2,1)}, u32[]{:S(2)}, u32[]{:S(2)}) collective-permute-start(bf16[144,256]{1,0:T(8,128)(2,1)} %shard_map.142.refs_0_), channel_id=1, source_target_pairs={{0,1},{1,2},{2,3},{3,4},{4,5},{5,6},{6,7},{7,0},{8,15},{9,8},{10,9... | collective-permute-start | bytes 221192 | tf_op jit(solution)/shard_map/ppermute | solution.py:390
  34.8 4.3 %collective-permute-done.11.refs_3_ = bf16[144,256]{1,0:T(8,128)(2,1)} collective-permute-done((bf16[144,256]{1,0:T(8,128)(2,1)}, bf16[144,256]{1,0:T(8,128)(2,1)}, u32[]{:S(2)}, u32[]{:S(2)}) %collective-permute-start.11) | collective-permute-done | bytes 73760 | tf_op jit(solution)/shard_map/ppermute | solution.py:390
  39.7 3.9 %collective-permute-start.9 = (bf16[144,256]{1,0:T(8,128)(2,1)}, bf16[144,256]{1,0:T(8,128)(2,1)}, u32[]{:S(2)}, u32[]{:S(2)}) collective-permute-start(bf16[144,256]{1,0:T(8,128)(2,1)} %shard_map.142.refs_0_), channel_id=1, source_target_pairs={{0,4},{1,5},{2,6},{3,7},{4,0},{5,1},{6,2},{7,3},{8,12},{9,13},{10,... | collective-permute-start | bytes 221192 | tf_op jit(solution)/shard_map/ppermute | solution.py:391
  45.1 1.9 %shard_map.141.normed = bf16[8,256,256]{2,1,0:T(8,128)(2,1)S(1)} custom-call(s32[1]{0:T(128)} %bitcast.me, s32[1]{0:T(128)} %bitcast.1.core, bf16[128,256]{1,0:T(8,128)(2,1)} %bitcast.10, bf16[128,256]{1,0:T(8,128)(2,1)} %copy-done.7, bf16[128,256]{1,0:T(8,128)(2,1)} %copy-done.15, bf16[128,256]{1,0:T(8,128)(2,1)} %copy-done.16, ...), custom_call_target="tpu_custom_call" | custom-call | tf_op jit(solution)/shard_map/pallas_call | solution.py:398
  47.0 2.0 %collective-permute-done.9.refs_1_ = bf16[144,256]{1,0:T(8,128)(2,1)} collective-permute-done((bf16[144,256]{1,0:T(8,128)(2,1)}, bf16[144,256]{1,0:T(8,128)(2,1)}, u32[]{:S(2)}, u32[]{:S(2)}) %collective-permute-start.9) | collective-permute-done | bytes 73760 | tf_op jit(solution)/shard_map/ppermute | solution.py:391
  50.1 14.3 %all_to_all.25.got = bf16[16,48,128]{2,1,0:T(8,128)(2,1)S(1)} all-to-all(bf16[16,48,128]{2,1,0:T(8,128)(2,1)S(1)} %get-tuple-element.38), channel_id=1, replica_groups={{0,16,32,48,64,80,96,112,128,144,160,176,192,208,224,240},{8,24,40,56,7..., dimensions={0} | all-to-all | bytes 393216 | tf_op jit(solution)/shard_map/all_to_all | solution.py:434
  65.3 11.1 %all_to_all.26 = bf16[32,16,128]{2,1,0:T(8,128)(2,1)S(1)} all-to-all(bf16[32,16,128]{2,1,0:T(8,128)(2,1)S(1)} %bitcast.15), channel_id=1, replica_groups=mesh['tok'=32,'mlp'=8] {'tok'}, dimensions={0} | all-to-all | bytes 262144 | tf_op jit(solution)/shard_map/all_to_all | solution.py:444
  77.0 3.2 %collective-permute-start.18 = (bf16[192,256]{1,0:T(8,128)(2,1)S(1)}, bf16[192,256]{1,0:T(8,128)(2,1)S(1)}, u32[]{:S(2)}, u32[]{:S(2)}) collective-permute-start(bf16[192,256]{1,0:T(8,128)(2,1)S(1)} %get-tuple-element.45), channel_id=1, source_target_pairs={{0,7},{1,0},{2,1},{3,2},{4,3},{5,4},{6,5},{7,6},{8,15},{9,8},{10,9... | collective-permute-start | bytes 294920 | tf_op jit(solution)/shard_map/ppermute | solution.py:463
  80.7 3.6 %collective-permute-start.20 = (bf16[192,256]{1,0:T(8,128)(2,1)S(1)}, bf16[192,256]{1,0:T(8,128)(2,1)S(1)}, u32[]{:S(2)}, u32[]{:S(2)}) collective-permute-start(bf16[192,256]{1,0:T(8,128)(2,1)S(1)} %get-tuple-element.47), channel_id=1, source_target_pairs={{0,6},{1,7},{2,0},{3,1},{4,2},{5,3},{6,4},{7,5},{8,14},{9,15},{10,... | collective-permute-start | bytes 294920 | tf_op jit(solution)/shard_map/ppermute | solution.py:463
  84.4 5.0 %collective-permute-start.22 = (bf16[192,256]{1,0:T(8,128)(2,1)S(1)}, bf16[192,256]{1,0:T(8,128)(2,1)S(1)}, u32[]{:S(2)}, u32[]{:S(2)}) collective-permute-start(bf16[192,256]{1,0:T(8,128)(2,1)S(1)} %get-tuple-element.49), channel_id=1, source_target_pairs={{0,5},{1,6},{2,7},{3,0},{4,1},{5,2},{6,3},{7,4},{8,13},{9,14},{10,... | collective-permute-start | bytes 294920 | tf_op jit(solution)/shard_map/ppermute | solution.py:463
  89.4 3.2 %collective-permute-start.23 = (bf16[192,256]{1,0:T(8,128)(2,1)S(1)}, bf16[192,256]{1,0:T(8,128)(2,1)S(1)}, u32[]{:S(2)}, u32[]{:S(2)}) collective-permute-start(bf16[192,256]{1,0:T(8,128)(2,1)S(1)} %get-tuple-element.50), channel_id=1, source_target_pairs={{0,4},{1,5},{2,6},{3,7},{4,0},{5,1},{6,2},{7,3},{8,12},{9,13},{10,... | collective-permute-start | bytes 294920 | tf_op jit(solution)/shard_map/ppermute | solution.py:463
  92.6 4.1 %collective-permute-done.21.refs_5_ = bf16[192,256]{1,0:T(8,128)(2,1)S(1)} collective-permute-done((bf16[192,256]{1,0:T(8,128)(2,1)S(1)}, bf16[192,256]{1,0:T(8,128)(2,1)S(1)}, u32[]{:S(2)}, u32[]{:S(2)}) %collective-permute-start.21) | collective-permute-done | bytes 98336 | tf_op jit(solution)/shard_map/ppermute | solution.py:463
  96.7 2.1 %collective-permute-done.22.refs_6_ = bf16[192,256]{1,0:T(8,128)(2,1)S(1)} collective-permute-done((bf16[192,256]{1,0:T(8,128)(2,1)S(1)}, bf16[192,256]{1,0:T(8,128)(2,1)S(1)}, u32[]{:S(2)}, u32[]{:S(2)}) %collective-permute-start.22) | collective-permute-done | bytes 98336 | tf_op jit(solution)/shard_map/ppermute | solution.py:463
  98.8 23.9 %all_to_all.27.got = bf16[8,128,256]{2,1,0:T(8,128)(2,1)S(1)} all-to-all(bf16[8,128,256]{2,1,0:T(8,128)(2,1)S(1)} %get-tuple-element.51), channel_id=1, replica_groups=mesh['tok'=32,'mlp'=8] {'mlp'}, dimensions={0} | all-to-all | bytes 1048576 | tf_op jit(solution)/shard_map/all_to_all | solution.py:470
  122.7 4.4 %shard_map.147 = bf16[8,128,384]{2,1,0:T(8,128)(2,1)} custom-call(s32[1]{0:T(128)} %bitcast.me, s32[1]{0:T(128)} %bitcast.1.core, bf16[8,128,256]{2,1,0:T(8,128)(2,1)S(1)} %all_to_all.27.got, bf16[144,256]{1,0:T(8,128)(2,1)} %shard_map.142.refs_0_, bf16[144,256]{1,0:T(8,128)(2,1)} %collective-permute-done.9.refs_1_, ...), custom_call_target="tpu_custom_call" | custom-call | tf_op jit(solution)/shard_map/pallas_call | solution.py:472
  127.2 3.6 %all-to-all-start.4 = ((bf16[8,128,384]{2,1,0:T(8,128)(2,1)}), bf16[8,128,384]{2,1,0:T(8,128)(2,1)S(1)}, u32[]{:S(2)}, u32[]{:S(2)}) async-start(bf16[8,128,384]{2,1,0:T(8,128)(2,1)} %shard_map.147), calls=%async_computation.4 | async-start | bytes 1572864 | tf_op jit(solution)/shard_map/all_to_all | solution.py:491
  130.8 12.6 %shard_map.148.normal = f32[128,768]{1,0:T(8,128)S(1)} custom-call(bf16[8,64,256]{2,1,0:T(8,128)(2,1)S(1)} %get-tuple-element.61.slots), custom_call_target="tpu_custom_call" | custom-call | flops 4000000000 | bytes 1000000 | tf_op jit(solution)/shard_map/pallas_call | solution.py:494
  143.4 8.7 %all-to-all-done.4.got = bf16[8,128,384]{2,1,0:T(8,128)(2,1)S(1)} async-done(((bf16[8,128,384]{2,1,0:T(8,128)(2,1)}), bf16[8,128,384]{2,1,0:T(8,128)(2,1)S(1)}, u32[]{:S(2)}, u32[]{:S(2)}) %all-to-all-start.4) | async-done | bytes 786464 | tf_op jit(solution)/shard_map/all_to_all | solution.py:491
  (77 shorter events, 11.6 us)
Async XLA Ops:
  3.4 45.7 %all-to-all-start = ((bf16[32,272,128]{2,1,0:T(8,128)(2,1)}), bf16[32,272,128]{2,1,0:T(8,128)(2,1)S(1)}, u32[]{:S(2)}, u32[]{:S(2)}) async-start(bf16[32,272,128]{2,1,0:T(8,128)(2,1)} %shard_map.140), calls=%async_computation | async-start | bytes 4456448 | tf_op jit(solution)/shard_map/all_to_all | solution.py:380
  12.4 19.5 %collective-permute-start.5 = (bf16[256,256]{1,0:T(8,128)(2,1)S(1)}, bf16[256,256]{1,0:T(8,128)(2,1)S(1)}, u32[]{:S(2)}, u32[]{:S(2)}) collective-permute-start(bf16[256,256]{1,0:T(8,128)(2,1)S(1)} %pad_maximum_fusion), channel_id=1, source_target_pairs={{0,3},{1,4},{2,5},{3,6},{4,7},{5,0},{6,1},{7,2},{8,13},{9,14},{10,... | collective-permute-start | bytes 393224 | tf_op jit(solution)/shard_map/ppermute | solution.py:390
  17.1 14.9 %collective-permute-start.4 = (bf16[256,256]{1,0:T(8,128)(2,1)S(1)}, bf16[256,256]{1,0:T(8,128)(2,1)S(1)}, u32[]{:S(2)}, u32[]{:S(2)}) collective-permute-start(bf16[256,256]{1,0:T(8,128)(2,1)S(1)} %pad_maximum_fusion), channel_id=1, source_target_pairs={{0,2},{1,3},{2,4},{3,5},{4,6},{5,7},{6,0},{7,1},{8,14},{9,15},{10,... | collective-permute-start | bytes 393224 | tf_op jit(solution)/shard_map/ppermute | solution.py:390
  20.7 11.2 %collective-permute-start.1 = (bf16[128,256]{1,0:T(8,128)(2,1)S(1)}, bf16[128,256]{1,0:T(8,128)(2,1)S(1)}, u32[]{:S(2)}, u32[]{:S(2)}) collective-permute-start(bf16[128,256]{1,0:T(8,128)(2,1)S(1)} %bitcast.13), channel_id=1, source_target_pairs={{0,4},{1,5},{2,6},{3,7},{4,0},{5,1},{6,2},{7,3},{8,12},{9,13},{10,... | collective-permute-start | bytes 196616 | tf_op jit(solution)/shard_map/ppermute | solution.py:391
  21.6 17.6 %collective-permute-start.3 = (bf16[256,256]{1,0:T(8,128)(2,1)S(1)}, bf16[256,256]{1,0:T(8,128)(2,1)S(1)}, u32[]{:S(2)}, u32[]{:S(2)}) collective-permute-start(bf16[256,256]{1,0:T(8,128)(2,1)S(1)} %pad_maximum_fusion), channel_id=1, source_target_pairs={{0,1},{1,2},{2,3},{3,4},{4,5},{5,6},{6,7},{7,0},{8,15},{9,8},{10,9... | collective-permute-start | bytes 393224 | tf_op jit(solution)/shard_map/ppermute | solution.py:390
  23.7 9.1 %collective-permute-start.12 = (bf16[144,256]{1,0:T(8,128)(2,1)}, bf16[144,256]{1,0:T(8,128)(2,1)S(1)}, u32[]{:S(2)}, u32[]{:S(2)}) collective-permute-start(bf16[144,256]{1,0:T(8,128)(2,1)} %shard_map.142.refs_0_), channel_id=1, source_target_pairs={{0,3},{1,4},{2,5},{3,6},{4,7},{5,0},{6,1},{7,2},{8,13},{9,14},{10,... | collective-permute-start | bytes 221192 | tf_op jit(solution)/shard_map/ppermute | solution.py:390
  31.9 7.3 %collective-permute-start.11 = (bf16[144,256]{1,0:T(8,128)(2,1)}, bf16[144,256]{1,0:T(8,128)(2,1)}, u32[]{:S(2)}, u32[]{:S(2)}) collective-permute-start(bf16[144,256]{1,0:T(8,128)(2,1)} %shard_map.142.refs_0_), channel_id=1, source_target_pairs={{0,2},{1,3},{2,4},{3,5},{4,6},{5,7},{6,0},{7,1},{8,14},{9,15},{10,... | collective-permute-start | bytes 221192 | tf_op jit(solution)/shard_map/ppermute | solution.py:390
  31.9 11.7 %collective-permute-start.8 = (bf16[256,256]{1,0:T(8,128)(2,1)S(1)}, bf16[256,256]{1,0:T(8,128)(2,1)S(1)}, u32[]{:S(2)}, u32[]{:S(2)}) collective-permute-start(bf16[256,256]{1,0:T(8,128)(2,1)S(1)} %collective-permute-done.5.refs_6_), channel_id=1, source_target_pairs={{0,8},{8,0},{16,24},{24,16},{32,40},{40,32},{48,56},{56,48},{64,72... | collective-permute-start | bytes 393224 | tf_op jit(solution)/shard_map/ppermute | solution.py:392
  32.0 12.1 %collective-permute-start.7 = (bf16[256,256]{1,0:T(8,128)(2,1)S(1)}, bf16[256,256]{1,0:T(8,128)(2,1)S(1)}, u32[]{:S(2)}, u32[]{:S(2)}) collective-permute-start(bf16[256,256]{1,0:T(8,128)(2,1)S(1)} %collective-permute-done.4.refs_5_), channel_id=1, source_target_pairs={{0,8},{8,0},{16,24},{24,16},{32,40},{40,32},{48,56},{56,48},{64,72... | collective-permute-start | bytes 393224 | tf_op jit(solution)/shard_map/ppermute | solution.py:392
  32.9 6.8 %collective-permute-start.10 = (bf16[144,256]{1,0:T(8,128)(2,1)}, bf16[144,256]{1,0:T(8,128)(2,1)}, u32[]{:S(2)}, u32[]{:S(2)}) collective-permute-start(bf16[144,256]{1,0:T(8,128)(2,1)} %shard_map.142.refs_0_), channel_id=1, source_target_pairs={{0,1},{1,2},{2,3},{3,4},{4,5},{5,6},{6,7},{7,0},{8,15},{9,8},{10,9... | collective-permute-start | bytes 221192 | tf_op jit(solution)/shard_map/ppermute | solution.py:390
  39.2 5.2 %collective-permute-start.6 = (bf16[256,256]{1,0:T(8,128)(2,1)S(1)}, bf16[256,256]{1,0:T(8,128)(2,1)S(1)}, u32[]{:S(2)}, u32[]{:S(2)}) collective-permute-start(bf16[256,256]{1,0:T(8,128)(2,1)S(1)} %collective-permute-done.3.refs_4_), channel_id=1, source_target_pairs={{0,8},{8,0},{16,24},{24,16},{32,40},{40,32},{48,56},{56,48},{64,72... | collective-permute-start | bytes 393224 | tf_op jit(solution)/shard_map/ppermute | solution.py:392
  39.7 9.4 %collective-permute-start.9 = (bf16[144,256]{1,0:T(8,128)(2,1)}, bf16[144,256]{1,0:T(8,128)(2,1)}, u32[]{:S(2)}, u32[]{:S(2)}) collective-permute-start(bf16[144,256]{1,0:T(8,128)(2,1)} %shard_map.142.refs_0_), channel_id=1, source_target_pairs={{0,4},{1,5},{2,6},{3,7},{4,0},{5,1},{6,2},{7,3},{8,12},{9,13},{10,... | collective-permute-start | bytes 221192 | tf_op jit(solution)/shard_map/ppermute | solution.py:391
  43.6 5.5 %collective-permute-start.15 = (bf16[144,256]{1,0:T(8,128)(2,1)S(1)}, bf16[144,256]{1,0:T(8,128)(2,1)}, u32[]{:S(2)}, u32[]{:S(2)}) collective-permute-start(bf16[144,256]{1,0:T(8,128)(2,1)S(1)} %collective-permute-done.12.refs_4_), channel_id=1, source_target_pairs={{0,8},{8,0},{16,24},{24,16},{32,40},{40,32},{48,56},{56,48},{64,72... | collective-permute-start | bytes 221192 | tf_op jit(solution)/shard_map/ppermute | solution.py:392
  43.6 5.4 %collective-permute-start.14 = (bf16[144,256]{1,0:T(8,128)(2,1)}, bf16[144,256]{1,0:T(8,128)(2,1)}, u32[]{:S(2)}, u32[]{:S(2)}) collective-permute-start(bf16[144,256]{1,0:T(8,128)(2,1)} %collective-permute-done.11.refs_3_), channel_id=1, source_target_pairs={{0,8},{8,0},{16,24},{24,16},{32,40},{40,32},{48,56},{56,48},{64,72... | collective-permute-start | bytes 221192 | tf_op jit(solution)/shard_map/ppermute | solution.py:392
  44.1 4.9 %collective-permute-start.13 = (bf16[144,256]{1,0:T(8,128)(2,1)}, bf16[144,256]{1,0:T(8,128)(2,1)}, u32[]{:S(2)}, u32[]{:S(2)}) collective-permute-start(bf16[144,256]{1,0:T(8,128)(2,1)} %collective-permute-done.10.refs_2_), channel_id=1, source_target_pairs={{0,8},{8,0},{16,24},{24,16},{32,40},{40,32},{48,56},{56,48},{64,72... | collective-permute-start | bytes 221192 | tf_op jit(solution)/shard_map/ppermute | solution.py:392
  50.0 26.4 %collective-permute-start.16 = (bf16[32,64,128]{2,1,0:T(8,128)(2,1)S(1)}, bf16[32,64,128]{2,1,0:T(8,128)(2,1)S(1)}, u32[]{:S(2)}, u32[]{:S(2)}) collective-permute-start(bf16[32,64,128]{2,1,0:T(8,128)(2,1)S(1)} %slice.3), channel_id=1, source_target_pairs={{0,8},{8,0},{16,24},{24,16},{32,40},{40,32},{48,56},{56,48},{64,72... | collective-permute-start | bytes 1572872 | tf_op jit(solution)/shard_map/ppermute | solution.py:436
  76.9 7.5 %collective-permute-start.17 = (bf16[192,256]{1,0:T(8,128)(2,1)S(1)}, bf16[192,256]{1,0:T(8,128)(2,1)S(1)}, u32[]{:S(2)}, u32[]{:S(2)}) collective-permute-start(bf16[192,256]{1,0:T(8,128)(2,1)S(1)} %get-tuple-element.44), channel_id=1, source_target_pairs={{0,1},{1,2},{2,3},{3,4},{4,5},{5,6},{6,7},{7,0},{8,9},{9,10},{10,1... | collective-permute-start | bytes 294920 | tf_op jit(solution)/shard_map/ppermute | solution.py:463
  77.0 12.4 %collective-permute-start.18 = (bf16[192,256]{1,0:T(8,128)(2,1)S(1)}, bf16[192,256]{1,0:T(8,128)(2,1)S(1)}, u32[]{:S(2)}, u32[]{:S(2)}) collective-permute-start(bf16[192,256]{1,0:T(8,128)(2,1)S(1)} %get-tuple-element.45), channel_id=1, source_target_pairs={{0,7},{1,0},{2,1},{3,2},{4,3},{5,4},{6,5},{7,6},{8,15},{9,8},{10,9... | collective-permute-start | bytes 294920 | tf_op jit(solution)/shard_map/ppermute | solution.py:463
  80.2 12.4 %collective-permute-start.19 = (bf16[192,256]{1,0:T(8,128)(2,1)S(1)}, bf16[192,256]{1,0:T(8,128)(2,1)S(1)}, u32[]{:S(2)}, u32[]{:S(2)}) collective-permute-start(bf16[192,256]{1,0:T(8,128)(2,1)S(1)} %get-tuple-element.46), channel_id=1, source_target_pairs={{0,2},{1,3},{2,4},{3,5},{4,6},{5,7},{6,0},{7,1},{8,10},{9,11},{10,... | collective-permute-start | bytes 294920 | tf_op jit(solution)/shard_map/ppermute | solution.py:463
  80.7 11.9 %collective-permute-start.20 = (bf16[192,256]{1,0:T(8,128)(2,1)S(1)}, bf16[192,256]{1,0:T(8,128)(2,1)S(1)}, u32[]{:S(2)}, u32[]{:S(2)}) collective-permute-start(bf16[192,256]{1,0:T(8,128)(2,1)S(1)} %get-tuple-element.47), channel_id=1, source_target_pairs={{0,6},{1,7},{2,0},{3,1},{4,2},{5,3},{6,4},{7,5},{8,14},{9,15},{10,... | collective-permute-start | bytes 294920 | tf_op jit(solution)/shard_map/ppermute | solution.py:463
  84.4 12.3 %collective-permute-start.21 = (bf16[192,256]{1,0:T(8,128)(2,1)S(1)}, bf16[192,256]{1,0:T(8,128)(2,1)S(1)}, u32[]{:S(2)}, u32[]{:S(2)}) collective-permute-start(bf16[192,256]{1,0:T(8,128)(2,1)S(1)} %get-tuple-element.48), channel_id=1, source_target_pairs={{0,3},{1,4},{2,5},{3,6},{4,7},{5,0},{6,1},{7,2},{8,11},{9,12},{10,... | collective-permute-start | bytes 294920 | tf_op jit(solution)/shard_map/ppermute | solution.py:463
  84.4 14.4 %collective-permute-start.22 = (bf16[192,256]{1,0:T(8,128)(2,1)S(1)}, bf16[192,256]{1,0:T(8,128)(2,1)S(1)}, u32[]{:S(2)}, u32[]{:S(2)}) collective-permute-start(bf16[192,256]{1,0:T(8,128)(2,1)S(1)} %get-tuple-element.49), channel_id=1, source_target_pairs={{0,5},{1,6},{2,7},{3,0},{4,1},{5,2},{6,3},{7,4},{8,13},{9,14},{10,... | collective-permute-start | bytes 294920 | tf_op jit(solution)/shard_map/ppermute | solution.py:463
  89.4 9.3 %collective-permute-start.23 = (bf16[192,256]{1,0:T(8,128)(2,1)S(1)}, bf16[192,256]{1,0:T(8,128)(2,1)S(1)}, u32[]{:S(2)}, u32[]{:S(2)}) collective-permute-start(bf16[192,256]{1,0:T(8,128)(2,1)S(1)} %get-tuple-element.50), channel_id=1, source_target_pairs={{0,4},{1,5},{2,6},{3,7},{4,0},{5,1},{6,2},{7,3},{8,12},{9,13},{10,... | collective-permute-start | bytes 294920 | tf_op jit(solution)/shard_map/ppermute | solution.py:463
  127.2 24.9 %all-to-all-start.4 = ((bf16[8,128,384]{2,1,0:T(8,128)(2,1)}), bf16[8,128,384]{2,1,0:T(8,128)(2,1)S(1)}, u32[]{:S(2)}, u32[]{:S(2)}) async-start(bf16[8,128,384]{2,1,0:T(8,128)(2,1)} %shard_map.147), calls=%async_computation.4 | async-start | bytes 1572864 | tf_op jit(solution)/shard_map/all_to_all | solution.py:491
  (19 other events, 551.7 us)

commit v5 on v4

--- a/solution.py
+++ b/solution.py
@@ -41,11 +41,14 @@
         copy.wait()
 
 
-def pack_kernel(*refs):
-    ins, out, bufs, counts, sem = refs[:7], refs[7], refs[8:16], refs[16], refs[17]
+def pack_kernel(core, *refs):
+    ins, (out, both, far), bufs = refs[:11], refs[11:14], refs[14:22]
+    counts, w_buf, g_buf, both_buf, far_buf, sem = refs[22:]
     wqkv, wout_t, patch, base, weight, value, blocks, obs = bufs
-    dests = [*bufs[:6], counts]
-    loads = [pltpu.make_async_copy(ins[i], dests[i], sem.at[i]) for i in range(7)]
+    dests = [*bufs[:6], counts, w_buf, g_buf]
+    dests += [both_buf.at[pl.ds(0, 128), :]]
+    loads = [pltpu.make_async_copy(ins[i], dests[i], sem.at[i]) for i in range(10)]
+    loads.append(pltpu.make_async_copy(ins[9], far_buf.at[pl.ds(0, 128), :], sem.at[10]))
     for load in loads:
         load.start()
     loads[0].wait()
@@ -56,13 +59,30 @@
         blocks[c, 192:256, :] = wout_t[:, 128 * c : 128 * c + 128]
     n = out.shape[0]
     copies = [
-        pltpu.make_async_copy(blocks.at[d % 2], out.at[d, pl.ds(0, 256), :], sem.at[7 + d])
+        pltpu.make_async_copy(blocks.at[d % 2], out.at[d, pl.ds(0, 256), :], sem.at[12 + d])
         for d in range(n)
     ]
     for copy in copies:
         copy.start()
     for load in loads[2:]:
         load.wait()
+    g = g_buf[...]
+    high = g.astype(BF).astype(F32)
+    mid = (g - high).astype(BF).astype(F32)
+    rows = jnp.concatenate([high, mid, g - high - mid, jnp.zeros((13, 256), F32)], axis=0)
+    both_buf[128:256, :] = ins[10][...]
+    both_buf[256:384, 0:128] = w_buf[0:128, :]
+    both_buf[256:384, 128:256] = w_buf[128:256, :]
+    both_buf[384:400, :] = rows.astype(BF)
+    both_buf[400:416, :] = jnp.zeros((16, 256), BF)
+    far_buf[128:208, :] = both_buf[pl.ds(pl.multiple_of(256 + 80 * core[0], 16), 80), :]
+    more = [
+        pltpu.make_async_copy(both_buf, both, sem.at[13 + n]),
+        pltpu.make_async_copy(far_buf, far, sem.at[14 + n]),
+    ]
+    for copy in more:
+        copy.start()
+    copies += more
     slots = lanes((4, 64))
     zero = jnp.zeros((1, 64), F32)
     rest = jnp.zeros((12, 128), F32)
@@ -74,23 +94,11 @@
         other = [v, patch[0, row, :].astype(F32), base[0, row, :].astype(F32), zero]
         both = jnp.concatenate([w, jnp.concatenate(other, axis=0)], axis=1)
         obs[dest] = jnp.concatenate([both, rest], axis=0).astype(BF)
-    last = pltpu.make_async_copy(obs, out.at[:, pl.ds(256, 16), :], sem.at[7 + n])
+    last = pltpu.make_async_copy(obs, out.at[:, pl.ds(256, 16), :], sem.at[12 + n])
     last.start()
     for copy in copies:
         copy.wait()
     last.wait()
-
-
-def shared_kernel(wdec, gain, out, w_buf, g_buf, buf, sem):
-    fetch([(gain, g_buf), (wdec, w_buf)], sem)
-    g = g_buf[...]
-    high = g.astype(BF).astype(F32)
-    mid = (g - high).astype(BF).astype(F32)
-    rows = jnp.concatenate([high, mid, g - high - mid, jnp.zeros((13, 256), F32)], axis=0)
-    buf[0:128, 0:128] = w_buf[0:128, :]
-    buf[0:128, 128:256] = w_buf[128:256, :]
-    buf[128:144, :] = rows.astype(BF)
-    fetch([(buf, out)], sem)
 
 
 def groups_of(me, core):
@@ -101,18 +109,17 @@
 
 
 def norm_kernel(me, core, *refs):
-    x, other, far, far_sib, mine, theirs = *refs[:4], refs[4:7], refs[7:10]
-    gain, out, buf, sem = refs[10:]
+    both, far, far_sib, mine, theirs = *refs[:3], refs[3:6], refs[6:9]
+    gain, out, buf, sem = refs[9:]
     near, across, opposite = groups_of(me, core)
     low, top = pl.ds(0, 128), pl.ds(128, 128)
     pairs = [
-        (x, buf.at[me[0], low, :]),
-        (other, buf.at[me[0], top, :]),
-        (far, buf.at[opposite, low, :]),
-        (far_sib, buf.at[opposite, top, :]),
+        (both.at[pl.ds(0, 256), :], buf.at[me[0]]),
+        (far.at[low, :], buf.at[opposite, low, :]),
+        (far_sib.at[low, :], buf.at[opposite, top, :]),
     ]
     for k in range(3):
-        pairs.append((mine[k], buf.at[near[k]]))
+        pairs.append((mine[k].at[pl.ds(0, 256), :], buf.at[near[k]]))
         pairs.append((theirs[k].at[top, :], buf.at[across[k], low, :]))
         pairs.append((theirs[k].at[low, :], buf.at[across[k], top, :]))
     fetch(pairs, sem)
@@ -266,13 +273,17 @@
 
 
 def ffn_kernel(me, core, got, *refs):
-    own, far, mine, theirs = refs[0], refs[1], refs[2:5], refs[5:8]
-    up, down, resid, own_dec, out, shared, sem = refs[8:]
+    own, far, far_sib, mine, theirs = refs[0], refs[1], refs[2], refs[3:6], refs[6:9]
+    up, down, resid, own_dec, out, shared, sem = refs[9:]
     near, across, opposite = groups_of(me, core)
-    pairs = [(own, shared.at[me[0]]), (far, shared.at[opposite])]
+    common = pl.ds(256, 160)
+    pairs = [(own.at[common, :], shared.at[me[0]])]
+    for half_far, c in ((far, core[0]), (far_sib, 1 - core[0])):
+        side = pl.ds(pl.multiple_of(80 * c, 16), 80)
+        pairs.append((half_far.at[pl.ds(128, 80), :], shared.at[opposite, side, :]))
     for k in range(3):
-        pairs.append((mine[k], shared.at[near[k]]))
-        pairs.append((theirs[k], shared.at[across[k]]))
+        pairs.append((mine[k].at[common, :], shared.at[near[k]]))
+        pairs.append((theirs[k].at[common, :], shared.at[across[k]]))
     fetch(pairs, sem)
     squares = jnp.zeros((128, 1), F32)
     for k in range(8):
@@ -357,11 +368,16 @@
     smem = pl.BlockSpec(memory_space=pltpu.SMEM)
     whole = lambda *shape: pl.BlockSpec(shape, lambda i: (0,) * len(shape))
 
-    send = pl.pallas_call(
+    other = lax.ppermute(x, "tok", pairs)
+    send, both, far = pl.pallas_call(
         pack_kernel,
-        in_specs=[hbm] * 7,
-        out_specs=hbm,
-        out_shape=pltpu.HBM((32, 272, 128), BF),
+        in_specs=[smem] + [hbm] * 10 + [vmem],
+        out_specs=(hbm, hbm, hbm),
+        out_shape=(
+            pltpu.HBM((32, 272, 128), BF),
+            pltpu.HBM((416, 256), BF),
+            pltpu.HBM((208, 256), BF),
+        ),
         scratch_shapes=[
             pltpu.VMEM((64, 768), BF),
             pltpu.VMEM((64, 256), BF),
@@ -372,12 +388,22 @@
             pltpu.VMEM((2, 256, 128), BF),
             pltpu.VMEM((32, 16, 128), BF),
             pltpu.SMEM((1, 32), jnp.int32),
-            pltpu.SemaphoreType.DMA((40,)),
+            pltpu.VMEM((256, 128), BF),
+            pltpu.VMEM((1, 256), F32),
+            pltpu.VMEM((416, 256), BF),
+            pltpu.VMEM((208, 256), BF),
+            pltpu.SemaphoreType.DMA((47,)),
         ],
         compiler_params=params(8),
-    )(*map(stay, (w_qkv, w_out.T, obs_patch, obs_base, obs_weight, obs_value, obs_count)))
-
-    weights_in = lax.all_to_all(send, "tok", 0, 0, tiled=True)
+    )(
+        core,
+        *map(stay, (w_qkv, w_out.T, obs_patch, obs_base, obs_weight, obs_value, obs_count)),
+        stay(w_dec),
+        stay(gain_mlp.reshape(1, 256)),
+        stay(x),
+        other,
+    )
+
 
     def shifted(k):
         return [
@@ -392,40 +418,21 @@
         theirs = [lax.ppermute(r, "tok", pairs) for r in mine]
         return far_in, mine, theirs
 
-    other = lax.ppermute(x, "tok", pairs)
-    both, first, _ = lax.optimization_barrier((jnp.concatenate([x, other], axis=0), x, send))
-    far_in, mine, theirs = gathered(both, first)
+    weights_in = lax.all_to_all(send, "tok", 0, 0, tiled=True)
+    far_in, mine, theirs = gathered(both, far)
+    packs = (both, far_in, lax.ppermute(far_in, "tok", pairs), *mine, *theirs)
     normed = pl.pallas_call(
         norm_kernel,
-        in_specs=[smem] * 2 + [hbm] * 10 + [vmem],
+        in_specs=[smem] * 2 + [hbm] * 9 + [vmem],
         out_shape=sds((8, 256, 256)),
         scratch_shapes=[pltpu.VMEM((8, 256, 256), BF), pltpu.SemaphoreType.DMA((13,))],
         compiler_params=params(8),
     )(
         me,
         core,
-        *map(stay, (x, other, far_in, lax.ppermute(far_in, "tok", pairs), *mine, *theirs)),
+        *map(stay, packs),
         gain_attn.reshape(8, 1, 256),
     )
-    shared = pl.pallas_call(
-        shared_kernel,
-        in_specs=[hbm] * 2,
-        out_specs=hbm,
-        out_shape=pltpu.HBM((144, 256), BF),
-        scratch_shapes=[
-            pltpu.VMEM((256, 128), BF),
-            pltpu.VMEM((1, 256), F32),
-            pltpu.VMEM((144, 256), BF),
-            pltpu.SemaphoreType.DMA((2,)),
-        ],
-        compiler_params=params(4),
-    )(stay(w_dec), stay(gain_mlp.reshape(1, 256)))
-    shared, _ = lax.optimization_barrier((shared, both))
-    far_shared, mine_shared, theirs_shared = gathered(shared, shared)
-    weights_in, *others = lax.optimization_barrier(
-        (weights_in, far_shared, *mine_shared, *theirs_shared)
-    )
-
     qkv, slots = pl.pallas_call(
         qkv_kernel,
         out_shape=(sds((16, 48, 128)), sds((64, 256))),
@@ -471,18 +478,18 @@
 
     down_out = pl.pallas_call(
         ffn_kernel,
-        in_specs=[smem] * 2 + [vmem] + [hbm] * 8 + [vmem] * 4,
+        in_specs=[smem] * 2 + [vmem] + [hbm] * 9 + [vmem] * 4,
         out_shape=sds((8, 128, 384)),
         scratch_shapes=[
-            pltpu.VMEM((8, 144, 256), BF),
-            pltpu.SemaphoreType.DMA((8,)),
+            pltpu.VMEM((8, 160, 256), BF),
+            pltpu.SemaphoreType.DMA((9,)),
         ],
         compiler_params=params(8),
     )(
         me,
         core,
         wide,
-        *map(stay, (shared, *others)),
+        *map(stay, packs),
         w_up,
         w_down,
         resid,

time: 154 us -> 149 us (0.968)
  starting transfers between devices: 49.8 us -> 45 us
  waiting for transfers between devices: 25.9 us -> 27.7 us
    ppermute x6 -> x3, starting transfers between devices: 15.9 us -> 9.3 us  [gathered(): mine = [lax.ppermute(near, ('tok', 'mlp'), shifted(k)) for k in (1, 2, 3)]]
    ppermute x6 -> x3, starting transfers between devices: 1.86 us -> 7.4 us  [gathered(): theirs = [lax.ppermute(r, 'tok', pairs) for r in mine]]
    ppermute x2 -> x1, starting transfers between devices: 4.82 us -> 0.54 us  [gathered(): far_in = lax.ppermute(far, 'mlp', ring[4])]
    ppermute x6 -> x3, waiting for transfers between devices: 4.74 us -> 8.2 us  [gathered(): mine = [lax.ppermute(near, ('tok', 'mlp'), shifted(k)) for k in (1, 2, 3)]]
    ppermute x2 -> x1, waiting for transfers between devices: 5.13 us -> 2.43 us  [gathered(): far_in = lax.ppermute(far, 'mlp', ring[4])]
    pallas_call x4 -> x3, Pallas kernels: 10.6 us -> 9.18 us  [the longest x1 4.49 us: body(): pl.pallas_call(ffn_kernel, in_specs=[smem] * 2 + [vmem] + [hbm] * 9 + [vm...]
  transfers between devices with their start and end apart: 26 -> 19, of which waited for: 8 -> 9; matrix products, arithmetic and copies ran while one was open for 0% -> 0% of each run, Pallas kernels for 11% -> 10%
where the time goes in v5:
time: 149 us
  blocking collectives  49.1 us (33%)
  starting transfers between devices  45 us (30%)
  waiting for transfers between devices  27.7 us (19%)
  Pallas kernels  25.2 us (17%)
    all_to_all x1, blocking collectives, body(): wide = lax.all_to_all(scaled, 'mlp', 0, 0, tiled=True)  23.6 us
    ppermute x7, starting transfers between devices, body(): lax.ppermute(shares[d], 'mlp', ring[d])  16.1 us
    all_to_all x1, blocking collectives, body(): lax.all_to_all(qkv, 'tok', 0, 0, tiled=True, axis_index_groups=chips)  14.4 us
    pallas_call x1, Pallas kernels, body(): pl.pallas_call(normal_kernel, grid=(1,), in_specs=[whole(8, 64, 256)], ou...  12.6 us
    all_to_all x1, blocking collectives, body(): lax.all_to_all(attended.reshape(32, 16, 128), 'tok', 0, 0, tiled=True)  11.1 us
    ppermute x3, starting transfers between devices, gathered(): mine = [lax.ppermute(near, ('tok', 'mlp'), shifted(k)) for k in (1, 2, 3)]  9.3 us
    all_to_all x1, waiting for transfers between devices, body(): down_in = lax.all_to_all(down_out, 'mlp', 0, 0, tiled=True)  8.43 us
    ppermute x3, waiting for transfers between devices, gathered(): mine = [lax.ppermute(near, ('tok', 'mlp'), shifted(k)) for k in (1, 2, 3)]  8.2 us
  transfers between devices with their start and end apart: 19, of which 9 were waited for; matrix products, arithmetic and copies ran while one was open for 0% of the time, Pallas kernels for 10%

profile of v5, /device:TPU:2, one launch (start us, length us, event | category | flops | bytes accessed | tf_op | source)
XLA Modules:
  0.0 148.7 jit_solution(7236444638309505985)
XLA Ops:
  0.8 1.4 collective-permute-done.refs_10_
  2.2 2.8 %shard_map.140 = (bf16[32,272,128]{2,1,0:T(8,128)(2,1)}, bf16[416,256]{1,0:T(8,128)(2,1)}, bf16[208,256]{1,0:T(8,128)(2,1)}) custom-call(s32[1]{0:T(128)} %bitcast.1.core, bf16[64,768]{1,0:T(8,128)(2,1)} %refs_0_.1, bf16[64,256]{1,0:T(8,128)(2,1)} %bitcast.18, s32[1,32,64]{2,1,0:T(8,128)} %refs_2_.1, s32[1,32,64]{2,1,0:T(8,128)} %refs_3_.1, ...), custom_call_target="tpu_custom_call" | custom-call | tf_op jit(solution)/shard_map/pallas_call | solution.py:372
  5.0 7.8 %all-to-all-start = ((bf16[32,272,128]{2,1,0:T(8,128)(2,1)}), bf16[32,272,128]{2,1,0:T(8,128)(2,1)S(1)}, u32[]{:S(2)}, u32[]{:S(2)}) async-start(bf16[32,272,128]{2,1,0:T(8,128)(2,1)} %get-tuple-element.28), calls=%async_computation | async-start | bytes 4456448 | tf_op jit(solution)/shard_map/all_to_all | solution.py:421
  12.8 4.7 %collective-permute-start.5 = (bf16[416,256]{1,0:T(8,128)(2,1)S(1)}, bf16[416,256]{1,0:T(8,128)(2,1)S(1)}, u32[]{:S(2)}, u32[]{:S(2)}) collective-permute-start(bf16[416,256]{1,0:T(8,128)(2,1)S(1)} %copy-done.6), channel_id=1, source_target_pairs={{0,3},{1,4},{2,5},{3,6},{4,7},{5,0},{6,1},{7,2},{8,13},{9,14},{10,... | collective-permute-start | bytes 638984 | tf_op jit(solution)/shard_map/ppermute | solution.py:416
  17.5 3.6 %collective-permute-start.4 = (bf16[416,256]{1,0:T(8,128)(2,1)S(1)}, bf16[416,256]{1,0:T(8,128)(2,1)S(1)}, u32[]{:S(2)}, u32[]{:S(2)}) collective-permute-start(bf16[416,256]{1,0:T(8,128)(2,1)S(1)} %copy-done.6), channel_id=1, source_target_pairs={{0,2},{1,3},{2,4},{3,5},{4,6},{5,7},{6,0},{7,1},{8,14},{9,15},{10,... | collective-permute-start | bytes 638984 | tf_op jit(solution)/shard_map/ppermute | solution.py:416
  23.6 5.5 %collective-permute-start.8 = (bf16[416,256]{1,0:T(8,128)(2,1)S(1)}, bf16[416,256]{1,0:T(8,128)(2,1)S(1)}, u32[]{:S(2)}, u32[]{:S(2)}) collective-permute-start(bf16[416,256]{1,0:T(8,128)(2,1)S(1)} %collective-permute-done.5.refs_5_), channel_id=1, source_target_pairs={{0,8},{8,0},{16,24},{24,16},{32,40},{40,32},{48,56},{56,48},{64,72... | collective-permute-start | bytes 638984 | tf_op jit(solution)/shard_map/ppermute | solution.py:418
  29.1 5.3 %collective-permute-done.4.refs_4_ = bf16[416,256]{1,0:T(8,128)(2,1)S(1)} collective-permute-done((bf16[416,256]{1,0:T(8,128)(2,1)S(1)}, bf16[416,256]{1,0:T(8,128)(2,1)S(1)}, u32[]{:S(2)}, u32[]{:S(2)}) %collective-permute-start.4) | collective-permute-done | bytes 213024 | tf_op jit(solution)/shard_map/ppermute | solution.py:416
  34.4 1.9 %collective-permute-done.3.refs_3_ = bf16[416,256]{1,0:T(8,128)(2,1)S(1)} collective-permute-done((bf16[416,256]{1,0:T(8,128)(2,1)S(1)}, bf16[416,256]{1,0:T(8,128)(2,1)S(1)}, u32[]{:S(2)}, u32[]{:S(2)}) %collective-permute-start.3) | collective-permute-done | bytes 213024 | tf_op jit(solution)/shard_map/ppermute | solution.py:416
  36.3 1.9 %collective-permute-start.6 = (bf16[416,256]{1,0:T(8,128)(2,1)S(1)}, bf16[416,256]{1,0:T(8,128)(2,1)S(1)}, u32[]{:S(2)}, u32[]{:S(2)}) collective-permute-start(bf16[416,256]{1,0:T(8,128)(2,1)S(1)} %collective-permute-done.3.refs_3_), channel_id=1, source_target_pairs={{0,8},{8,0},{16,24},{24,16},{32,40},{40,32},{48,56},{56,48},{64,72... | collective-permute-start | bytes 638984 | tf_op jit(solution)/shard_map/ppermute | solution.py:418
  38.2 2.4 %collective-permute-done.1.refs_1_ = bf16[208,256]{1,0:T(8,128)(2,1)S(1)} collective-permute-done((bf16[208,256]{1,0:T(8,128)(2,1)}, bf16[208,256]{1,0:T(8,128)(2,1)S(1)}, u32[]{:S(2)}, u32[]{:S(2)}) %collective-permute-start.1) | collective-permute-done | bytes 106528 | tf_op jit(solution)/shard_map/ppermute | solution.py:417
  42.9 1.9 %shard_map.141.normed = bf16[8,256,256]{2,1,0:T(8,128)(2,1)S(1)} custom-call(s32[1]{0:T(128)} %bitcast.me, s32[1]{0:T(128)} %bitcast.1.core, bf16[416,256]{1,0:T(8,128)(2,1)} %get-tuple-element.26.refs_0_, bf16[208,256]{1,0:T(8,128)(2,1)} %copy-done.12, bf16[208,256]{1,0:T(8,128)(2,1)} %collective-permute-done.2.refs_2_, bf16[416,256]{1,0:T(8,128)(2,1)} %copy-done.9, ...), custom_call_target="tpu_custom_call" | custom-call | tf_op jit(solution)/shard_map/pallas_call | solution.py:424
  46.0 14.4 %all_to_all.25.got = bf16[16,48,128]{2,1,0:T(8,128)(2,1)S(1)} all-to-all(bf16[16,48,128]{2,1,0:T(8,128)(2,1)S(1)} %get-tuple-element.29), channel_id=1, replica_groups={{0,16,32,48,64,80,96,112,128,144,160,176,192,208,224,240},{8,24,40,56,7..., dimensions={0} | all-to-all | bytes 393216 | tf_op jit(solution)/shard_map/all_to_all | solution.py:441
  61.3 11.1 %all_to_all.26 = bf16[32,16,128]{2,1,0:T(8,128)(2,1)S(1)} all-to-all(bf16[32,16,128]{2,1,0:T(8,128)(2,1)S(1)} %bitcast.10), channel_id=1, replica_groups=mesh['tok'=32,'mlp'=8] {'tok'}, dimensions={0} | all-to-all | bytes 262144 | tf_op jit(solution)/shard_map/all_to_all | solution.py:451
  73.0 3.2 %collective-permute-start.11 = (bf16[192,256]{1,0:T(8,128)(2,1)S(1)}, bf16[192,256]{1,0:T(8,128)(2,1)S(1)}, u32[]{:S(2)}, u32[]{:S(2)}) collective-permute-start(bf16[192,256]{1,0:T(8,128)(2,1)S(1)} %get-tuple-element.36), channel_id=1, source_target_pairs={{0,7},{1,0},{2,1},{3,2},{4,3},{5,4},{6,5},{7,6},{8,15},{9,8},{10,9... | collective-permute-start | bytes 294920 | tf_op jit(solution)/shard_map/ppermute | solution.py:470
  76.2 4.1 %collective-permute-start.13 = (bf16[192,256]{1,0:T(8,128)(2,1)S(1)}, bf16[192,256]{1,0:T(8,128)(2,1)S(1)}, u32[]{:S(2)}, u32[]{:S(2)}) collective-permute-start(bf16[192,256]{1,0:T(8,128)(2,1)S(1)} %get-tuple-element.38), channel_id=1, source_target_pairs={{0,6},{1,7},{2,0},{3,1},{4,2},{5,3},{6,4},{7,5},{8,14},{9,15},{10,... | collective-permute-start | bytes 294920 | tf_op jit(solution)/shard_map/ppermute | solution.py:470
  80.4 5.0 %collective-permute-start.15 = (bf16[192,256]{1,0:T(8,128)(2,1)S(1)}, bf16[192,256]{1,0:T(8,128)(2,1)S(1)}, u32[]{:S(2)}, u32[]{:S(2)}) collective-permute-start(bf16[192,256]{1,0:T(8,128)(2,1)S(1)} %get-tuple-element.40), channel_id=1, source_target_pairs={{0,5},{1,6},{2,7},{3,0},{4,1},{5,2},{6,3},{7,4},{8,13},{9,14},{10,... | collective-permute-start | bytes 294920 | tf_op jit(solution)/shard_map/ppermute | solution.py:470
  85.4 3.6 %collective-permute-start.16 = (bf16[192,256]{1,0:T(8,128)(2,1)S(1)}, bf16[192,256]{1,0:T(8,128)(2,1)S(1)}, u32[]{:S(2)}, u32[]{:S(2)}) collective-permute-start(bf16[192,256]{1,0:T(8,128)(2,1)S(1)} %get-tuple-element.41), channel_id=1, source_target_pairs={{0,4},{1,5},{2,6},{3,7},{4,0},{5,1},{6,2},{7,3},{8,12},{9,13},{10,... | collective-permute-start | bytes 294920 | tf_op jit(solution)/shard_map/ppermute | solution.py:470
  89.0 3.0 %collective-permute-done.14.refs_5_ = bf16[192,256]{1,0:T(8,128)(2,1)S(1)} collective-permute-done((bf16[192,256]{1,0:T(8,128)(2,1)S(1)}, bf16[192,256]{1,0:T(8,128)(2,1)S(1)}, u32[]{:S(2)}, u32[]{:S(2)}) %collective-permute-start.14) | collective-permute-done | bytes 98336 | tf_op jit(solution)/shard_map/ppermute | solution.py:470
  92.1 2.7 %collective-permute-done.15.refs_6_ = bf16[192,256]{1,0:T(8,128)(2,1)S(1)} collective-permute-done((bf16[192,256]{1,0:T(8,128)(2,1)S(1)}, bf16[192,256]{1,0:T(8,128)(2,1)S(1)}, u32[]{:S(2)}, u32[]{:S(2)}) %collective-permute-start.15) | collective-permute-done | bytes 98336 | tf_op jit(solution)/shard_map/ppermute | solution.py:470
  94.9 23.6 %all_to_all.27.got = bf16[8,128,256]{2,1,0:T(8,128)(2,1)S(1)} all-to-all(bf16[8,128,256]{2,1,0:T(8,128)(2,1)S(1)} %get-tuple-element.42), channel_id=1, replica_groups=mesh['tok'=32,'mlp'=8] {'mlp'}, dimensions={0} | all-to-all | bytes 1048576 | tf_op jit(solution)/shard_map/all_to_all | solution.py:477
  118.5 4.5 %shard_map.146 = bf16[8,128,384]{2,1,0:T(8,128)(2,1)} custom-call(s32[1]{0:T(128)} %bitcast.me, s32[1]{0:T(128)} %bitcast.1.core, bf16[8,128,256]{2,1,0:T(8,128)(2,1)S(1)} %all_to_all.27.got, bf16[416,256]{1,0:T(8,128)(2,1)} %get-tuple-element.26.refs_0_, bf16[208,256]{1,0:T(8,128)(2,1)} %copy-done.12, bf16[208,256]{1,0:T(8,128)(2,1)} %collective-permute-done.2.refs_2_, ...), custom_call_target="tpu_custom_call" | custom-call | tf_op jit(solution)/shard_map/pallas_call | solution.py:479
  123.0 3.6 %all-to-all-start.4 = ((bf16[8,128,384]{2,1,0:T(8,128)(2,1)}), bf16[8,128,384]{2,1,0:T(8,128)(2,1)S(1)}, u32[]{:S(2)}, u32[]{:S(2)}) async-start(bf16[8,128,384]{2,1,0:T(8,128)(2,1)} %shard_map.146), calls=%async_computation.4 | async-start | bytes 1572864 | tf_op jit(solution)/shard_map/all_to_all | solution.py:498
  126.6 12.6 %shard_map.147.normal = f32[128,768]{1,0:T(8,128)S(1)} custom-call(bf16[8,64,256]{2,1,0:T(8,128)(2,1)S(1)} %get-tuple-element.45.slots), custom_call_target="tpu_custom_call" | custom-call | flops 4000000000 | bytes 1000000 | tf_op jit(solution)/shard_map/pallas_call | solution.py:501
  139.2 8.4 %all-to-all-done.4.got = bf16[8,128,384]{2,1,0:T(8,128)(2,1)S(1)} async-done(((bf16[8,128,384]{2,1,0:T(8,128)(2,1)}), bf16[8,128,384]{2,1,0:T(8,128)(2,1)S(1)}, u32[]{:S(2)}, u32[]{:S(2)}) %all-to-all-start.4) | async-done | bytes 786464 | tf_op jit(solution)/shard_map/all_to_all | solution.py:498
  (53 shorter events, 8.7 us)
Async XLA Ops:
  0.6 1.6 %collective-permute-start = (bf16[128,256]{1,0:T(8,128)(2,1)}, bf16[128,256]{1,0:T(8,128)(2,1)S(1)}, u32[]{:S(2)}, u32[]{:S(2)}) collective-permute-start(bf16[128,256]{1,0:T(8,128)(2,1)} %bitcast.12), channel_id=1, source_target_pairs={{0,8},{8,0},{16,24},{24,16},{32,40},{40,32},{48,56},{56,48},{64,72... | collective-permute-start | bytes 196616 | tf_op jit(solution)/shard_map/ppermute | solution.py:371
  5.0 39.8 %all-to-all-start = ((bf16[32,272,128]{2,1,0:T(8,128)(2,1)}), bf16[32,272,128]{2,1,0:T(8,128)(2,1)S(1)}, u32[]{:S(2)}, u32[]{:S(2)}) async-start(bf16[32,272,128]{2,1,0:T(8,128)(2,1)} %get-tuple-element.28), calls=%async_computation | async-start | bytes 4456448 | tf_op jit(solution)/shard_map/all_to_all | solution.py:421
  12.8 10.9 %collective-permute-start.5 = (bf16[416,256]{1,0:T(8,128)(2,1)S(1)}, bf16[416,256]{1,0:T(8,128)(2,1)S(1)}, u32[]{:S(2)}, u32[]{:S(2)}) collective-permute-start(bf16[416,256]{1,0:T(8,128)(2,1)S(1)} %copy-done.6), channel_id=1, source_target_pairs={{0,3},{1,4},{2,5},{3,6},{4,7},{5,0},{6,1},{7,2},{8,13},{9,14},{10,... | collective-permute-start | bytes 638984 | tf_op jit(solution)/shard_map/ppermute | solution.py:416
  17.5 17.0 %collective-permute-start.4 = (bf16[416,256]{1,0:T(8,128)(2,1)S(1)}, bf16[416,256]{1,0:T(8,128)(2,1)S(1)}, u32[]{:S(2)}, u32[]{:S(2)}) collective-permute-start(bf16[416,256]{1,0:T(8,128)(2,1)S(1)} %copy-done.6), channel_id=1, source_target_pairs={{0,2},{1,3},{2,4},{3,5},{4,6},{5,7},{6,0},{7,1},{8,14},{9,15},{10,... | collective-permute-start | bytes 638984 | tf_op jit(solution)/shard_map/ppermute | solution.py:416
  21.0 15.3 %collective-permute-start.3 = (bf16[416,256]{1,0:T(8,128)(2,1)S(1)}, bf16[416,256]{1,0:T(8,128)(2,1)S(1)}, u32[]{:S(2)}, u32[]{:S(2)}) collective-permute-start(bf16[416,256]{1,0:T(8,128)(2,1)S(1)} %copy-done.6), channel_id=1, source_target_pairs={{0,1},{1,2},{2,3},{3,4},{4,5},{5,6},{6,7},{7,0},{8,15},{9,8},{10,9... | collective-permute-start | bytes 638984 | tf_op jit(solution)/shard_map/ppermute | solution.py:416
  22.1 18.6 %collective-permute-start.1 = (bf16[208,256]{1,0:T(8,128)(2,1)}, bf16[208,256]{1,0:T(8,128)(2,1)S(1)}, u32[]{:S(2)}, u32[]{:S(2)}) collective-permute-start(bf16[208,256]{1,0:T(8,128)(2,1)} %get-tuple-element.27), channel_id=1, source_target_pairs={{0,4},{1,5},{2,6},{3,7},{4,0},{5,1},{6,2},{7,3},{8,12},{9,13},{10,... | collective-permute-start | bytes 319496 | tf_op jit(solution)/shard_map/ppermute | solution.py:417
  23.6 18.5 %collective-permute-start.8 = (bf16[416,256]{1,0:T(8,128)(2,1)S(1)}, bf16[416,256]{1,0:T(8,128)(2,1)S(1)}, u32[]{:S(2)}, u32[]{:S(2)}) collective-permute-start(bf16[416,256]{1,0:T(8,128)(2,1)S(1)} %collective-permute-done.5.refs_5_), channel_id=1, source_target_pairs={{0,8},{8,0},{16,24},{24,16},{32,40},{40,32},{48,56},{56,48},{64,72... | collective-permute-start | bytes 638984 | tf_op jit(solution)/shard_map/ppermute | solution.py:418
  34.4 7.7 %collective-permute-start.7 = (bf16[416,256]{1,0:T(8,128)(2,1)S(1)}, bf16[416,256]{1,0:T(8,128)(2,1)}, u32[]{:S(2)}, u32[]{:S(2)}) collective-permute-start(bf16[416,256]{1,0:T(8,128)(2,1)S(1)} %collective-permute-done.4.refs_4_), channel_id=1, source_target_pairs={{0,8},{8,0},{16,24},{24,16},{32,40},{40,32},{48,56},{56,48},{64,72... | collective-permute-start | bytes 638984 | tf_op jit(solution)/shard_map/ppermute | solution.py:418
  36.3 5.8 %collective-permute-start.6 = (bf16[416,256]{1,0:T(8,128)(2,1)S(1)}, bf16[416,256]{1,0:T(8,128)(2,1)S(1)}, u32[]{:S(2)}, u32[]{:S(2)}) collective-permute-start(bf16[416,256]{1,0:T(8,128)(2,1)S(1)} %collective-permute-done.3.refs_3_), channel_id=1, source_target_pairs={{0,8},{8,0},{16,24},{24,16},{32,40},{40,32},{48,56},{56,48},{64,72... | collective-permute-start | bytes 638984 | tf_op jit(solution)/shard_map/ppermute | solution.py:418
  40.7 1.4 collective-permute-start.2
  44.8 50.0 %copy-start.3 = (bf16[8,16,256]{2,1,0:T(8,128)(2,1)S(1)}, bf16[8,16,256]{2,1,0:T(8,128)(2,1)}, u32[]{:S(2)}) copy-start(bf16[8,16,256]{2,1,0:T(8,128)(2,1)} %param.13) | copy-start | bytes 196612
  44.8 50.0 %copy-start.5 = (f32[256]{0:T(256)S(1)}, f32[256]{0:T(256)}, u32[]{:S(2)}) copy-start(f32[256]{0:T(256)} %param.20) | copy-start | bytes 3076
  44.8 73.7 %copy-start.1 = (bf16[1024,2048]{1,0:T(8,128)(2,1)S(1)}, bf16[1024,2048]{1,0:T(8,128)(2,1)}, u32[]{:S(2)}) copy-start(bf16[1024,2048]{1,0:T(8,128)(2,1)} %refs_10_.1) | copy-start | bytes 12582916
  45.6 72.8 %copy-start = (bf16[2048,1024]{1,0:T(8,128)(2,1)S(1)}, bf16[2048,1024]{1,0:T(8,128)(2,1)}, u32[]{:S(2)}) copy-start(bf16[2048,1024]{1,0:T(8,128)(2,1)} %refs_9_.1) | copy-start | bytes 12582916
  45.6 72.8 %copy-start.2 = (bf16[256,128]{1,0:T(8,128)(2,1)S(1)}, bf16[256,128]{1,0:T(8,128)(2,1)}, u32[]{:S(2)}) copy-start(bf16[256,128]{1,0:T(8,128)(2,1)} %own_dec.1) | copy-start | bytes 196612
  45.7 26.7 %collective-permute-start.9 = (bf16[32,64,128]{2,1,0:T(8,128)(2,1)S(1)}, bf16[32,64,128]{2,1,0:T(8,128)(2,1)S(1)}, u32[]{:S(2)}, u32[]{:S(2)}) collective-permute-start(bf16[32,64,128]{2,1,0:T(8,128)(2,1)S(1)} %slice.3), channel_id=1, source_target_pairs={{0,8},{8,0},{16,24},{24,16},{32,40},{40,32},{48,56},{56,48},{64,72... | collective-permute-start | bytes 1572872 | tf_op jit(solution)/shard_map/ppermute | solution.py:443
  72.9 7.5 %collective-permute-start.10 = (bf16[192,256]{1,0:T(8,128)(2,1)S(1)}, bf16[192,256]{1,0:T(8,128)(2,1)S(1)}, u32[]{:S(2)}, u32[]{:S(2)}) collective-permute-start(bf16[192,256]{1,0:T(8,128)(2,1)S(1)} %get-tuple-element.35), channel_id=1, source_target_pairs={{0,1},{1,2},{2,3},{3,4},{4,5},{5,6},{6,7},{7,0},{8,9},{9,10},{10,1... | collective-permute-start | bytes 294920 | tf_op jit(solution)/shard_map/ppermute | solution.py:470
  73.0 12.4 %collective-permute-start.11 = (bf16[192,256]{1,0:T(8,128)(2,1)S(1)}, bf16[192,256]{1,0:T(8,128)(2,1)S(1)}, u32[]{:S(2)}, u32[]{:S(2)}) collective-permute-start(bf16[192,256]{1,0:T(8,128)(2,1)S(1)} %get-tuple-element.36), channel_id=1, source_target_pairs={{0,7},{1,0},{2,1},{3,2},{4,3},{5,4},{6,5},{7,6},{8,15},{9,8},{10,9... | collective-permute-start | bytes 294920 | tf_op jit(solution)/shard_map/ppermute | solution.py:470
  76.2 12.8 %collective-permute-start.12 = (bf16[192,256]{1,0:T(8,128)(2,1)S(1)}, bf16[192,256]{1,0:T(8,128)(2,1)S(1)}, u32[]{:S(2)}, u32[]{:S(2)}) collective-permute-start(bf16[192,256]{1,0:T(8,128)(2,1)S(1)} %get-tuple-element.37), channel_id=1, source_target_pairs={{0,2},{1,3},{2,4},{3,5},{4,6},{5,7},{6,0},{7,1},{8,10},{9,11},{10,... | collective-permute-start | bytes 294920 | tf_op jit(solution)/shard_map/ppermute | solution.py:470
  76.2 12.8 %collective-permute-start.13 = (bf16[192,256]{1,0:T(8,128)(2,1)S(1)}, bf16[192,256]{1,0:T(8,128)(2,1)S(1)}, u32[]{:S(2)}, u32[]{:S(2)}) collective-permute-start(bf16[192,256]{1,0:T(8,128)(2,1)S(1)} %get-tuple-element.38), channel_id=1, source_target_pairs={{0,6},{1,7},{2,0},{3,1},{4,2},{5,3},{6,4},{7,5},{8,14},{9,15},{10,... | collective-permute-start | bytes 294920 | tf_op jit(solution)/shard_map/ppermute | solution.py:470
  80.4 11.7 %collective-permute-start.14 = (bf16[192,256]{1,0:T(8,128)(2,1)S(1)}, bf16[192,256]{1,0:T(8,128)(2,1)S(1)}, u32[]{:S(2)}, u32[]{:S(2)}) collective-permute-start(bf16[192,256]{1,0:T(8,128)(2,1)S(1)} %get-tuple-element.39), channel_id=1, source_target_pairs={{0,3},{1,4},{2,5},{3,6},{4,7},{5,0},{6,1},{7,2},{8,11},{9,12},{10,... | collective-permute-start | bytes 294920 | tf_op jit(solution)/shard_map/ppermute | solution.py:470
  80.4 14.4 %collective-permute-start.15 = (bf16[192,256]{1,0:T(8,128)(2,1)S(1)}, bf16[192,256]{1,0:T(8,128)(2,1)S(1)}, u32[]{:S(2)}, u32[]{:S(2)}) collective-permute-start(bf16[192,256]{1,0:T(8,128)(2,1)S(1)} %get-tuple-element.40), channel_id=1, source_target_pairs={{0,5},{1,6},{2,7},{3,0},{4,1},{5,2},{6,3},{7,4},{8,13},{9,14},{10,... | collective-permute-start | bytes 294920 | tf_op jit(solution)/shard_map/ppermute | solution.py:470
  85.4 9.3 %collective-permute-start.16 = (bf16[192,256]{1,0:T(8,128)(2,1)S(1)}, bf16[192,256]{1,0:T(8,128)(2,1)S(1)}, u32[]{:S(2)}, u32[]{:S(2)}) collective-permute-start(bf16[192,256]{1,0:T(8,128)(2,1)S(1)} %get-tuple-element.41), channel_id=1, source_target_pairs={{0,4},{1,5},{2,6},{3,7},{4,0},{5,1},{6,2},{7,3},{8,12},{9,13},{10,... | collective-permute-start | bytes 294920 | tf_op jit(solution)/shard_map/ppermute | solution.py:470
  123.0 24.6 %all-to-all-start.4 = ((bf16[8,128,384]{2,1,0:T(8,128)(2,1)}), bf16[8,128,384]{2,1,0:T(8,128)(2,1)S(1)}, u32[]{:S(2)}, u32[]{:S(2)}) async-start(bf16[8,128,384]{2,1,0:T(8,128)(2,1)} %shard_map.146), calls=%async_computation.4 | async-start | bytes 1572864 | tf_op jit(solution)/shard_map/all_to_all | solution.py:498
  (8 other events, 85.7 us)

commit v6 on v5

--- a/solution.py
+++ b/solution.py
@@ -361,7 +361,7 @@
     core = lax.rem(lax.axis_index("tok"), 2).astype(jnp.int32).reshape(1)
     pairs = [(i, i ^ 1) for i in range(n_tok)]
     chips = [[2 * i + c for i in range(16)] for c in range(2)]
-    order = (1, 7, 2, 6, 3, 5, 4)
+    order = (4, 3, 5, 2, 6, 1, 7)
     ring = [[(i, (i + d) % n_mlp) for i in range(n_mlp)] for d in range(n_mlp)]
     vmem = pl.BlockSpec(memory_space=pltpu.VMEM)
     hbm = pl.BlockSpec(memory_space=pltpu.HBM)

time: 149 us -> 146 us (0.980)
  waiting for transfers between devices: 27.7 us -> 31.4 us
  blocking collectives: 49.1 us -> 45.8 us
  starting transfers between devices: 45 us -> 41.8 us
    ppermute x7, waiting for transfers between devices: 5.72 us -> 10.4 us  [body(): lax.ppermute(shares[d], 'mlp', ring[d])]
    all_to_all x1, blocking collectives: 23.6 us -> 20.3 us  [body(): wide = lax.all_to_all(scaled, 'mlp', 0, 0, tiled=True)]
    ppermute x7, starting transfers between devices: 16.1 us -> 12.9 us  [body(): lax.ppermute(shares[d], 'mlp', ring[d])]
  transfers between devices with their start and end apart: 19 -> 19, of which waited for: 9 -> 11; matrix products, arithmetic and copies ran while one was open for 0% -> 0% of each run, Pallas kernels for 10% -> 11%
where the time goes in v6:
time: 146 us
  blocking collectives  45.8 us (31%)
  starting transfers between devices  41.8 us (29%)
  waiting for transfers between devices  31.4 us (22%)
  Pallas kernels  25.2 us (17%)
    all_to_all x1, blocking collectives, body(): wide = lax.all_to_all(scaled, 'mlp', 0, 0, tiled=True)  20.3 us
    all_to_all x1, blocking collectives, body(): lax.all_to_all(qkv, 'tok', 0, 0, tiled=True, axis_index_groups=chips)  14.4 us
    ppermute x7, starting transfers between devices, body(): lax.ppermute(shares[d], 'mlp', ring[d])  12.9 us
    pallas_call x1, Pallas kernels, body(): pl.pallas_call(normal_kernel, grid=(1,), in_specs=[whole(8, 64, 256)], ou...  12.6 us
    all_to_all x1, blocking collectives, body(): lax.all_to_all(attended.reshape(32, 16, 128), 'tok', 0, 0, tiled=True)  11.1 us
    ppermute x7, waiting for transfers between devices, body(): lax.ppermute(shares[d], 'mlp', ring[d])  10.4 us
    ppermute x3, starting transfers between devices, gathered(): mine = [lax.ppermute(near, ('tok', 'mlp'), shifted(k)) for k in (1, 2, 3)]  9.3 us
    ppermute x3, waiting for transfers between devices, gathered(): mine = [lax.ppermute(near, ('tok', 'mlp'), shifted(k)) for k in (1, 2, 3)]  8.2 us
  transfers between devices with their start and end apart: 19, of which 11 were waited for; matrix products, arithmetic and copies ran while one was open for 0% of the time, Pallas kernels for 11%

profile of v6, /device:TPU:2, one launch (start us, length us, event | category | flops | bytes accessed | tf_op | source)
XLA Modules:
  0.0 145.8 jit_solution(17125088868930561933)
XLA Ops:
  2.2 2.8 %shard_map.140 = (bf16[32,272,128]{2,1,0:T(8,128)(2,1)}, bf16[416,256]{1,0:T(8,128)(2,1)}, bf16[208,256]{1,0:T(8,128)(2,1)}) custom-call(s32[1]{0:T(128)} %bitcast.1.core, bf16[64,768]{1,0:T(8,128)(2,1)} %refs_0_.1, bf16[64,256]{1,0:T(8,128)(2,1)} %bitcast.18, s32[1,32,64]{2,1,0:T(8,128)} %refs_2_.1, s32[1,32,64]{2,1,0:T(8,128)} %refs_3_.1, ...), custom_call_target="tpu_custom_call" | custom-call | tf_op jit(solution)/shard_map/pallas_call | solution.py:372
  5.0 7.8 %all-to-all-start = ((bf16[32,272,128]{2,1,0:T(8,128)(2,1)}), bf16[32,272,128]{2,1,0:T(8,128)(2,1)S(1)}, u32[]{:S(2)}, u32[]{:S(2)}) async-start(bf16[32,272,128]{2,1,0:T(8,128)(2,1)} %get-tuple-element.28), calls=%async_computation | async-start | bytes 4456448 | tf_op jit(solution)/shard_map/all_to_all | solution.py:421
  12.8 4.7 %collective-permute-start.5 = (bf16[416,256]{1,0:T(8,128)(2,1)S(1)}, bf16[416,256]{1,0:T(8,128)(2,1)S(1)}, u32[]{:S(2)}, u32[]{:S(2)}) collective-permute-start(bf16[416,256]{1,0:T(8,128)(2,1)S(1)} %copy-done.6), channel_id=1, source_target_pairs={{0,3},{1,4},{2,5},{3,6},{4,7},{5,0},{6,1},{7,2},{8,13},{9,14},{10,... | collective-permute-start | bytes 638984 | tf_op jit(solution)/shard_map/ppermute | solution.py:416
  17.5 3.6 %collective-permute-start.4 = (bf16[416,256]{1,0:T(8,128)(2,1)S(1)}, bf16[416,256]{1,0:T(8,128)(2,1)S(1)}, u32[]{:S(2)}, u32[]{:S(2)}) collective-permute-start(bf16[416,256]{1,0:T(8,128)(2,1)S(1)} %copy-done.6), channel_id=1, source_target_pairs={{0,2},{1,3},{2,4},{3,5},{4,6},{5,7},{6,0},{7,1},{8,14},{9,15},{10,... | collective-permute-start | bytes 638984 | tf_op jit(solution)/shard_map/ppermute | solution.py:416
  23.6 5.5 %collective-permute-start.8 = (bf16[416,256]{1,0:T(8,128)(2,1)S(1)}, bf16[416,256]{1,0:T(8,128)(2,1)S(1)}, u32[]{:S(2)}, u32[]{:S(2)}) collective-permute-start(bf16[416,256]{1,0:T(8,128)(2,1)S(1)} %collective-permute-done.5.refs_5_), channel_id=1, source_target_pairs={{0,8},{8,0},{16,24},{24,16},{32,40},{40,32},{48,56},{56,48},{64,72... | collective-permute-start | bytes 638984 | tf_op jit(solution)/shard_map/ppermute | solution.py:418
  29.1 5.3 %collective-permute-done.4.refs_4_ = bf16[416,256]{1,0:T(8,128)(2,1)S(1)} collective-permute-done((bf16[416,256]{1,0:T(8,128)(2,1)S(1)}, bf16[416,256]{1,0:T(8,128)(2,1)S(1)}, u32[]{:S(2)}, u32[]{:S(2)}) %collective-permute-start.4) | collective-permute-done | bytes 213024 | tf_op jit(solution)/shard_map/ppermute | solution.py:416
  34.4 1.9 %collective-permute-done.3.refs_3_ = bf16[416,256]{1,0:T(8,128)(2,1)S(1)} collective-permute-done((bf16[416,256]{1,0:T(8,128)(2,1)S(1)}, bf16[416,256]{1,0:T(8,128)(2,1)S(1)}, u32[]{:S(2)}, u32[]{:S(2)}) %collective-permute-start.3) | collective-permute-done | bytes 213024 | tf_op jit(solution)/shard_map/ppermute | solution.py:416
  36.3 1.9 %collective-permute-start.6 = (bf16[416,256]{1,0:T(8,128)(2,1)S(1)}, bf16[416,256]{1,0:T(8,128)(2,1)S(1)}, u32[]{:S(2)}, u32[]{:S(2)}) collective-permute-start(bf16[416,256]{1,0:T(8,128)(2,1)S(1)} %collective-permute-done.3.refs_3_), channel_id=1, source_target_pairs={{0,8},{8,0},{16,24},{24,16},{32,40},{40,32},{48,56},{56,48},{64,72... | collective-permute-start | bytes 638984 | tf_op jit(solution)/shard_map/ppermute | solution.py:418
  38.2 2.4 %collective-permute-done.1.refs_1_ = bf16[208,256]{1,0:T(8,128)(2,1)S(1)} collective-permute-done((bf16[208,256]{1,0:T(8,128)(2,1)}, bf16[208,256]{1,0:T(8,128)(2,1)S(1)}, u32[]{:S(2)}, u32[]{:S(2)}) %collective-permute-start.1) | collective-permute-done | bytes 106528 | tf_op jit(solution)/shard_map/ppermute | solution.py:417
  42.9 1.9 %shard_map.141.normed = bf16[8,256,256]{2,1,0:T(8,128)(2,1)S(1)} custom-call(s32[1]{0:T(128)} %bitcast.me, s32[1]{0:T(128)} %bitcast.1.core, bf16[416,256]{1,0:T(8,128)(2,1)} %get-tuple-element.26.refs_0_, bf16[208,256]{1,0:T(8,128)(2,1)} %copy-done.12, bf16[208,256]{1,0:T(8,128)(2,1)} %collective-permute-done.2.refs_2_, bf16[416,256]{1,0:T(8,128)(2,1)} %copy-done.9, ...), custom_call_target="tpu_custom_call" | custom-call | tf_op jit(solution)/shard_map/pallas_call | solution.py:424
  46.0 14.4 %all_to_all.25.got = bf16[16,48,128]{2,1,0:T(8,128)(2,1)S(1)} all-to-all(bf16[16,48,128]{2,1,0:T(8,128)(2,1)S(1)} %get-tuple-element.29), channel_id=1, replica_groups={{0,16,32,48,64,80,96,112,128,144,160,176,192,208,224,240},{8,24,40,56,7..., dimensions={0} | all-to-all | bytes 393216 | tf_op jit(solution)/shard_map/all_to_all | solution.py:441
  61.3 11.1 %all_to_all.26 = bf16[32,16,128]{2,1,0:T(8,128)(2,1)S(1)} all-to-all(bf16[32,16,128]{2,1,0:T(8,128)(2,1)S(1)} %bitcast.10), channel_id=1, replica_groups=mesh['tok'=32,'mlp'=8] {'tok'}, dimensions={0} | all-to-all | bytes 262144 | tf_op jit(solution)/shard_map/all_to_all | solution.py:451
  72.9 3.7 %collective-permute-start.10 = (bf16[192,256]{1,0:T(8,128)(2,1)S(1)}, bf16[192,256]{1,0:T(8,128)(2,1)S(1)}, u32[]{:S(2)}, u32[]{:S(2)}) collective-permute-start(bf16[192,256]{1,0:T(8,128)(2,1)S(1)} %get-tuple-element.35), channel_id=1, source_target_pairs={{0,4},{1,5},{2,6},{3,7},{4,0},{5,1},{6,2},{7,3},{8,12},{9,13},{10,... | collective-permute-start | bytes 294920 | tf_op jit(solution)/shard_map/ppermute | solution.py:470
  77.4 4.2 %collective-permute-start.12 = (bf16[192,256]{1,0:T(8,128)(2,1)S(1)}, bf16[192,256]{1,0:T(8,128)(2,1)S(1)}, u32[]{:S(2)}, u32[]{:S(2)}) collective-permute-start(bf16[192,256]{1,0:T(8,128)(2,1)S(1)} %get-tuple-element.37), channel_id=1, source_target_pairs={{0,5},{1,6},{2,7},{3,0},{4,1},{5,2},{6,3},{7,4},{8,13},{9,14},{10,... | collective-permute-start | bytes 294920 | tf_op jit(solution)/shard_map/ppermute | solution.py:470
  81.7 1.6 %collective-permute-start.13 = (bf16[192,256]{1,0:T(8,128)(2,1)S(1)}, bf16[192,256]{1,0:T(8,128)(2,1)S(1)}, u32[]{:S(2)}, u32[]{:S(2)}) collective-permute-start(bf16[192,256]{1,0:T(8,128)(2,1)S(1)} %get-tuple-element.38), channel_id=1, source_target_pairs={{0,2},{1,3},{2,4},{3,5},{4,6},{5,7},{6,0},{7,1},{8,10},{9,11},{10,... | collective-permute-start | bytes 294920 | tf_op jit(solution)/shard_map/ppermute | solution.py:470
  83.3 2.5 %collective-permute-start.14 = (bf16[192,256]{1,0:T(8,128)(2,1)S(1)}, bf16[192,256]{1,0:T(8,128)(2,1)S(1)}, u32[]{:S(2)}, u32[]{:S(2)}) collective-permute-start(bf16[192,256]{1,0:T(8,128)(2,1)S(1)} %get-tuple-element.39), channel_id=1, source_target_pairs={{0,6},{1,7},{2,0},{3,1},{4,2},{5,3},{6,4},{7,5},{8,14},{9,15},{10,... | collective-permute-start | bytes 294920 | tf_op jit(solution)/shard_map/ppermute | solution.py:470
  85.8 5.8 %collective-permute-done.11.refs_2_ = bf16[192,256]{1,0:T(8,128)(2,1)S(1)} collective-permute-done((bf16[192,256]{1,0:T(8,128)(2,1)S(1)}, bf16[192,256]{1,0:T(8,128)(2,1)S(1)}, u32[]{:S(2)}, u32[]{:S(2)}) %collective-permute-start.11) | collective-permute-done | bytes 98336 | tf_op jit(solution)/shard_map/ppermute | solution.py:470
  91.6 1.9 %collective-permute-done.14.refs_5_ = bf16[192,256]{1,0:T(8,128)(2,1)S(1)} collective-permute-done((bf16[192,256]{1,0:T(8,128)(2,1)S(1)}, bf16[192,256]{1,0:T(8,128)(2,1)S(1)}, u32[]{:S(2)}, u32[]{:S(2)}) %collective-permute-start.14) | collective-permute-done | bytes 98336 | tf_op jit(solution)/shard_map/ppermute | solution.py:470
  94.4 1.8 %collective-permute-done.16.refs_7_ = bf16[192,256]{1,0:T(8,128)(2,1)S(1)} collective-permute-done((bf16[192,256]{1,0:T(8,128)(2,1)S(1)}, bf16[192,256]{1,0:T(8,128)(2,1)S(1)}, u32[]{:S(2)}, u32[]{:S(2)}) %collective-permute-start.16) | collective-permute-done | bytes 98336 | tf_op jit(solution)/shard_map/ppermute | solution.py:470
  96.3 20.3 %all_to_all.27.got = bf16[8,128,256]{2,1,0:T(8,128)(2,1)S(1)} all-to-all(bf16[8,128,256]{2,1,0:T(8,128)(2,1)S(1)} %get-tuple-element.42), channel_id=1, replica_groups=mesh['tok'=32,'mlp'=8] {'mlp'}, dimensions={0} | all-to-all | bytes 1048576 | tf_op jit(solution)/shard_map/all_to_all | solution.py:477
  116.6 4.5 %shard_map.146 = bf16[8,128,384]{2,1,0:T(8,128)(2,1)} custom-call(s32[1]{0:T(128)} %bitcast.me, s32[1]{0:T(128)} %bitcast.1.core, bf16[8,128,256]{2,1,0:T(8,128)(2,1)S(1)} %all_to_all.27.got, bf16[416,256]{1,0:T(8,128)(2,1)} %get-tuple-element.26.refs_0_, bf16[208,256]{1,0:T(8,128)(2,1)} %copy-done.12, bf16[208,256]{1,0:T(8,128)(2,1)} %collective-permute-done.2.refs_2_, ...), custom_call_target="tpu_custom_call" | custom-call | tf_op jit(solution)/shard_map/pallas_call | solution.py:479
  121.1 3.6 %all-to-all-start.4 = ((bf16[8,128,384]{2,1,0:T(8,128)(2,1)}), bf16[8,128,384]{2,1,0:T(8,128)(2,1)S(1)}, u32[]{:S(2)}, u32[]{:S(2)}) async-start(bf16[8,128,384]{2,1,0:T(8,128)(2,1)} %shard_map.146), calls=%async_computation.4 | async-start | bytes 1572864 | tf_op jit(solution)/shard_map/all_to_all | solution.py:498
  124.7 12.6 %shard_map.147.normal = f32[128,768]{1,0:T(8,128)S(1)} custom-call(bf16[8,64,256]{2,1,0:T(8,128)(2,1)S(1)} %get-tuple-element.45.slots), custom_call_target="tpu_custom_call" | custom-call | flops 4000000000 | bytes 1000000 | tf_op jit(solution)/shard_map/pallas_call | solution.py:501
  137.3 7.5 %all-to-all-done.4.got = bf16[8,128,384]{2,1,0:T(8,128)(2,1)S(1)} async-done(((bf16[8,128,384]{2,1,0:T(8,128)(2,1)}), bf16[8,128,384]{2,1,0:T(8,128)(2,1)S(1)}, u32[]{:S(2)}, u32[]{:S(2)}) %all-to-all-start.4) | async-done | bytes 786464 | tf_op jit(solution)/shard_map/all_to_all | solution.py:498
  (53 shorter events, 11.7 us)
Async XLA Ops:
  0.6 1.6 %collective-permute-start = (bf16[128,256]{1,0:T(8,128)(2,1)}, bf16[128,256]{1,0:T(8,128)(2,1)S(1)}, u32[]{:S(2)}, u32[]{:S(2)}) collective-permute-start(bf16[128,256]{1,0:T(8,128)(2,1)} %bitcast.12), channel_id=1, source_target_pairs={{0,8},{8,0},{16,24},{24,16},{32,40},{40,32},{48,56},{56,48},{64,72... | collective-permute-start | bytes 196616 | tf_op jit(solution)/shard_map/ppermute | solution.py:371
  5.0 39.8 %all-to-all-start = ((bf16[32,272,128]{2,1,0:T(8,128)(2,1)}), bf16[32,272,128]{2,1,0:T(8,128)(2,1)S(1)}, u32[]{:S(2)}, u32[]{:S(2)}) async-start(bf16[32,272,128]{2,1,0:T(8,128)(2,1)} %get-tuple-element.28), calls=%async_computation | async-start | bytes 4456448 | tf_op jit(solution)/shard_map/all_to_all | solution.py:421
  12.8 10.9 %collective-permute-start.5 = (bf16[416,256]{1,0:T(8,128)(2,1)S(1)}, bf16[416,256]{1,0:T(8,128)(2,1)S(1)}, u32[]{:S(2)}, u32[]{:S(2)}) collective-permute-start(bf16[416,256]{1,0:T(8,128)(2,1)S(1)} %copy-done.6), channel_id=1, source_target_pairs={{0,3},{1,4},{2,5},{3,6},{4,7},{5,0},{6,1},{7,2},{8,13},{9,14},{10,... | collective-permute-start | bytes 638984 | tf_op jit(solution)/shard_map/ppermute | solution.py:416
  17.5 17.0 %collective-permute-start.4 = (bf16[416,256]{1,0:T(8,128)(2,1)S(1)}, bf16[416,256]{1,0:T(8,128)(2,1)S(1)}, u32[]{:S(2)}, u32[]{:S(2)}) collective-permute-start(bf16[416,256]{1,0:T(8,128)(2,1)S(1)} %copy-done.6), channel_id=1, source_target_pairs={{0,2},{1,3},{2,4},{3,5},{4,6},{5,7},{6,0},{7,1},{8,14},{9,15},{10,... | collective-permute-start | bytes 638984 | tf_op jit(solution)/shard_map/ppermute | solution.py:416
  21.0 15.3 %collective-permute-start.3 = (bf16[416,256]{1,0:T(8,128)(2,1)S(1)}, bf16[416,256]{1,0:T(8,128)(2,1)S(1)}, u32[]{:S(2)}, u32[]{:S(2)}) collective-permute-start(bf16[416,256]{1,0:T(8,128)(2,1)S(1)} %copy-done.6), channel_id=1, source_target_pairs={{0,1},{1,2},{2,3},{3,4},{4,5},{5,6},{6,7},{7,0},{8,15},{9,8},{10,9... | collective-permute-start | bytes 638984 | tf_op jit(solution)/shard_map/ppermute | solution.py:416
  22.1 18.6 %collective-permute-start.1 = (bf16[208,256]{1,0:T(8,128)(2,1)}, bf16[208,256]{1,0:T(8,128)(2,1)S(1)}, u32[]{:S(2)}, u32[]{:S(2)}) collective-permute-start(bf16[208,256]{1,0:T(8,128)(2,1)} %get-tuple-element.27), channel_id=1, source_target_pairs={{0,4},{1,5},{2,6},{3,7},{4,0},{5,1},{6,2},{7,3},{8,12},{9,13},{10,... | collective-permute-start | bytes 319496 | tf_op jit(solution)/shard_map/ppermute | solution.py:417
  23.6 18.5 %collective-permute-start.8 = (bf16[416,256]{1,0:T(8,128)(2,1)S(1)}, bf16[416,256]{1,0:T(8,128)(2,1)S(1)}, u32[]{:S(2)}, u32[]{:S(2)}) collective-permute-start(bf16[416,256]{1,0:T(8,128)(2,1)S(1)} %collective-permute-done.5.refs_5_), channel_id=1, source_target_pairs={{0,8},{8,0},{16,24},{24,16},{32,40},{40,32},{48,56},{56,48},{64,72... | collective-permute-start | bytes 638984 | tf_op jit(solution)/shard_map/ppermute | solution.py:418
  34.4 7.7 %collective-permute-start.7 = (bf16[416,256]{1,0:T(8,128)(2,1)S(1)}, bf16[416,256]{1,0:T(8,128)(2,1)}, u32[]{:S(2)}, u32[]{:S(2)}) collective-permute-start(bf16[416,256]{1,0:T(8,128)(2,1)S(1)} %collective-permute-done.4.refs_4_), channel_id=1, source_target_pairs={{0,8},{8,0},{16,24},{24,16},{32,40},{40,32},{48,56},{56,48},{64,72... | collective-permute-start | bytes 638984 | tf_op jit(solution)/shard_map/ppermute | solution.py:418
  36.3 5.8 %collective-permute-start.6 = (bf16[416,256]{1,0:T(8,128)(2,1)S(1)}, bf16[416,256]{1,0:T(8,128)(2,1)S(1)}, u32[]{:S(2)}, u32[]{:S(2)}) collective-permute-start(bf16[416,256]{1,0:T(8,128)(2,1)S(1)} %collective-permute-done.3.refs_3_), channel_id=1, source_target_pairs={{0,8},{8,0},{16,24},{24,16},{32,40},{40,32},{48,56},{56,48},{64,72... | collective-permute-start | bytes 638984 | tf_op jit(solution)/shard_map/ppermute | solution.py:418
  40.7 1.4 collective-permute-start.2
  44.8 51.4 %copy-start.3 = (bf16[8,16,256]{2,1,0:T(8,128)(2,1)S(1)}, bf16[8,16,256]{2,1,0:T(8,128)(2,1)}, u32[]{:S(2)}) copy-start(bf16[8,16,256]{2,1,0:T(8,128)(2,1)} %param.13) | copy-start | bytes 196612
  44.8 51.4 %copy-start.5 = (f32[256]{0:T(256)S(1)}, f32[256]{0:T(256)}, u32[]{:S(2)}) copy-start(f32[256]{0:T(256)} %param.20) | copy-start | bytes 3076
  44.8 71.8 %copy-start.1 = (bf16[1024,2048]{1,0:T(8,128)(2,1)S(1)}, bf16[1024,2048]{1,0:T(8,128)(2,1)}, u32[]{:S(2)}) copy-start(bf16[1024,2048]{1,0:T(8,128)(2,1)} %refs_10_.1) | copy-start | bytes 12582916
  45.6 71.0 %copy-start = (bf16[2048,1024]{1,0:T(8,128)(2,1)S(1)}, bf16[2048,1024]{1,0:T(8,128)(2,1)}, u32[]{:S(2)}) copy-start(bf16[2048,1024]{1,0:T(8,128)(2,1)} %refs_9_.1) | copy-start | bytes 12582916
  45.6 71.0 %copy-start.2 = (bf16[256,128]{1,0:T(8,128)(2,1)S(1)}, bf16[256,128]{1,0:T(8,128)(2,1)}, u32[]{:S(2)}) copy-start(bf16[256,128]{1,0:T(8,128)(2,1)} %own_dec.1) | copy-start | bytes 196612
  45.7 26.7 %collective-permute-start.9 = (bf16[32,64,128]{2,1,0:T(8,128)(2,1)S(1)}, bf16[32,64,128]{2,1,0:T(8,128)(2,1)S(1)}, u32[]{:S(2)}, u32[]{:S(2)}) collective-permute-start(bf16[32,64,128]{2,1,0:T(8,128)(2,1)S(1)} %slice.3), channel_id=1, source_target_pairs={{0,8},{8,0},{16,24},{24,16},{32,40},{40,32},{48,56},{56,48},{64,72... | collective-permute-start | bytes 1572872 | tf_op jit(solution)/shard_map/ppermute | solution.py:443
  72.9 12.9 %collective-permute-start.10 = (bf16[192,256]{1,0:T(8,128)(2,1)S(1)}, bf16[192,256]{1,0:T(8,128)(2,1)S(1)}, u32[]{:S(2)}, u32[]{:S(2)}) collective-permute-start(bf16[192,256]{1,0:T(8,128)(2,1)S(1)} %get-tuple-element.35), channel_id=1, source_target_pairs={{0,4},{1,5},{2,6},{3,7},{4,0},{5,1},{6,2},{7,3},{8,12},{9,13},{10,... | collective-permute-start | bytes 294920 | tf_op jit(solution)/shard_map/ppermute | solution.py:470
  76.6 15.0 %collective-permute-start.11 = (bf16[192,256]{1,0:T(8,128)(2,1)S(1)}, bf16[192,256]{1,0:T(8,128)(2,1)S(1)}, u32[]{:S(2)}, u32[]{:S(2)}) collective-permute-start(bf16[192,256]{1,0:T(8,128)(2,1)S(1)} %get-tuple-element.36), channel_id=1, source_target_pairs={{0,3},{1,4},{2,5},{3,6},{4,7},{5,0},{6,1},{7,2},{8,11},{9,12},{10,... | collective-permute-start | bytes 294920 | tf_op jit(solution)/shard_map/ppermute | solution.py:470
  77.4 14.2 %collective-permute-start.12 = (bf16[192,256]{1,0:T(8,128)(2,1)S(1)}, bf16[192,256]{1,0:T(8,128)(2,1)S(1)}, u32[]{:S(2)}, u32[]{:S(2)}) collective-permute-start(bf16[192,256]{1,0:T(8,128)(2,1)S(1)} %get-tuple-element.37), channel_id=1, source_target_pairs={{0,5},{1,6},{2,7},{3,0},{4,1},{5,2},{6,3},{7,4},{8,13},{9,14},{10,... | collective-permute-start | bytes 294920 | tf_op jit(solution)/shard_map/ppermute | solution.py:470
  81.7 9.9 %collective-permute-start.13 = (bf16[192,256]{1,0:T(8,128)(2,1)S(1)}, bf16[192,256]{1,0:T(8,128)(2,1)S(1)}, u32[]{:S(2)}, u32[]{:S(2)}) collective-permute-start(bf16[192,256]{1,0:T(8,128)(2,1)S(1)} %get-tuple-element.38), channel_id=1, source_target_pairs={{0,2},{1,3},{2,4},{3,5},{4,6},{5,7},{6,0},{7,1},{8,10},{9,11},{10,... | collective-permute-start | bytes 294920 | tf_op jit(solution)/shard_map/ppermute | solution.py:470
  83.3 10.2 %collective-permute-start.14 = (bf16[192,256]{1,0:T(8,128)(2,1)S(1)}, bf16[192,256]{1,0:T(8,128)(2,1)S(1)}, u32[]{:S(2)}, u32[]{:S(2)}) collective-permute-start(bf16[192,256]{1,0:T(8,128)(2,1)S(1)} %get-tuple-element.39), channel_id=1, source_target_pairs={{0,6},{1,7},{2,0},{3,1},{4,2},{5,3},{6,4},{7,5},{8,14},{9,15},{10,... | collective-permute-start | bytes 294920 | tf_op jit(solution)/shard_map/ppermute | solution.py:470
  85.8 8.6 %collective-permute-start.15 = (bf16[192,256]{1,0:T(8,128)(2,1)S(1)}, bf16[192,256]{1,0:T(8,128)(2,1)S(1)}, u32[]{:S(2)}, u32[]{:S(2)}) collective-permute-start(bf16[192,256]{1,0:T(8,128)(2,1)S(1)} %get-tuple-element.40), channel_id=1, source_target_pairs={{0,1},{1,2},{2,3},{3,4},{4,5},{5,6},{6,7},{7,0},{8,9},{9,10},{10,1... | collective-permute-start | bytes 294920 | tf_op jit(solution)/shard_map/ppermute | solution.py:470
  91.6 4.6 %collective-permute-start.16 = (bf16[192,256]{1,0:T(8,128)(2,1)S(1)}, bf16[192,256]{1,0:T(8,128)(2,1)S(1)}, u32[]{:S(2)}, u32[]{:S(2)}) collective-permute-start(bf16[192,256]{1,0:T(8,128)(2,1)S(1)} %get-tuple-element.41), channel_id=1, source_target_pairs={{0,7},{1,0},{2,1},{3,2},{4,3},{5,4},{6,5},{7,6},{8,15},{9,8},{10,9... | collective-permute-start | bytes 294920 | tf_op jit(solution)/shard_map/ppermute | solution.py:470
  121.1 23.6 %all-to-all-start.4 = ((bf16[8,128,384]{2,1,0:T(8,128)(2,1)}), bf16[8,128,384]{2,1,0:T(8,128)(2,1)S(1)}, u32[]{:S(2)}, u32[]{:S(2)}) async-start(bf16[8,128,384]{2,1,0:T(8,128)(2,1)} %shard_map.146), calls=%async_computation.4 | async-start | bytes 1572864 | tf_op jit(solution)/shard_map/all_to_all | solution.py:498
  (8 other events, 85.7 us)

commit v7 on v6

--- a/solution.py
+++ b/solution.py
@@ -267,14 +267,15 @@
         total += got[d][0:128, :].astype(F32)
         slots[d] = got[d][128:192, :]
     resid[...] = total
-    out = (total * gain[...]).astype(BF)
-    for k in range(8):
-        scaled[k] = out
-
-
-def ffn_kernel(me, core, got, *refs):
+    scaled[...] = (total * gain[...]).astype(BF)
+
+
+def ffn_kernel(me, core, *refs):
+    blocks, refs = refs[:8], refs[8:]
     own, far, far_sib, mine, theirs = refs[0], refs[1], refs[2], refs[3:6], refs[6:9]
-    up, down, resid, own_dec, out, shared, sem = refs[9:]
+    up, down, resid, own_dec, out, shared, got, sem = refs[9:]
+    for d in range(8):
+        got[lax.rem(me[0] - d + 8, 8)] = blocks[d][...]
     near, across, opposite = groups_of(me, core)
     common = pl.ds(256, 160)
     pairs = [(own.at[common, :], shared.at[me[0]])]
@@ -471,24 +472,26 @@
 
     resid, scaled, slots_in = pl.pallas_call(
         resid_kernel,
-        out_shape=(sds((128, 256), F32), sds((8, 128, 256)), sds((8, 64, 256))),
+        out_shape=(sds((128, 256), F32), sds((128, 256)), sds((8, 64, 256))),
         compiler_params=params(8),
     )(x, gain_mlp.reshape(1, 256), *shares_in)
-    wide = lax.all_to_all(scaled, "mlp", 0, 0, tiled=True)
+    wide = {d: lax.ppermute(scaled, "mlp", ring[d]) for d in order}
+    wide[0] = scaled
 
     down_out = pl.pallas_call(
         ffn_kernel,
-        in_specs=[smem] * 2 + [vmem] + [hbm] * 9 + [vmem] * 4,
+        in_specs=[smem] * 2 + [vmem] * 8 + [hbm] * 9 + [vmem] * 4,
         out_shape=sds((8, 128, 384)),
         scratch_shapes=[
             pltpu.VMEM((8, 160, 256), BF),
+            pltpu.VMEM((8, 128, 256), BF),
             pltpu.SemaphoreType.DMA((9,)),
         ],
         compiler_params=params(8),
     )(
         me,
         core,
-        wide,
+        *[wide[d] for d in range(8)],
         *map(stay, packs),
         w_up,
         w_down,

time: 146 us -> 152 us (1.041); the launches traced: 146 us -> 150 us
  blocking collectives: 45.8 us -> 25.5 us
  starting transfers between devices: 41.8 us -> 55.3 us
  waiting for transfers between devices: 31.4 us -> 42.1 us
    all_to_all x1 -> x0, blocking collectives: 20.3 us -> none  [body(): wide = lax.all_to_all(scaled, 'mlp', 0, 0, tiled=True)]
    ppermute x0 -> x7, starting transfers between devices: none -> 12.7 us  [body(): wide = {d: lax.ppermute(scaled, 'mlp', ring[d]) for d in order}]
    ppermute x0 -> x7, waiting for transfers between devices: none -> 8.17 us  [body(): wide = {d: lax.ppermute(scaled, 'mlp', ring[d]) for d in order}]
    all_to_all x1, waiting for transfers between devices: 7.45 us -> 9.97 us  [body(): down_in = lax.all_to_all(down_out, 'mlp', 0, 0, tiled=True)]
  transfers between devices with their start and end apart: 19 -> 26, of which waited for: 11 -> 15; matrix products, arithmetic and copies ran while one was open for 0% -> 0% of each run, Pallas kernels for 11% -> 10%
where the time goes in v7:
time: 152 us; the launch traced here: 150 us
  starting transfers between devices  55.3 us (36%)
  waiting for transfers between devices  42.1 us (28%)
  blocking collectives  25.5 us (17%)
  Pallas kernels  25.2 us (17%)
    all_to_all x1, blocking collectives, body(): lax.all_to_all(qkv, 'tok', 0, 0, tiled=True, axis_index_groups=chips)  14.4 us
    ppermute x7, starting transfers between devices, body(): lax.ppermute(shares[d], 'mlp', ring[d])  12.9 us
    ppermute x7, starting transfers between devices, body(): wide = {d: lax.ppermute(scaled, 'mlp', ring[d]) for d in order}  12.7 us
    pallas_call x1, Pallas kernels, body(): pl.pallas_call(normal_kernel, grid=(1,), in_specs=[whole(8, 64, 256)], ou...  12.6 us
    all_to_all x1, blocking collectives, body(): lax.all_to_all(attended.reshape(32, 16, 128), 'tok', 0, 0, tiled=True)  11.1 us
    ppermute x7, waiting for transfers between devices, body(): lax.ppermute(shares[d], 'mlp', ring[d])  10.4 us
    all_to_all x1, waiting for transfers between devices, body(): down_in = lax.all_to_all(down_out, 'mlp', 0, 0, tiled=True)  9.97 us
    ppermute x3, starting transfers between devices, gathered(): mine = [lax.ppermute(near, ('tok', 'mlp'), shifted(k)) for k in (1, 2, 3)]  9.3 us
  transfers between devices with their start and end apart: 26, of which 15 were waited for; matrix products, arithmetic and copies ran while one was open for 0% of the time, Pallas kernels for 10%

profile of v7, /device:TPU:2, one launch (start us, length us, event | category | flops | bytes accessed | tf_op | source)
XLA Modules:
  0.0 149.8 jit_solution(9002731194755541091)
XLA Ops:
  2.2 2.8 %shard_map.140 = (bf16[32,272,128]{2,1,0:T(8,128)(2,1)}, bf16[416,256]{1,0:T(8,128)(2,1)}, bf16[208,256]{1,0:T(8,128)(2,1)}) custom-call(s32[1]{0:T(128)} %bitcast.1.core, bf16[64,768]{1,0:T(8,128)(2,1)} %refs_0_.1, bf16[64,256]{1,0:T(8,128)(2,1)} %bitcast.18, s32[1,32,64]{2,1,0:T(8,128)} %refs_2_.1, s32[1,32,64]{2,1,0:T(8,128)} %refs_3_.1, ...), custom_call_target="tpu_custom_call" | custom-call | tf_op jit(solution)/shard_map/pallas_call | solution.py:373
  5.0 7.8 %all-to-all-start = ((bf16[32,272,128]{2,1,0:T(8,128)(2,1)}), bf16[32,272,128]{2,1,0:T(8,128)(2,1)S(1)}, u32[]{:S(2)}, u32[]{:S(2)}) async-start(bf16[32,272,128]{2,1,0:T(8,128)(2,1)} %get-tuple-element.28), calls=%async_computation | async-start | bytes 4456448 | tf_op jit(solution)/shard_map/all_to_all | solution.py:422
  12.8 4.7 %collective-permute-start.5 = (bf16[416,256]{1,0:T(8,128)(2,1)S(1)}, bf16[416,256]{1,0:T(8,128)(2,1)S(1)}, u32[]{:S(2)}, u32[]{:S(2)}) collective-permute-start(bf16[416,256]{1,0:T(8,128)(2,1)S(1)} %copy-done.6), channel_id=1, source_target_pairs={{0,3},{1,4},{2,5},{3,6},{4,7},{5,0},{6,1},{7,2},{8,13},{9,14},{10,... | collective-permute-start | bytes 638984 | tf_op jit(solution)/shard_map/ppermute | solution.py:417
  17.5 3.6 %collective-permute-start.4 = (bf16[416,256]{1,0:T(8,128)(2,1)S(1)}, bf16[416,256]{1,0:T(8,128)(2,1)S(1)}, u32[]{:S(2)}, u32[]{:S(2)}) collective-permute-start(bf16[416,256]{1,0:T(8,128)(2,1)S(1)} %copy-done.6), channel_id=1, source_target_pairs={{0,2},{1,3},{2,4},{3,5},{4,6},{5,7},{6,0},{7,1},{8,14},{9,15},{10,... | collective-permute-start | bytes 638984 | tf_op jit(solution)/shard_map/ppermute | solution.py:417
  23.6 5.5 %collective-permute-start.8 = (bf16[416,256]{1,0:T(8,128)(2,1)S(1)}, bf16[416,256]{1,0:T(8,128)(2,1)S(1)}, u32[]{:S(2)}, u32[]{:S(2)}) collective-permute-start(bf16[416,256]{1,0:T(8,128)(2,1)S(1)} %collective-permute-done.5.refs_5_.refs_13_), channel_id=1, source_target_pairs={{0,8},{8,0},{16,24},{24,16},{32,40},{40,32},{48,56},{56,48},{64,72... | collective-permute-start | bytes 638984 | tf_op jit(solution)/shard_map/ppermute | solution.py:419
  29.2 5.3 %collective-permute-done.4.refs_4_.refs_12_ = bf16[416,256]{1,0:T(8,128)(2,1)S(1)} collective-permute-done((bf16[416,256]{1,0:T(8,128)(2,1)S(1)}, bf16[416,256]{1,0:T(8,128)(2,1)S(1)}, u32[]{:S(2)}, u32[]{:S(2)}) %collective-permute-start.4) | collective-permute-done | bytes 213024 | tf_op jit(solution)/shard_map/ppermute | solution.py:417
  34.5 1.9 %collective-permute-done.3.refs_3_.refs_11_ = bf16[416,256]{1,0:T(8,128)(2,1)S(1)} collective-permute-done((bf16[416,256]{1,0:T(8,128)(2,1)S(1)}, bf16[416,256]{1,0:T(8,128)(2,1)S(1)}, u32[]{:S(2)}, u32[]{:S(2)}) %collective-permute-start.3) | collective-permute-done | bytes 213024 | tf_op jit(solution)/shard_map/ppermute | solution.py:417
  36.4 1.9 %collective-permute-start.6 = (bf16[416,256]{1,0:T(8,128)(2,1)S(1)}, bf16[416,256]{1,0:T(8,128)(2,1)S(1)}, u32[]{:S(2)}, u32[]{:S(2)}) collective-permute-start(bf16[416,256]{1,0:T(8,128)(2,1)S(1)} %collective-permute-done.3.refs_3_.refs_11_), channel_id=1, source_target_pairs={{0,8},{8,0},{16,24},{24,16},{32,40},{40,32},{48,56},{56,48},{64,72... | collective-permute-start | bytes 638984 | tf_op jit(solution)/shard_map/ppermute | solution.py:419
  38.2 2.4 %collective-permute-done.1.refs_1_.refs_9_ = bf16[208,256]{1,0:T(8,128)(2,1)S(1)} collective-permute-done((bf16[208,256]{1,0:T(8,128)(2,1)}, bf16[208,256]{1,0:T(8,128)(2,1)S(1)}, u32[]{:S(2)}, u32[]{:S(2)}) %collective-permute-start.1) | collective-permute-done | bytes 106528 | tf_op jit(solution)/shard_map/ppermute | solution.py:418
  42.9 1.9 %shard_map.141.normed = bf16[8,256,256]{2,1,0:T(8,128)(2,1)S(1)} custom-call(s32[1]{0:T(128)} %bitcast.me, s32[1]{0:T(128)} %bitcast.1.core, bf16[416,256]{1,0:T(8,128)(2,1)} %get-tuple-element.26.refs_0_.refs_8_, bf16[208,256]{1,0:T(8,128)(2,1)} %copy-done.12, bf16[208,256]{1,0:T(8,128)(2,1)} %collective-permute-done.2.refs_2_.refs_10_, ...), custom_call_target="tpu_custom_call" | custom-call | tf_op jit(solution)/shard_map/pallas_call | solution.py:425
  46.0 14.4 %all_to_all.20.got = bf16[16,48,128]{2,1,0:T(8,128)(2,1)S(1)} all-to-all(bf16[16,48,128]{2,1,0:T(8,128)(2,1)S(1)} %get-tuple-element.29), channel_id=1, replica_groups={{0,16,32,48,64,80,96,112,128,144,160,176,192,208,224,240},{8,24,40,56,7..., dimensions={0} | all-to-all | bytes 393216 | tf_op jit(solution)/shard_map/all_to_all | solution.py:442
  61.3 11.1 %all_to_all.21 = bf16[32,16,128]{2,1,0:T(8,128)(2,1)S(1)} all-to-all(bf16[32,16,128]{2,1,0:T(8,128)(2,1)S(1)} %bitcast.10), channel_id=1, replica_groups=mesh['tok'=32,'mlp'=8] {'tok'}, dimensions={0} | all-to-all | bytes 262144 | tf_op jit(solution)/shard_map/all_to_all | solution.py:452
  72.9 3.7 %collective-permute-start.10 = (bf16[192,256]{1,0:T(8,128)(2,1)S(1)}, bf16[192,256]{1,0:T(8,128)(2,1)S(1)}, u32[]{:S(2)}, u32[]{:S(2)}) collective-permute-start(bf16[192,256]{1,0:T(8,128)(2,1)S(1)} %get-tuple-element.35), channel_id=1, source_target_pairs={{0,4},{1,5},{2,6},{3,7},{4,0},{5,1},{6,2},{7,3},{8,12},{9,13},{10,... | collective-permute-start | bytes 294920 | tf_op jit(solution)/shard_map/ppermute | solution.py:471
  77.4 4.2 %collective-permute-start.12 = (bf16[192,256]{1,0:T(8,128)(2,1)S(1)}, bf16[192,256]{1,0:T(8,128)(2,1)S(1)}, u32[]{:S(2)}, u32[]{:S(2)}) collective-permute-start(bf16[192,256]{1,0:T(8,128)(2,1)S(1)} %get-tuple-element.37), channel_id=1, source_target_pairs={{0,5},{1,6},{2,7},{3,0},{4,1},{5,2},{6,3},{7,4},{8,13},{9,14},{10,... | collective-permute-start | bytes 294920 | tf_op jit(solution)/shard_map/ppermute | solution.py:471
  83.3 2.5 %collective-permute-start.14 = (bf16[192,256]{1,0:T(8,128)(2,1)S(1)}, bf16[192,256]{1,0:T(8,128)(2,1)S(1)}, u32[]{:S(2)}, u32[]{:S(2)}) collective-permute-start(bf16[192,256]{1,0:T(8,128)(2,1)S(1)} %get-tuple-element.39), channel_id=1, source_target_pairs={{0,6},{1,7},{2,0},{3,1},{4,2},{5,3},{6,4},{7,5},{8,14},{9,15},{10,... | collective-permute-start | bytes 294920 | tf_op jit(solution)/shard_map/ppermute | solution.py:471
  85.8 5.8 %collective-permute-done.11.refs_2_ = bf16[192,256]{1,0:T(8,128)(2,1)S(1)} collective-permute-done((bf16[192,256]{1,0:T(8,128)(2,1)S(1)}, bf16[192,256]{1,0:T(8,128)(2,1)S(1)}, u32[]{:S(2)}, u32[]{:S(2)}) %collective-permute-start.11) | collective-permute-done | bytes 98336 | tf_op jit(solution)/shard_map/ppermute | solution.py:471
  97.8 2.3 %collective-permute-start.22 = (bf16[128,256]{1,0:T(8,128)(2,1)S(1)}, bf16[128,256]{1,0:T(8,128)(2,1)S(1)}, u32[]{:S(2)}, u32[]{:S(2)}) collective-permute-start(bf16[128,256]{1,0:T(8,128)(2,1)S(1)} %get-tuple-element.42.refs_0_), channel_id=1, source_target_pairs={{0,6},{1,7},{2,0},{3,1},{4,2},{5,3},{6,4},{7,5},{8,14},{9,15},{10,... | collective-permute-start | bytes 196616 | tf_op jit(solution)/shard_map/ppermute | solution.py:478
  101.2 3.2 %collective-permute-start.20 = (bf16[128,256]{1,0:T(8,128)(2,1)S(1)}, bf16[128,256]{1,0:T(8,128)(2,1)S(1)}, u32[]{:S(2)}, u32[]{:S(2)}) collective-permute-start(bf16[128,256]{1,0:T(8,128)(2,1)S(1)} %get-tuple-element.42.refs_0_), channel_id=1, source_target_pairs={{0,4},{1,5},{2,6},{3,7},{4,0},{5,1},{6,2},{7,3},{8,12},{9,13},{10,... | collective-permute-start | bytes 196616 | tf_op jit(solution)/shard_map/ppermute | solution.py:478
  104.9 3.3 %collective-permute-start.18 = (bf16[128,256]{1,0:T(8,128)(2,1)S(1)}, bf16[128,256]{1,0:T(8,128)(2,1)S(1)}, u32[]{:S(2)}, u32[]{:S(2)}) collective-permute-start(bf16[128,256]{1,0:T(8,128)(2,1)S(1)} %get-tuple-element.42.refs_0_), channel_id=1, source_target_pairs={{0,2},{1,3},{2,4},{3,5},{4,6},{5,7},{6,0},{7,1},{8,10},{9,11},{10,... | collective-permute-start | bytes 196616 | tf_op jit(solution)/shard_map/ppermute | solution.py:478
  109.5 5.0 %collective-permute-done.19.refs_3_ = bf16[128,256]{1,0:T(8,128)(2,1)S(1)} collective-permute-done((bf16[128,256]{1,0:T(8,128)(2,1)S(1)}, bf16[128,256]{1,0:T(8,128)(2,1)S(1)}, u32[]{:S(2)}, u32[]{:S(2)}) %collective-permute-start.19) | collective-permute-done | bytes 65568 | tf_op jit(solution)/shard_map/ppermute | solution.py:478
  117.3 4.5 %shard_map.146 = bf16[8,128,384]{2,1,0:T(8,128)(2,1)} custom-call(s32[1]{0:T(128)} %bitcast.me, s32[1]{0:T(128)} %bitcast.1.core, bf16[128,256]{1,0:T(8,128)(2,1)S(1)} %get-tuple-element.42.refs_0_, bf16[128,256]{1,0:T(8,128)(2,1)S(1)} %collective-permute-done.17.refs_1_, bf16[128,256]{1,0:T(8,128)(2,1)S(1)} %collective-permute-done.18.refs_2_, ...), custom_call_target="tpu_custom_call" | custom-call | tf_op jit(solution)/shard_map/pallas_call | solution.py:481
  121.8 4.4 %all-to-all-start.3 = ((bf16[8,128,384]{2,1,0:T(8,128)(2,1)}), bf16[8,128,384]{2,1,0:T(8,128)(2,1)S(1)}, u32[]{:S(2)}, u32[]{:S(2)}) async-start(bf16[8,128,384]{2,1,0:T(8,128)(2,1)} %shard_map.146), calls=%async_computation.3 | async-start | bytes 1572864 | tf_op jit(solution)/shard_map/all_to_all | solution.py:501
  126.2 12.6 %shard_map.147.normal = f32[128,768]{1,0:T(8,128)S(1)} custom-call(bf16[8,64,256]{2,1,0:T(8,128)(2,1)S(1)} %get-tuple-element.45.slots), custom_call_target="tpu_custom_call" | custom-call | flops 4000000000 | bytes 1000000 | tf_op jit(solution)/shard_map/pallas_call | solution.py:504
  138.8 10.0 %all-to-all-done.3.got = bf16[8,128,384]{2,1,0:T(8,128)(2,1)S(1)} async-done(((bf16[8,128,384]{2,1,0:T(8,128)(2,1)}), bf16[8,128,384]{2,1,0:T(8,128)(2,1)S(1)}, u32[]{:S(2)}, u32[]{:S(2)}) %all-to-all-start.3) | async-done | bytes 786464 | tf_op jit(solution)/shard_map/all_to_all | solution.py:501
  (66 shorter events, 24.1 us)
Async XLA Ops:
  5.0 39.8 %all-to-all-start = ((bf16[32,272,128]{2,1,0:T(8,128)(2,1)}), bf16[32,272,128]{2,1,0:T(8,128)(2,1)S(1)}, u32[]{:S(2)}, u32[]{:S(2)}) async-start(bf16[32,272,128]{2,1,0:T(8,128)(2,1)} %get-tuple-element.28), calls=%async_computation | async-start | bytes 4456448 | tf_op jit(solution)/shard_map/all_to_all | solution.py:422
  12.8 10.9 %collective-permute-start.5 = (bf16[416,256]{1,0:T(8,128)(2,1)S(1)}, bf16[416,256]{1,0:T(8,128)(2,1)S(1)}, u32[]{:S(2)}, u32[]{:S(2)}) collective-permute-start(bf16[416,256]{1,0:T(8,128)(2,1)S(1)} %copy-done.6), channel_id=1, source_target_pairs={{0,3},{1,4},{2,5},{3,6},{4,7},{5,0},{6,1},{7,2},{8,13},{9,14},{10,... | collective-permute-start | bytes 638984 | tf_op jit(solution)/shard_map/ppermute | solution.py:417
  17.5 17.0 %collective-permute-start.4 = (bf16[416,256]{1,0:T(8,128)(2,1)S(1)}, bf16[416,256]{1,0:T(8,128)(2,1)S(1)}, u32[]{:S(2)}, u32[]{:S(2)}) collective-permute-start(bf16[416,256]{1,0:T(8,128)(2,1)S(1)} %copy-done.6), channel_id=1, source_target_pairs={{0,2},{1,3},{2,4},{3,5},{4,6},{5,7},{6,0},{7,1},{8,14},{9,15},{10,... | collective-permute-start | bytes 638984 | tf_op jit(solution)/shard_map/ppermute | solution.py:417
  21.1 15.3 %collective-permute-start.3 = (bf16[416,256]{1,0:T(8,128)(2,1)S(1)}, bf16[416,256]{1,0:T(8,128)(2,1)S(1)}, u32[]{:S(2)}, u32[]{:S(2)}) collective-permute-start(bf16[416,256]{1,0:T(8,128)(2,1)S(1)} %copy-done.6), channel_id=1, source_target_pairs={{0,1},{1,2},{2,3},{3,4},{4,5},{5,6},{6,7},{7,0},{8,15},{9,8},{10,9... | collective-permute-start | bytes 638984 | tf_op jit(solution)/shard_map/ppermute | solution.py:417
  22.1 18.6 %collective-permute-start.1 = (bf16[208,256]{1,0:T(8,128)(2,1)}, bf16[208,256]{1,0:T(8,128)(2,1)S(1)}, u32[]{:S(2)}, u32[]{:S(2)}) collective-permute-start(bf16[208,256]{1,0:T(8,128)(2,1)} %get-tuple-element.27), channel_id=1, source_target_pairs={{0,4},{1,5},{2,6},{3,7},{4,0},{5,1},{6,2},{7,3},{8,12},{9,13},{10,... | collective-permute-start | bytes 319496 | tf_op jit(solution)/shard_map/ppermute | solution.py:418
  23.6 18.5 %collective-permute-start.8 = (bf16[416,256]{1,0:T(8,128)(2,1)S(1)}, bf16[416,256]{1,0:T(8,128)(2,1)S(1)}, u32[]{:S(2)}, u32[]{:S(2)}) collective-permute-start(bf16[416,256]{1,0:T(8,128)(2,1)S(1)} %collective-permute-done.5.refs_5_.refs_13_), channel_id=1, source_target_pairs={{0,8},{8,0},{16,24},{24,16},{32,40},{40,32},{48,56},{56,48},{64,72... | collective-permute-start | bytes 638984 | tf_op jit(solution)/shard_map/ppermute | solution.py:419
  34.5 7.7 %collective-permute-start.7 = (bf16[416,256]{1,0:T(8,128)(2,1)S(1)}, bf16[416,256]{1,0:T(8,128)(2,1)}, u32[]{:S(2)}, u32[]{:S(2)}) collective-permute-start(bf16[416,256]{1,0:T(8,128)(2,1)S(1)} %collective-permute-done.4.refs_4_.refs_12_), channel_id=1, source_target_pairs={{0,8},{8,0},{16,24},{24,16},{32,40},{40,32},{48,56},{56,48},{64,72... | collective-permute-start | bytes 638984 | tf_op jit(solution)/shard_map/ppermute | solution.py:419
  36.4 5.8 %collective-permute-start.6 = (bf16[416,256]{1,0:T(8,128)(2,1)S(1)}, bf16[416,256]{1,0:T(8,128)(2,1)S(1)}, u32[]{:S(2)}, u32[]{:S(2)}) collective-permute-start(bf16[416,256]{1,0:T(8,128)(2,1)S(1)} %collective-permute-done.3.refs_3_.refs_11_), channel_id=1, source_target_pairs={{0,8},{8,0},{16,24},{24,16},{32,40},{40,32},{48,56},{56,48},{64,72... | collective-permute-start | bytes 638984 | tf_op jit(solution)/shard_map/ppermute | solution.py:419
  45.7 26.7 %collective-permute-start.9 = (bf16[32,64,128]{2,1,0:T(8,128)(2,1)S(1)}, bf16[32,64,128]{2,1,0:T(8,128)(2,1)S(1)}, u32[]{:S(2)}, u32[]{:S(2)}) collective-permute-start(bf16[32,64,128]{2,1,0:T(8,128)(2,1)S(1)} %slice.3), channel_id=1, source_target_pairs={{0,8},{8,0},{16,24},{24,16},{32,40},{40,32},{48,56},{56,48},{64,72... | collective-permute-start | bytes 1572872 | tf_op jit(solution)/shard_map/ppermute | solution.py:444
  72.9 12.9 %collective-permute-start.10 = (bf16[192,256]{1,0:T(8,128)(2,1)S(1)}, bf16[192,256]{1,0:T(8,128)(2,1)S(1)}, u32[]{:S(2)}, u32[]{:S(2)}) collective-permute-start(bf16[192,256]{1,0:T(8,128)(2,1)S(1)} %get-tuple-element.35), channel_id=1, source_target_pairs={{0,4},{1,5},{2,6},{3,7},{4,0},{5,1},{6,2},{7,3},{8,12},{9,13},{10,... | collective-permute-start | bytes 294920 | tf_op jit(solution)/shard_map/ppermute | solution.py:471
  76.6 15.0 %collective-permute-start.11 = (bf16[192,256]{1,0:T(8,128)(2,1)S(1)}, bf16[192,256]{1,0:T(8,128)(2,1)S(1)}, u32[]{:S(2)}, u32[]{:S(2)}) collective-permute-start(bf16[192,256]{1,0:T(8,128)(2,1)S(1)} %get-tuple-element.36), channel_id=1, source_target_pairs={{0,3},{1,4},{2,5},{3,6},{4,7},{5,0},{6,1},{7,2},{8,11},{9,12},{10,... | collective-permute-start | bytes 294920 | tf_op jit(solution)/shard_map/ppermute | solution.py:471
  77.4 14.2 %collective-permute-start.12 = (bf16[192,256]{1,0:T(8,128)(2,1)S(1)}, bf16[192,256]{1,0:T(8,128)(2,1)S(1)}, u32[]{:S(2)}, u32[]{:S(2)}) collective-permute-start(bf16[192,256]{1,0:T(8,128)(2,1)S(1)} %get-tuple-element.37), channel_id=1, source_target_pairs={{0,5},{1,6},{2,7},{3,0},{4,1},{5,2},{6,3},{7,4},{8,13},{9,14},{10,... | collective-permute-start | bytes 294920 | tf_op jit(solution)/shard_map/ppermute | solution.py:471
  81.7 9.9 %collective-permute-start.13 = (bf16[192,256]{1,0:T(8,128)(2,1)S(1)}, bf16[192,256]{1,0:T(8,128)(2,1)S(1)}, u32[]{:S(2)}, u32[]{:S(2)}) collective-permute-start(bf16[192,256]{1,0:T(8,128)(2,1)S(1)} %get-tuple-element.38), channel_id=1, source_target_pairs={{0,2},{1,3},{2,4},{3,5},{4,6},{5,7},{6,0},{7,1},{8,10},{9,11},{10,... | collective-permute-start | bytes 294920 | tf_op jit(solution)/shard_map/ppermute | solution.py:471
  83.3 10.2 %collective-permute-start.14 = (bf16[192,256]{1,0:T(8,128)(2,1)S(1)}, bf16[192,256]{1,0:T(8,128)(2,1)S(1)}, u32[]{:S(2)}, u32[]{:S(2)}) collective-permute-start(bf16[192,256]{1,0:T(8,128)(2,1)S(1)} %get-tuple-element.39), channel_id=1, source_target_pairs={{0,6},{1,7},{2,0},{3,1},{4,2},{5,3},{6,4},{7,5},{8,14},{9,15},{10,... | collective-permute-start | bytes 294920 | tf_op jit(solution)/shard_map/ppermute | solution.py:471
  85.8 8.6 %collective-permute-start.15 = (bf16[192,256]{1,0:T(8,128)(2,1)S(1)}, bf16[192,256]{1,0:T(8,128)(2,1)S(1)}, u32[]{:S(2)}, u32[]{:S(2)}) collective-permute-start(bf16[192,256]{1,0:T(8,128)(2,1)S(1)} %get-tuple-element.40), channel_id=1, source_target_pairs={{0,1},{1,2},{2,3},{3,4},{4,5},{5,6},{6,7},{7,0},{8,9},{9,10},{10,1... | collective-permute-start | bytes 294920 | tf_op jit(solution)/shard_map/ppermute | solution.py:471
  91.6 4.6 %collective-permute-start.16 = (bf16[192,256]{1,0:T(8,128)(2,1)S(1)}, bf16[192,256]{1,0:T(8,128)(2,1)S(1)}, u32[]{:S(2)}, u32[]{:S(2)}) collective-permute-start(bf16[192,256]{1,0:T(8,128)(2,1)S(1)} %get-tuple-element.41), channel_id=1, source_target_pairs={{0,7},{1,0},{2,1},{3,2},{4,3},{5,4},{6,5},{7,6},{8,15},{9,8},{10,9... | collective-permute-start | bytes 294920 | tf_op jit(solution)/shard_map/ppermute | solution.py:471
  96.3 8.6 %collective-permute-start.23 = (bf16[128,256]{1,0:T(8,128)(2,1)S(1)}, bf16[128,256]{1,0:T(8,128)(2,1)S(1)}, u32[]{:S(2)}, u32[]{:S(2)}) collective-permute-start(bf16[128,256]{1,0:T(8,128)(2,1)S(1)} %get-tuple-element.42.refs_0_), channel_id=1, source_target_pairs={{0,7},{1,0},{2,1},{3,2},{4,3},{5,4},{6,5},{7,6},{8,15},{9,8},{10,9... | collective-permute-start | bytes 196616 | tf_op jit(solution)/shard_map/ppermute | solution.py:478
  97.8 10.4 %collective-permute-start.22 = (bf16[128,256]{1,0:T(8,128)(2,1)S(1)}, bf16[128,256]{1,0:T(8,128)(2,1)S(1)}, u32[]{:S(2)}, u32[]{:S(2)}) collective-permute-start(bf16[128,256]{1,0:T(8,128)(2,1)S(1)} %get-tuple-element.42.refs_0_), channel_id=1, source_target_pairs={{0,6},{1,7},{2,0},{3,1},{4,2},{5,3},{6,4},{7,5},{8,14},{9,15},{10,... | collective-permute-start | bytes 196616 | tf_op jit(solution)/shard_map/ppermute | solution.py:478
  100.1 9.0 %collective-permute-start.21 = (bf16[128,256]{1,0:T(8,128)(2,1)S(1)}, bf16[128,256]{1,0:T(8,128)(2,1)S(1)}, u32[]{:S(2)}, u32[]{:S(2)}) collective-permute-start(bf16[128,256]{1,0:T(8,128)(2,1)S(1)} %get-tuple-element.42.refs_0_), channel_id=1, source_target_pairs={{0,5},{1,6},{2,7},{3,0},{4,1},{5,2},{6,3},{7,4},{8,13},{9,14},{10,... | collective-permute-start | bytes 196616 | tf_op jit(solution)/shard_map/ppermute | solution.py:478
  101.2 8.3 %collective-permute-start.20 = (bf16[128,256]{1,0:T(8,128)(2,1)S(1)}, bf16[128,256]{1,0:T(8,128)(2,1)S(1)}, u32[]{:S(2)}, u32[]{:S(2)}) collective-permute-start(bf16[128,256]{1,0:T(8,128)(2,1)S(1)} %get-tuple-element.42.refs_0_), channel_id=1, source_target_pairs={{0,4},{1,5},{2,6},{3,7},{4,0},{5,1},{6,2},{7,3},{8,12},{9,13},{10,... | collective-permute-start | bytes 196616 | tf_op jit(solution)/shard_map/ppermute | solution.py:478
  104.3 10.2 %collective-permute-start.19 = (bf16[128,256]{1,0:T(8,128)(2,1)S(1)}, bf16[128,256]{1,0:T(8,128)(2,1)S(1)}, u32[]{:S(2)}, u32[]{:S(2)}) collective-permute-start(bf16[128,256]{1,0:T(8,128)(2,1)S(1)} %get-tuple-element.42.refs_0_), channel_id=1, source_target_pairs={{0,3},{1,4},{2,5},{3,6},{4,7},{5,0},{6,1},{7,2},{8,11},{9,12},{10,... | collective-permute-start | bytes 196616 | tf_op jit(solution)/shard_map/ppermute | solution.py:478
  104.9 11.1 %collective-permute-start.18 = (bf16[128,256]{1,0:T(8,128)(2,1)S(1)}, bf16[128,256]{1,0:T(8,128)(2,1)S(1)}, u32[]{:S(2)}, u32[]{:S(2)}) collective-permute-start(bf16[128,256]{1,0:T(8,128)(2,1)S(1)} %get-tuple-element.42.refs_0_), channel_id=1, source_target_pairs={{0,2},{1,3},{2,4},{3,5},{4,6},{5,7},{6,0},{7,1},{8,10},{9,11},{10,... | collective-permute-start | bytes 196616 | tf_op jit(solution)/shard_map/ppermute | solution.py:478
  108.2 9.0 %collective-permute-start.17 = (bf16[128,256]{1,0:T(8,128)(2,1)S(1)}, bf16[128,256]{1,0:T(8,128)(2,1)S(1)}, u32[]{:S(2)}, u32[]{:S(2)}) collective-permute-start(bf16[128,256]{1,0:T(8,128)(2,1)S(1)} %get-tuple-element.42.refs_0_), channel_id=1, source_target_pairs={{0,1},{1,2},{2,3},{3,4},{4,5},{5,6},{6,7},{7,0},{8,9},{9,10},{10,1... | collective-permute-start | bytes 196616 | tf_op jit(solution)/shard_map/ppermute | solution.py:478
  121.8 26.9 %all-to-all-start.3 = ((bf16[8,128,384]{2,1,0:T(8,128)(2,1)}), bf16[8,128,384]{2,1,0:T(8,128)(2,1)S(1)}, u32[]{:S(2)}, u32[]{:S(2)}) async-start(bf16[8,128,384]{2,1,0:T(8,128)(2,1)} %shard_map.146), calls=%async_computation.3 | async-start | bytes 1572864 | tf_op jit(solution)/shard_map/all_to_all | solution.py:501
  (15 other events, 408.8 us)
